TPU v7x, 32 devices: a whole 2x2x4 slice. The times are simulated.
32 devices in a mesh: gx: 8 (over z, y), gy: 4 (over x, core).
Axes of the slice: x: 2, y: 2, z: 4, core: 2. Of those that a mesh axis runs over, the one named last changes fastest.
Arguments:
- pressure: float32 [12, 256, 512], P(None, 'gx', 'gy'), may hold values from 0.5 to 1.5
- saturation: float32 [2, 12, 256, 512], P(None, None, 'gx', 'gy'), may hold values from 0.05 to 0.35
- permeability: float32 [3, 12, 256, 512], P(None, None, 'gx', 'gy'), may hold values from 0.25 to 8
- pore_volume: float32 [12, 256, 512], P(None, 'gx', 'gy'), may hold values from 0.5 to 8
- cell_depth: float32 [12, 256, 512], P(None, 'gx', 'gy'), may hold values from -4 to 4
- residual: float32 [3, 12, 256, 512], P(None, None, 'gx', 'gy'), may hold values from -12 to 12
- upstream_flags: int32 [12, 256, 512], P(None, 'gx', 'gy'), may hold values from 0 to 7
- perf_cell: int32 [32, 1024], P(('gx', 'gy')), may hold values from 0 to 49151
- perf_well: int32 [32, 1024], P(('gx', 'gy')), may hold values from -1 to 1023, as said below
- perf_index: float32 [32, 1024], P(('gx', 'gy')), may hold values from 0.5 to 4
- well_mode: int32 [1024], P(('gx', 'gy')), may hold values from 0 to 1
- well_target: float32 [1024], P(('gx', 'gy')), may hold values from 0.2 to 1.2
Outputs:
- new_pressure: float32 [12, 256, 512], P(None, 'gx', 'gy')
- well_bhp: float32 [1024], P(('gx', 'gy'))
Inputs may be any that keep to these rules, and one draw needn't show every extreme that they name: `upstream_flags`: bit 1 set: the cell is upstream on its face towards the next cell along x; bit 2: along y; bit 4: along z. `perf_cell`: the local cell number, within its row's block of columns, of the perforated cell. `perf_well`: -1 marks an empty slot; in each row the live slots come first; every well has at least one live slot; in every draw some row has all 1024 slots live. `well_mode`: 0: the well holds its bottom-hole pressure at well_target; 1: it produces well_target.
All inputs are finite; a program needn't handle non-finite values.
Results may differ from a plain program's by a relative error of at most 0.0003.
Values sent between devices are 32-bit elements; how exact they have to be, the bound alone decides.
No kernel may reach another device: no remote copies, remote signals or barrier semaphores. Data moves between devices by JAX's collectives and lax.ppermute only.
A program may use at most 64 MiB of HBM per device.

v0:
```python
import jax
import jax.numpy as jnp
from jax import lax
from jax.sharding import PartitionSpec as P

SWEEPS = 2


MU_OIL = 2.0
MU_WATER = 1.0
MU_GAS = 0.2
COMP_OIL = 0.2
COMP_WATER = 0.05
GRAV_OIL = 0.4
GRAV_WATER = 0.5
GRAV_GAS = 0.08
RELAXATION = 0.8


def extended(cells, sides, width):
    for axis, dim in sides:
        count = lax.axis_size(axis)
        ends = count - 1
        head = lax.slice_in_dim(cells, 0, width, axis=dim)
        tail = lax.slice_in_dim(cells, cells.shape[dim] - width, cells.shape[dim], axis=dim)
        cells = jnp.concatenate(
            [
                lax.ppermute(tail, axis, [(i, (i + 1) % count) for i in range(ends)]),
                cells,
                lax.ppermute(head, axis, [((i + 1) % count, i) for i in range(ends)]),
            ],
            axis=dim,
        )
    return cells


def phase_weights(pressure):
    b_oil = 1.0 + COMP_OIL * (pressure - 1.0)
    b_water = 1.0 + COMP_WATER * (pressure - 1.0)
    return (1.0 / b_oil, 1.0 / b_water, 1.0 / pressure)


def phase_mobility(pressure, sat_water, sat_gas):
    sat_oil = 1.0 - sat_water - sat_gas
    b_oil = 1.0 + COMP_OIL * (pressure - 1.0)
    b_water = 1.0 + COMP_WATER * (pressure - 1.0)
    return (
        sat_oil * sat_oil * b_oil / MU_OIL,
        sat_water * sat_water * b_water / MU_WATER,
        sat_gas * sat_gas * pressure / MU_GAS,
    )


def storage_term(weights, sat_water, sat_gas):
    sat_oil = 1.0 - sat_water - sat_gas
    return (
        sat_oil * COMP_OIL * weights[0] + sat_water * COMP_WATER * weights[1] + sat_gas * weights[2]
    )


def flag_bits(flag_code):
    bit_x = jnp.mod(flag_code, 2.0)
    remainder = (flag_code - bit_x) * 0.5
    bit_y = jnp.mod(remainder, 2.0)
    return (bit_x, bit_y, (remainder - bit_y) * 0.5)


def face_terms(weights, mob_center, mob_beside, perm_center, perm_beside, center_up, depth_drop):
    transmit = 2.0 * perm_center * perm_beside / (perm_center + perm_beside)
    coupling = jnp.zeros_like(transmit)
    gravity = jnp.zeros_like(transmit)
    for weight, center, beside, lift_rate in zip(
        weights, mob_center, mob_beside, (GRAV_OIL, GRAV_WATER, GRAV_GAS)
    ):
        flux_term = weight * (transmit * jnp.where(center_up, center, beside))
        coupling = coupling + flux_term
        gravity = gravity + flux_term * lift_rate
    return (coupling, gravity * depth_drop)


def direction_terms(weights, center, plus_side, minus_side, bit_center, bit_minus):
    coup_plus, grav_plus = face_terms(
        weights,
        center[0],
        plus_side[0],
        center[1],
        plus_side[1],
        bit_center > 0.5,
        center[2] - plus_side[2],
    )
    coup_minus, grav_minus = face_terms(
        weights,
        center[0],
        minus_side[0],
        center[1],
        minus_side[1],
        bit_minus < 0.5,
        center[2] - minus_side[2],
    )
    return ((coup_plus, coup_minus), grav_plus + grav_minus)


def neighbour(grid_field, axis_dim, offset):
    padding = [(0, 0)] * grid_field.ndim
    padding[axis_dim] = (1, 1)
    padded = jnp.pad(grid_field, padding)
    return lax.slice_in_dim(
        padded, 1 + offset, 1 + offset + grid_field.shape[axis_dim], axis=axis_dim
    )


def plus_minus(rim_field, direction):
    if direction == 0:
        return (rim_field[:, 2:, 1:-1], rim_field[:, :-2, 1:-1])
    return (rim_field[:, 1:-1, 2:], rim_field[:, 1:-1, :-2])


def coupled_sum(couplings, besides):
    running = couplings[0] * besides[0]
    for coupling, beside in zip(couplings[1:], besides[1:]):
        running = running + coupling * beside
    return running


def body(
    pressure,
    saturation,
    permeability,
    pore_volume,
    cell_depth,
    residual,
    upstream_flags,
    perf_cell,
    perf_well,
    perf_index,
    well_mode,
    well_target,
):
    sat_water, sat_gas = (saturation[0], saturation[1])
    weights = phase_weights(pressure)
    mobility = phase_mobility(pressure, sat_water, sat_gas)
    storage = pore_volume * storage_term(weights, sat_water, sat_gas)
    flag_code = upstream_flags.astype(jnp.float32)
    flag_parts = flag_bits(flag_code)
    planes = jnp.stack(
        mobility + (pressure, permeability[0], permeability[1], cell_depth, flag_code)
    )
    rimmed = extended(planes, (("gx", 2), ("gy", 3)), 1)
    rim_sets = [
        (rimmed[0], rimmed[1], rimmed[2], rimmed[3], rimmed[4 + direction], rimmed[6], rimmed[7])
        for direction in range(2)
    ]
    couplings = ()
    gravity = jnp.zeros_like(pressure)
    for direction in range(3):
        if direction < 2:
            fields = rim_sets[direction]
            mob_sides = [plus_minus(fields[index], direction) for index in range(3)]
            perm_sides = plus_minus(fields[4], direction)
            depth_sides = plus_minus(fields[5], direction)
            bit_minus = flag_bits(plus_minus(fields[6], direction)[1])[direction]
        else:
            mob_sides = [
                (neighbour(phase_field, 0, 1), neighbour(phase_field, 0, -1))
                for phase_field in mobility
            ]
            perm_sides = (neighbour(permeability[2], 0, 1), neighbour(permeability[2], 0, -1))
            depth_sides = (neighbour(cell_depth, 0, 1), neighbour(cell_depth, 0, -1))
            bit_minus = neighbour(flag_parts[2], 0, -1)
        center = (mobility, permeability[direction], cell_depth)
        plus_side = (tuple((sides[0] for sides in mob_sides)), perm_sides[0], depth_sides[0])
        minus_side = (tuple((sides[1] for sides in mob_sides)), perm_sides[1], depth_sides[1])
        coupled, grav_part = direction_terms(
            weights, center, plus_side, minus_side, flag_parts[direction], bit_minus
        )
        couplings = couplings + coupled
        gravity = gravity + grav_part
    first_besides = plus_minus(rim_sets[0][3], 0) + plus_minus(rim_sets[1][3], 1)
    faces_total = (
        couplings[0] + couplings[1] + couplings[2] + couplings[3] + couplings[4] + couplings[5]
    )
    combined = weights[0] * residual[0] + weights[1] * residual[1] + weights[2] * residual[2]
    rhs_base = storage * pressure - combined + gravity
    total_mob = weights[0] * mobility[0] + weights[1] * mobility[1] + weights[2] * mobility[2]
    owned_count = well_mode.shape[0]
    wells_count = owned_count * lax.axis_size("gx") * lax.axis_size("gy")
    cell_count = total_mob.size
    perf_slots = perf_cell[0]
    is_live = perf_well[0] >= 0
    well_ids = jnp.where(is_live, perf_well[0], 0)
    perf_factor = jnp.where(is_live, perf_index[0] * total_mob.reshape(-1)[perf_slots], 0.0)
    well_base = jax.ops.segment_sum(perf_factor, well_ids, num_segments=wells_count)
    well_diag = (
        jnp.zeros((cell_count,), jnp.float32)
        .at[perf_slots]
        .add(perf_factor)
        .reshape(pressure.shape)
    )
    total_diag = storage + faces_total + well_diag
    controls = lax.all_gather(
        jnp.stack((well_mode.astype(jnp.float32), well_target)), ("gx", "gy"), axis=1, tiled=True
    )
    current = pressure
    well_bhp = well_target
    for sweep_index in range(SWEEPS):
        if sweep_index == 0:
            areal_besides = first_besides
        else:
            rim_current = extended(current, (("gx", 1), ("gy", 2)), 1)
            areal_besides = plus_minus(rim_current, 0) + plus_minus(rim_current, 1)
        at_perf = current.reshape(-1)[perf_slots]
        well_part = jax.ops.segment_sum(perf_factor * at_perf, well_ids, num_segments=wells_count)
        if sweep_index == 0:
            partial_value = jnp.stack((well_part, well_base))
        else:
            partial_value = well_part[None]
        reduced = lax.psum(partial_value, ("gx", "gy"))
        if sweep_index == 0:
            every_base = reduced[1]
        every_bhp = jnp.where(
            controls[0] < 0.5, controls[1], (reduced[0] - controls[1]) / every_base
        )
        well_bhp = lax.dynamic_slice_in_dim(
            every_bhp, lax.axis_index(("gx", "gy")) * owned_count, owned_count
        )
        well_rhs = (
            jnp.zeros((cell_count,), jnp.float32)
            .at[perf_slots]
            .add(perf_factor * every_bhp[well_ids])
            .reshape(pressure.shape)
        )
        besides = areal_besides + (neighbour(current, 0, 1), neighbour(current, 0, -1))
        current = (
            current
            + RELAXATION
            * (rhs_base + well_rhs - total_diag * current + coupled_sum(couplings, besides))
            / total_diag
        )
    return (current, well_bhp)


def solution(mesh):
    return jax.shard_map(
        body,
        mesh=mesh,
        in_specs=(
            P(None, "gx", "gy"),
            P(None, None, "gx", "gy"),
            P(None, None, "gx", "gy"),
            P(None, "gx", "gy"),
            P(None, "gx", "gy"),
            P(None, None, "gx", "gy"),
            P(None, "gx", "gy"),
            P(("gx", "gy"), None),
            P(("gx", "gy"), None),
            P(("gx", "gy"), None),
            P(("gx", "gy")),
            P(("gx", "gy")),
        ),
        out_specs=(P(None, "gx", "gy"), P(("gx", "gy"))),
        check_vma=False,
    )
```

profile of v0, /device:TPU:0, one launch (start us, length us, event | category | flops | bytes accessed | tf_op | source)
XLA Modules:
  0.0 250.0 jit_solution(16264751669940376441)
XLA Ops:
  0.6 0.0 copy-start.4
  0.7 0.0 copy-start.13
  0.7 2.0 multiply_add_fusion
  2.8 0.0 copy-start.26
  3.0 0.1 fusion.121
  3.1 4.9 %collective-permute-start = (f32[8,12,1,128]{3,2,1,0:T(1,128)S(1)}, f32[8,12,1,128]{3,2,1,0:T(1,128)S(1)}, u32[]{:S(2)}, u32[]{:S(2)}) collective-permute-start(f32[8,12,1,128]{3,2,1,0:T(1,128)S(1)} %get-tuple-element.24), channel_id=1, source_target_pairs={{0,4},{4,8},{8,12},{12,16},{16,20},{20,24},{24,28},{1,5},{5,9},{9,... | collective-permute-start | bytes 147464 | tf_op jit(solution)/shard_map/ppermute | solution.py:28
  8.0 1.3 collective-permute-start.1
  9.3 0.7 slice_bitcast_fusion.8
  10.0 0.9 subtract_multiply_fusion
  11.0 6.2 %gather_fusion = f32[1024]{0:T(1024)S(1)} fusion(f32[49152]{0:T(1024)S(1)} %bitcast.242, s32[1024]{0:T(1024)S(1)} %get-tuple-element.36), kind=kCustom, calls=%fused_computation | custom fusion | bytes 12288 | tf_op jit(solution)/shard_map/gather | solution.py:191
  17.2 0.0 copy-start.27
  17.2 0.0 copy-start.29
  17.2 0.0 copy-start.28
  17.2 6.2 %gather_fusion.1 = f32[1024]{0:T(1024)S(1)} fusion(f32[49152]{0:T(1024)S(1)} %bitcast.240, s32[1024]{0:T(1024)S(1)} %get-tuple-element.36), kind=kCustom, calls=%fused_computation.1 | custom fusion | bytes 12288 | tf_op jit(solution)/shard_map/gather | solution.py:211
  23.4 7.6 %scatter_custom_fusion.1 = f32[1024]{0:T(1024)S(1)} fusion(s32[1024]{0:T(1024)S(1)} %bitcast.261, f32[1024]{0:T(1024)S(1)} %get-tuple-element.10, f32[]{:T(128)} %constant.50.clone.1), kind=kCustom, calls=%fused_computation.235 | custom fusion | flops 1024 | bytes 4100 | tf_op jit(solution)/shard_map/scatter-add | solution.py:192
  31.0 7.6 %scatter_custom_fusion = f32[1024]{0:T(1024)S(1)} fusion(s32[1024]{0:T(1024)S(1)} %bitcast.262, f32[1024]{0:T(1024)S(1)} %get-tuple-element.9, f32[]{:T(128)} %constant.50.clone.1), kind=kCustom, calls=%fused_computation.237 | custom fusion | flops 1024 | bytes 4100 | tf_op jit(solution)/shard_map/scatter-add | solution.py:212
  38.7 41.8 %psum.14 = f32[2,1024]{1,0:T(2,128)S(1)} all-reduce(f32[2,1024]{1,0:T(2,128)S(1)} %pad_maximum_fusion.11), channel_id=1, replica_groups=mesh['gx'=8,'gy'=4] {'gx','gy'}, use_global_device_ids=true, to_apply=%region_2.3 | all-reduce | flops 2048 | bytes 16384 | tf_op jit(solution)/shard_map/psum | solution.py:217
  80.5 41.1 %all-gather = f32[32,32,2]{1,2,0:T(2,128)S(1)} all-gather(f32[1,32,2]{1,2,0:T(2,128)S(1)} %maximum_bitcast_fusion), channel_id=1, replica_groups=mesh['gx'=8,'gy'=4] {'gx','gy'}, dimensions={0}, use_global_device_ids=true | all-gather | bytes 8448 | tf_op jit(solution)/shard_map/all_gather | solution.py:200
  121.6 0.1 reshape.190
  121.8 0.3 pad_maximum_fusion.1
  122.1 1.9 fusion.120
  124.0 2.3 copy.55
  126.3 2.2 collective-permute-start.2
  128.5 0.8 copy.56
  129.3 1.3 collective-permute-start.3
  130.6 6.6 %scatter_custom_fusion.3 = f32[49152]{0:T(1024)} fusion(s32[1024]{0:T(1024)S(1)} %bitcast.256, f32[1024]{0:T(1024)S(1)} %get-tuple-element.10, f32[]{:T(128)} %constant.50.clone.1), kind=kCustom, calls=%fused_computation.216 | custom fusion | flops 1024 | bytes 196612 | tf_op jit(solution)/shard_map/scatter-add | solution.py:196
  137.2 4.5 %gather_fusion.2 = f32[1024]{0:T(1024)S(1)} fusion(f32[1024]{0:T(1024)S(1)} %divide_select_fusion.1, s32[1024]{0:T(1024)S(1)} %get-tuple-element.35), kind=kCustom, calls=%fused_computation.2 | custom fusion | bytes 12288 | tf_op jit(solution)/shard_map/gather | solution.py:229
  141.8 6.6 %scatter_custom_fusion.2 = f32[49152]{0:T(1024)} fusion(s32[1024]{0:T(1024)S(1)} %bitcast.257, f32[1024]{0:T(1024)S(1)} %mul.456, f32[]{:T(128)} %constant.50.clone.1), kind=kCustom, calls=%fused_computation.218 | custom fusion | flops 1024 | bytes 196612 | tf_op jit(solution)/shard_map/scatter-add | solution.py:229
  148.3 0.8 copy.57
  149.1 2.1 copy.58
  151.2 4.0 %pad_maximum_fusion = f32[8,12,34,130]{3,2,1,0:T(8,128)S(1)} fusion(f32[8,12,34,1]{3,2,1,0:T(8,128)} %copy.58, f32[8,12,1,128]{3,2,1,0:T(1,128)S(1)} %collective-permute-done.1, f32[8,12,32,128]{3,2,1,0:T(8,128)} %copy-done.1, f32[8,12,1,128]{3,2,1,0:T(1,128)S(1)} %collective-permute-done, f32[8,12,34,1]{3,2,1,0:T(8,128)S(1)} %copy.57), kind=kLoop, calls=%fused_computation.11 | loop fusion | flops 1697280 | bytes 3394560 | tf_op jit(solution)/shard_map/concatenate | solution.py:26
  155.3 0.0 copy-start.5
  155.3 0.0 copy-start.12
  155.3 0.0 copy-start.14
  155.3 0.0 copy-start.16
  155.4 0.3 slice_bitcast_fusion.2
  155.7 0.7 copy-done.5
  156.3 0.0 copy-done.8
  156.4 0.1 copy-done.10
  156.4 0.4 copy-done.12
  156.8 0.2 copy-done.14
  157.0 0.1 copy-done.15
  157.1 0.1 copy-done.16
  157.2 0.1 copy-done.17
  157.2 0.1 copy-done.18
  157.3 0.1 copy-done.19
  157.3 0.1 copy-done.20
  157.4 3.1 %fusion.32 = (f32[12,32,128]{2,1,0:T(8,128)S(1)}, pred[12,32,128]{2,1,0:T(8,128)(4,1)S(1)}, pred[12,32,128]{2,1,0:T(8,128)(4,1)S(1)}, pred[12,32,128]{2,1,0:T(8,128)(4,1)}, pred[12,32,128]{2,1,0:T(8,128)(4,1)}) fusion(f32[12,32,128]{2,1,0:T(8,128)S(1)} %copy-done, f32[12,34,130]{2,1,0:T(8,128)S(1)} %get-tuple-element.15, f32[12,32,128]{2,1,0:T(8,128)S(1)} %bitcast.244, ...), kind=kLoop, calls=%fused_computation.75 | loop fusion | flops 11255808 | bytes 9043968 | tf_op jit(solution)/shard_map/add | solution.py:234
  160.5 0.6 fusion.123
  161.1 1.3 collective-permute-start.4
  162.4 5.1 %collective-permute-start.5 = (f32[12,1,128]{2,1,0:T(1,128)}, f32[12,1,128]{2,1,0:T(1,128)}, u32[]{:S(2)}, u32[]{:S(2)}) collective-permute-start(f32[12,1,128]{2,1,0:T(1,128)} %get-tuple-element.29), channel_id=1, source_target_pairs={{0,4},{4,8},{8,12},{12,16},{16,20},{20,24},{24,28},{1,5},{5,9},{9,... | collective-permute-start | bytes 18440 | tf_op jit(solution)/shard_map/ppermute | solution.py:28
  167.5 10.5 %gather_fusion.3 = f32[1024]{0:T(1024)} fusion(f32[49152]{0:T(1024)S(1)} %bitcast.241, s32[1024]{0:T(1024)S(1)} %get-tuple-element.36), kind=kCustom, calls=%fused_computation.3 | custom fusion | bytes 12288 | tf_op jit(solution)/shard_map/gather | solution.py:211
  178.1 1.3 mul.465
  179.3 7.8 %scatter_custom_fusion.4 = f32[1024]{0:T(1024)S(1)} fusion(s32[1024]{0:T(1024)} %bitcast.263, f32[1024]{0:T(1024)} %mul.465, f32[]{:T(128)} %constant.50.clone.1), kind=kCustom, calls=%fused_computation.233 | custom fusion | flops 1024 | bytes 4608 | tf_op jit(solution)/shard_map/scatter-add | solution.py:212
  187.1 37.2 %psum.15 = f32[1024]{0:T(1024)} all-reduce(f32[1024]{0:T(1024)S(1)} %scatter_custom_fusion.4), channel_id=1, replica_groups=mesh['gx'=8,'gy'=4] {'gx','gy'}, use_global_device_ids=true, to_apply=%region_6.7 | all-reduce | flops 1024 | bytes 8192 | tf_op jit(solution)/shard_map/psum | solution.py:217
  224.3 0.7 pad_maximum_fusion.2
  225.0 0.9 fusion.122
  225.9 1.3 collective-permute-start.6
  227.2 3.7 %collective-permute-start.7 = (f32[12,34,1]{2,1,0:T(8,128)}, f32[12,34,1]{2,1,0:T(8,128)}, u32[]{:S(2)}, u32[]{:S(2)}) collective-permute-start(f32[12,34,1]{2,1,0:T(8,128)} %get-tuple-element.28), channel_id=1, source_target_pairs={{0,1},{1,2},{2,3},{4,5},{5,6},{6,7},{8,9},{9,10},{10,11},{12,13},{... | collective-permute-start | bytes 4904 | tf_op jit(solution)/shard_map/ppermute | solution.py:28
  230.9 0.7 divide_select_fusion
  231.6 5.0 %gather_fusion.4 = f32[1024]{0:T(1024)S(1)} fusion(f32[1024]{0:T(1024)S(1)} %divide_select_fusion, s32[1024]{0:T(1024)} %copy-done.21), kind=kCustom, calls=%fused_computation.4 | custom fusion | bytes 12288 | tf_op jit(solution)/shard_map/gather | solution.py:229
  236.6 6.7 %scatter_custom_fusion.5 = f32[49152]{0:T(1024)} fusion(s32[1024]{0:T(1024)} %bitcast.258, f32[1024]{0:T(1024)S(1)} %mul.466, f32[]{:T(128)} %constant.50.clone.1), kind=kCustom, calls=%fused_computation.214 | custom fusion | flops 1024 | bytes 197120 | tf_op jit(solution)/shard_map/scatter-add | solution.py:229
  243.3 0.6 dynamic_slice.3
  243.9 5.9 %fusion.40 = f32[12,32,128]{2,1,0:T(8,128)} fusion(f32[12,32,128]{2,1,0:T(8,128)S(1)} %get-tuple-element.4, f32[12,34,1]{2,1,0:T(8,128)} %collective-permute-done.7, f32[12,1,128]{2,1,0:T(1,128)} %collective-permute-done.4, f32[12,1,128]{2,1,0:T(1,128)} %collective-permute-done.5, f32[12,34,1]{2,1,0:T(8,128)} %collective-permute-done.6, ...), kind=kLoop, calls=%fused_computation.83 | loop fusion | flops 11157504 | bytes 8076480 | tf_op jit(solution)/shard_map/add | solution.py:234
  (69 shorter events, 0.4 us)
Async XLA Ops:
  0.6 2.2 copy-start
  0.6 2.2 copy-start.2
  0.6 2.2 copy-start.4
  0.7 2.3 copy-start.13
  0.7 2.3 copy-start.6
  2.7 7.3 %copy-start.7 = (f32[12,32,128]{2,1,0:T(8,128)}, f32[12,32,128]{2,1,0:T(8,128)S(1)}, u32[]{:S(2)}) copy-start(f32[12,32,128]{2,1,0:T(8,128)S(1)} %get-tuple-element.12) | copy-start | bytes 589828
  2.7 7.3 %copy-start.9 = (f32[12,32,128]{2,1,0:T(8,128)}, f32[12,32,128]{2,1,0:T(8,128)S(1)}, u32[]{:S(2)}) copy-start(f32[12,32,128]{2,1,0:T(8,128)S(1)} %get-tuple-element.13) | copy-start | bytes 589828
  2.7 6.5 %copy-start.22 = (s32[1,1024]{1,0:T(1,128)S(1)}, s32[1,1024]{1,0:T(1,128)}, u32[]{:S(2)}) copy-start(s32[1,1024]{1,0:T(1,128)} %param.20) | copy-start | bytes 12292
  2.8 8.2 %copy-start.26 = (s32[1,1024]{1,0:T(1,128)S(1)}, s32[1,1024]{1,0:T(1,128)}, u32[]{:S(2)}) copy-start(s32[1,1024]{1,0:T(1,128)} %param.19) | copy-start | bytes 12292
  3.0 118.8 %copy-start.1 = (f32[8,12,32,128]{3,2,1,0:T(8,128)}, f32[8,12,32,128]{3,2,1,0:T(8,128)S(1)}, u32[]{:S(2)}) copy-start(f32[8,12,32,128]{3,2,1,0:T(8,128)S(1)} %bitcast_dynamic-update-slice_fusion) | copy-start | bytes 4718596
  3.1 118.7 %collective-permute-start = (f32[8,12,1,128]{3,2,1,0:T(1,128)S(1)}, f32[8,12,1,128]{3,2,1,0:T(1,128)S(1)}, u32[]{:S(2)}, u32[]{:S(2)}) collective-permute-start(f32[8,12,1,128]{3,2,1,0:T(1,128)S(1)} %get-tuple-element.24), channel_id=1, source_target_pairs={{0,4},{4,8},{8,12},{12,16},{16,20},{20,24},{24,28},{1,5},{5,9},{9,... | collective-permute-start | bytes 147464 | tf_op jit(solution)/shard_map/ppermute | solution.py:28
  8.0 113.8 %collective-permute-start.1 = (f32[8,12,1,128]{3,2,1,0:T(1,128)S(1)}, f32[8,12,1,128]{3,2,1,0:T(1,128)S(1)}, u32[]{:S(2)}, u32[]{:S(2)}) collective-permute-start(f32[8,12,1,128]{3,2,1,0:T(1,128)S(1)} %get-tuple-element.25), channel_id=1, source_target_pairs={{4,0},{8,4},{12,8},{16,12},{20,16},{24,20},{28,24},{5,1},{9,5},{13... | collective-permute-start | bytes 147464 | tf_op jit(solution)/shard_map/ppermute | solution.py:30
  9.3 21.7 %copy-start.25 = (s32[1024,1]{0,1:T(1,128)}, s32[1024,1]{0,1:T(1,128)S(1)}, u32[]{:S(2)}) copy-start(s32[1024,1]{0,1:T(1,128)S(1)} %get-tuple-element.34) | copy-start | bytes 12292
  11.0 130.8 %copy-start.23 = (s32[1024,1]{0,1:T(1,128)}, s32[1024,1]{0,1:T(1,128)S(1)}, u32[]{:S(2)}) copy-start(s32[1024,1]{0,1:T(1,128)S(1)} %compare_select_fusion.2) | copy-start | bytes 12292
  11.0 126.2 %copy-start.21 = (s32[1024]{0:T(1024)}, s32[1024]{0:T(1024)S(1)}, u32[]{:S(2)}) copy-start(s32[1024]{0:T(1024)S(1)} %get-tuple-element.35) | copy-start | bytes 12292
  17.2 6.2 %copy-start.27 = (f32[1,1024]{1,0:T(1,128)S(1)}, f32[1,1024]{1,0:T(1,128)}, u32[]{:S(2)}) copy-start(f32[1,1024]{1,0:T(1,128)} %param.21) | copy-start | bytes 12292
  17.2 63.3 %copy-start.29 = (s32[32]{0:T(128)S(1)}, s32[32]{0:T(128)}, u32[]{:S(2)}) copy-start(s32[32]{0:T(128)} %param.22) | copy-start | bytes 388
  17.2 63.3 %copy-start.28 = (f32[32]{0:T(128)S(1)}, f32[32]{0:T(128)}, u32[]{:S(2)}) copy-start(f32[32]{0:T(128)} %param.23) | copy-start | bytes 388
  121.7 8.9 %copy-start.24 = (pred[1024]{0:T(1024)(128)(4,1)}, pred[1024]{0:T(1024)(128)(4,1)S(1)}, u32[]{:S(2)}) copy-start(pred[1024]{0:T(1024)(128)(4,1)S(1)} %compare_reduce_fusion) | copy-start | bytes 3076
  126.3 22.0 %collective-permute-start.2 = (f32[8,12,34,1]{2,0,3,1:T(8,128)S(1)}, f32[8,12,34,1]{2,0,3,1:T(8,128)S(1)}, u32[]{:S(2)}, u32[]{:S(2)}) collective-permute-start(f32[8,12,34,1]{2,0,3,1:T(8,128)S(1)} %copy.55), channel_id=1, source_target_pairs={{0,1},{1,2},{2,3},{4,5},{5,6},{6,7},{8,9},{9,10},{10,11},{12,13},{... | collective-permute-start | bytes 39176 | tf_op jit(solution)/shard_map/ppermute | solution.py:28
  129.3 19.8 %collective-permute-start.3 = (f32[8,12,34,1]{2,0,3,1:T(8,128)S(1)}, f32[8,12,34,1]{2,0,3,1:T(8,128)S(1)}, u32[]{:S(2)}, u32[]{:S(2)}) collective-permute-start(f32[8,12,34,1]{2,0,3,1:T(8,128)S(1)} %copy.56), channel_id=1, source_target_pairs={{1,0},{2,1},{3,2},{5,4},{6,5},{7,6},{9,8},{10,9},{11,10},{13,12},{... | collective-permute-start | bytes 39176 | tf_op jit(solution)/shard_map/ppermute | solution.py:30
  155.3 1.1 copy-start.5
  155.3 1.1 copy-start.8
  155.3 1.1 copy-start.10
  155.3 1.5 copy-start.12
  155.3 1.7 copy-start.14
  155.3 1.8 copy-start.15
  155.3 1.8 copy-start.16
  155.3 1.9 copy-start.17
  155.4 1.9 copy-start.18
  155.4 2.0 copy-start.19
  155.4 2.0 copy-start.20
  155.6 4.8 %copy-start.3 = (f32[12,34,130]{2,1,0:T(8,128)}, f32[12,34,130]{2,1,0:T(8,128)S(1)}, u32[]{:S(2)}) copy-start(f32[12,34,130]{2,1,0:T(8,128)S(1)} %get-tuple-element.21) | copy-start | bytes 636484
  155.7 4.8 %copy-start.11 = (f32[12,34,130]{2,1,0:T(8,128)}, f32[12,34,130]{2,1,0:T(8,128)S(1)}, u32[]{:S(2)}) copy-start(f32[12,34,130]{2,1,0:T(8,128)S(1)} %get-tuple-element.14) | copy-start | bytes 636484
  161.1 63.2 %collective-permute-start.4 = (f32[12,1,128]{2,1,0:T(1,128)}, f32[12,1,128]{2,1,0:T(1,128)}, u32[]{:S(2)}, u32[]{:S(2)}) collective-permute-start(f32[12,1,128]{2,1,0:T(1,128)} %get-tuple-element.30), channel_id=1, source_target_pairs={{4,0},{8,4},{12,8},{16,12},{20,16},{24,20},{28,24},{5,1},{9,5},{13... | collective-permute-start | bytes 18440 | tf_op jit(solution)/shard_map/ppermute | solution.py:30
  162.4 61.9 %collective-permute-start.5 = (f32[12,1,128]{2,1,0:T(1,128)}, f32[12,1,128]{2,1,0:T(1,128)}, u32[]{:S(2)}, u32[]{:S(2)}) collective-permute-start(f32[12,1,128]{2,1,0:T(1,128)} %get-tuple-element.29), channel_id=1, source_target_pairs={{0,4},{4,8},{8,12},{12,16},{16,20},{20,24},{24,28},{1,5},{5,9},{9,... | collective-permute-start | bytes 18440 | tf_op jit(solution)/shard_map/ppermute | solution.py:28
  225.9 18.0 %collective-permute-start.6 = (f32[12,34,1]{2,1,0:T(8,128)}, f32[12,34,1]{2,1,0:T(8,128)}, u32[]{:S(2)}, u32[]{:S(2)}) collective-permute-start(f32[12,34,1]{2,1,0:T(8,128)} %get-tuple-element.27), channel_id=1, source_target_pairs={{1,0},{2,1},{3,2},{5,4},{6,5},{7,6},{9,8},{10,9},{11,10},{13,12},{... | collective-permute-start | bytes 4904 | tf_op jit(solution)/shard_map/ppermute | solution.py:30
  227.2 16.7 %collective-permute-start.7 = (f32[12,34,1]{2,1,0:T(8,128)}, f32[12,34,1]{2,1,0:T(8,128)}, u32[]{:S(2)}, u32[]{:S(2)}) collective-permute-start(f32[12,34,1]{2,1,0:T(8,128)} %get-tuple-element.28), channel_id=1, source_target_pairs={{0,1},{1,2},{2,3},{4,5},{5,6},{6,7},{8,9},{9,10},{10,11},{12,13},{... | collective-permute-start | bytes 4904 | tf_op jit(solution)/shard_map/ppermute | solution.py:28
where the time goes:
time: 253 us; the launch traced here: 250 us
  blocking collectives  120 us (47%)
  other arithmetic  62 us (25%)
  local copies, waits for them, and re-layouts  45.4 us (18%)
  starting transfers between devices  21.1 us (8%)
    psum x2, blocking collectives, body(): reduced = lax.psum(partial_value, ('gx', 'gy'))  78.9 us
    all_gather x1, blocking collectives, body(): lax.all_gather(jnp.stack((well_mode.astype(jnp.float32), well_target)), (...  41.1 us
    gather x2, local copies, waits for them, and re-layouts, body(): at_perf = current.reshape(-1)[perf_slots]  16.7 us
    ppermute x4, starting transfers between devices, extended(): lax.ppermute(tail, axis, [(i, (i + 1) % count) for i in range(ends)])  16 us
    scatter-add x2, other arithmetic, body(): jax.ops.segment_sum(perf_factor * at_perf, well_ids, num_segments=wells_c...  15.4 us
    scatter-add x2, other arithmetic, body(): well_rhs = jnp.zeros((cell_count,), jnp.float32).at[perf_slots].add(perf_...  13.3 us
    gather x2, local copies, waits for them, and re-layouts, body(): every_bhp[well_ids]  9.53 us
    add x2, other arithmetic, body(): current + RELAXATION * (rhs_base + well_rhs - total_diag * current + coup...  8.95 us
  transfers between devices with their start and end apart: 8, of which 0 were waited for; matrix products, arithmetic and copies ran while one was open for 32% of the time, Pallas kernels for 0%

commit v1 on v0

v1 whole, which is shorter than its diff:
```python
import jax
import jax.numpy as jnp
from jax import lax
from jax.experimental import pallas as pl
from jax.experimental.pallas import tpu as pltpu
from jax.sharding import PartitionSpec as P

COMP_OIL = 0.2
COMP_WATER = 0.05
GRAV_OIL = 0.4
GRAV_WATER = 0.5
GRAV_GAS = 0.08
RELAXATION = 0.8
LANES = 128
PLANES = 6
EDGE = 8

F32 = jnp.float32
BF16 = jnp.bfloat16
AXES = ("gx", "gy")


def nn(a, b):
    return lax.dot_general(a, b, (((1,), (0,)), ((), ())), preferred_element_type=F32)


def nt(a, b):
    return lax.dot_general(a, b, (((1,), (1,)), ((), ())), preferred_element_type=F32)


def halves(x):
    high = x.astype(BF16).astype(F32)
    return high, x - high


def iota(shape, dim):
    return lax.broadcasted_iota(jnp.int32, shape, dim)


def hot(index, count):
    return iota((count, index.shape[1]), 0) == index


def ones_of(mask):
    return jnp.where(mask, 1.0, 0.0).astype(BF16)


def bits_of(n):
    assert n & (n - 1) == 0
    return n.bit_length() - 1


def places(index, width):
    return lax.shift_right_arithmetic(index, bits_of(width)), lax.bitwise_and(index, width - 1)


def cell_gather(fields, row, lane):
    rows, lanes = fields[0].shape
    pick = ones_of(hot(lane, lanes))
    pick = jnp.concatenate([pick, pick], axis=0)
    at_row = hot(row, rows)
    found = []
    for field in fields:
        both = jnp.concatenate([part.astype(BF16) for part in halves(field)], axis=1)
        found.append(jnp.sum(jnp.where(at_row, nn(both, pick), 0.0), axis=0, keepdims=True))
    return found


def cell_scatter(value, row, lane, rows, lanes):
    spread = jnp.where(hot(lane, lanes), value, 0.0)
    spread = jnp.concatenate([part.astype(BF16) for part in halves(spread)], axis=0)
    total = nt(ones_of(hot(row, rows)), spread)
    return total[:, :lanes] + total[:, lanes:]


def well_scatter(values, row, lane, rows):
    mine = hot(row, rows)
    stack = []
    for value in values:
        stack.extend(halves(jnp.where(mine, value, 0.0)))
    total = nt(jnp.concatenate(stack, axis=0).astype(BF16), ones_of(hot(lane, LANES)))
    return [
        total[2 * i * rows : (2 * i + 1) * rows] + total[(2 * i + 1) * rows : (2 * i + 2) * rows]
        for i in range(len(values))
    ]


def well_gather(field, row, lane):
    rows = field.shape[0]
    both = jnp.concatenate(halves(field), axis=0).astype(BF16)
    found = nn(both, ones_of(hot(lane, LANES)))
    return jnp.sum(
        jnp.where(hot(row, rows), found[:rows] + found[rows:], 0.0), axis=0, keepdims=True
    )


def total_mobility(sat_water, sat_gas):
    sat_oil = 1.0 - sat_water - sat_gas
    return 0.5 * sat_oil * sat_oil + sat_water * sat_water + 5.0 * (sat_gas * sat_gas)


def phase_mobility(pressure, sat_water, sat_gas):
    sat_oil = 1.0 - sat_water - sat_gas
    b_oil = 1.0 + COMP_OIL * (pressure - 1.0)
    b_water = 1.0 + COMP_WATER * (pressure - 1.0)
    return (
        sat_oil * sat_oil * b_oil * 0.5,
        sat_water * sat_water * b_water,
        sat_gas * sat_gas * pressure * 5.0,
    )


def live_index(well_ref, index_ref):
    return jnp.where(well_ref[...] >= 0, index_ref[...], 0.0)


def first_wells(press_ref, sat_ref, cell_ref, well_ref, index_ref, mode_ref, target_ref, out_ref):
    layers, width, lanes = press_ref.shape
    rows = layers * width
    owned = mode_ref.shape[1]
    group = LANES // owned
    me = lax.axis_index(AXES)
    row, lane = places(cell_ref[...], lanes)
    well_row, well_lane = places(well_ref[...], LANES)
    sat = sat_ref[...].reshape(2, rows, lanes)
    mobility = total_mobility(sat[0], sat[1])
    press = press_ref[...].reshape(rows, lanes)
    at_mob, at_press = cell_gather([mobility, mobility * press], row, lane)
    index = live_index(well_ref, index_ref)
    chunk_rows = first_rows(out_ref)
    well_rows = (chunk_rows - 2) // 2
    part, base = well_scatter([index * at_press, index * at_mob], well_row, well_lane, well_rows)
    here = lax.shift_right_logical(iota((1, LANES), 1), bits_of(owned)) == lax.rem(me, group)
    controls = [
        jnp.where(here, jnp.concatenate([ref[...].astype(F32)] * group, axis=1), 0.0)
        for ref in (mode_ref, target_ref)
    ]
    block = jnp.concatenate([part, base] + controls, axis=0)
    block = jnp.concatenate([block] * 4, axis=0)
    height = block.shape[0]
    for i in range(out_ref.shape[0] // height):
        out_ref[i * height : (i + 1) * height, :] = block


def first_rows(out_ref):
    count = lax.axis_size("gx") * lax.axis_size("gy")
    return out_ref.shape[0] // count


def pack(after_ref, press_ref, sat_ref, perm_ref, depth_ref, flag_ref, xup_ref, xdn_ref, yup_ref, ydn_ref):
    layers, width, lanes = press_ref.shape
    rows = layers * width
    flags = flag_ref[...]
    bit_y = lax.bitwise_and(lax.shift_right_logical(flags, 1), 1).astype(F32)
    last = width - 1
    for edge, out_ref in ((last, xup_ref), (0, xdn_ref)):
        fields = [
            press_ref[:, edge, :],
            sat_ref[0, :, edge, :],
            sat_ref[1, :, edge, :],
            perm_ref[0, :, edge, :],
            depth_ref[:, edge, :],
            lax.bitwise_and(flag_ref[:, edge, :], 1).astype(F32),
        ]
        for i, field in enumerate(fields):
            out_ref[i * layers : (i + 1) * layers, :] = field
    planes = [press_ref[...], sat_ref[0], sat_ref[1], perm_ref[1], depth_ref[...], bit_y]
    pick_row, pick_lane = iota((2 * EDGE, 2 * lanes), 0), lax.rem(iota((2 * EDGE, 2 * lanes), 1), lanes)
    total = jnp.zeros((2 * EDGE, rows), F32)
    for i, plane in enumerate(planes):
        both = jnp.concatenate([part.astype(BF16) for part in halves(plane.reshape(rows, lanes))], axis=1)
        pick = ones_of(
            ((pick_row == i) & (pick_lane == lanes - 1)) | ((pick_row == EDGE + i) & (pick_lane == 0))
        )
        total = total + nt(pick, both)
    yup_ref[...] = total[:EDGE]
    ydn_ref[...] = total[EDGE:]


def upright(rows_list, lanes):
    stack = jnp.concatenate(rows_list, axis=0)
    stack = jnp.concatenate([stack, jnp.zeros((lanes - stack.shape[0], stack.shape[1]), F32)], axis=0)
    return jnp.transpose(stack)


def faces(perm, perm_next, mob, mob_next, first_up):
    transmit = 2.0 * perm * perm_next / (perm + perm_next)
    return [transmit * jnp.where(first_up, a, b) for a, b in zip(mob, mob_next)]


def main_terms(
    press_ref, sat_ref, perm_ref, pore_ref, depth_ref, res_ref, flag_ref, cell_ref, well_ref, index_ref,
    xup_ref, xdn_ref, yup_ref, ydn_ref,
    coup_ref, rhs_ref, gain_ref, start_ref, mob_ref,
    side_ref, share_ref,
):
    layers, width, lanes = press_ref.shape
    rows = layers * width
    row, lane = places(cell_ref[...], lanes)
    share_ref[...] = cell_scatter(live_index(well_ref, index_ref), row, lane, rows, lanes)
    stand = upright([yup_ref[...], ydn_ref[...]], lanes)
    stand = jnp.concatenate([part.astype(BF16) for part in halves(stand)], axis=1)
    wide = (2 * lanes, PLANES * lanes)
    from_lane = lax.rem(iota(wide, 0), lanes)
    to_plane, to_lane = places(iota(wide, 1), lanes)
    side_ref[...] = nn(
        stand,
        ones_of(
            ((from_lane == to_plane) & (to_lane == 0))
            | ((from_lane == to_plane + EDGE) & (to_lane == lanes - 1))
        ),
    )
    sub = iota((width, lanes), 0)
    along = iota((width, lanes), 1)
    x_first, x_last = sub == 0, sub == width - 1
    y_first, y_last = along == 0, along == lanes - 1

    def x_next(a, edge):
        return jnp.where(x_last, edge, pltpu.roll(a, width - 1, 0))

    def x_prev(a, edge):
        return jnp.where(x_first, edge, pltpu.roll(a, 1, 0))

    def y_next(a, edge):
        return jnp.where(y_last, edge, pltpu.roll(a, lanes - 1, 1))

    def y_prev(a, edge):
        return jnp.where(y_first, edge, pltpu.roll(a, 1, 1))

    def layer(z):
        press = press_ref[z]
        return press, phase_mobility(press, sat_ref[0, z], sat_ref[1, z])

    this = layer(0)
    before = None
    for z in range(layers):
        press, mob = this
        following = layer(z + 1) if z + 1 < layers else None
        sat_water, sat_gas = sat_ref[0, z], sat_ref[1, z]
        sat_oil = 1.0 - sat_water - sat_gas
        depth = depth_ref[z]
        flags = flag_ref[z]
        w_oil = 1.0 / (1.0 + COMP_OIL * (press - 1.0))
        w_water = 1.0 / (1.0 + COMP_WATER * (press - 1.0))
        w_gas = 1.0 / press
        storage = pore_ref[z] * (
            sat_oil * COMP_OIL * w_oil + sat_water * COMP_WATER * w_water + sat_gas * w_gas
        )
        couplings, besides, gravity = [], [], jnp.zeros_like(press)

        def add(flux, drop, beside):
            nonlocal gravity
            oil, water, gas = w_oil * flux[0], w_water * flux[1], w_gas * flux[2]
            couplings.append(oil + water + gas)
            gravity = gravity + (GRAV_OIL * oil + GRAV_WATER * water + GRAV_GAS * gas) * drop
            besides.append(beside)

        perm = perm_ref[0, z]
        up = [xup_ref[i * layers + z : i * layers + z + 1, :] for i in range(PLANES)]
        dn = [xdn_ref[i * layers + z : i * layers + z + 1, :] for i in range(PLANES)]
        mob_up, mob_dn = phase_mobility(*up[:3]), phase_mobility(*dn[:3])
        bit = lax.bitwise_and(flags, 1) > 0
        flux = faces(
            perm, x_next(perm, dn[3]), mob, [x_next(a, b) for a, b in zip(mob, mob_dn)], bit
        )
        drop = depth - x_next(depth, dn[4])
        add(flux, drop, x_next(press, dn[0]))
        edge = faces(up[3], perm[:1], mob_up, [a[:1] for a in mob], up[5] > 0.5)
        add(
            [x_prev(a, b) for a, b in zip(flux, edge)],
            -x_prev(drop, up[4] - depth[:1]),
            x_prev(press, up[0]),
        )
        perm = perm_ref[1, z]
        side = [
            side_ref[z * width : (z + 1) * width, i * lanes : (i + 1) * lanes] for i in range(PLANES)
        ]
        mob_side = phase_mobility(*side[:3])
        bit = lax.bitwise_and(flags, 2) > 0
        flux = faces(
            perm, y_next(perm, side[3]), mob, [y_next(a, b) for a, b in zip(mob, mob_side)], bit
        )
        drop = depth - y_next(depth, side[4])
        add(flux, drop, y_next(press, side[0]))
        edge = faces(side[3], perm, mob_side, mob, side[5] > 0.5)
        add(
            [y_prev(a, b) for a, b in zip(flux, edge)],
            -y_prev(drop, side[4] - depth),
            y_prev(press, side[0]),
        )
        if following is not None:
            bit = lax.bitwise_and(flags, 4) > 0
            flux = faces(perm_ref[2, z], perm_ref[2, z + 1], mob, following[1], bit)
            drop = depth - depth_ref[z + 1]
            add(flux, drop, following[0])
            after = (flux, drop, press)
        else:
            coup_ref[4, z] = jnp.zeros_like(press)
            after = None
        if before is not None:
            add(before[0], -before[1], before[2])
        else:
            coup_ref[5, z] = jnp.zeros_like(press)
        names = [0, 1, 2, 3] + ([4] if following is not None else []) + ([5] if before is not None else [])
        mobility = total_mobility(sat_water, sat_gas)
        diag = storage + mobility * share_ref[z * width : (z + 1) * width, :]
        for coupling in couplings:
            diag = diag + coupling
        scale = RELAXATION / diag
        rhs = (
            storage * press
            - (w_oil * res_ref[0, z] + w_water * res_ref[1, z] + w_gas * res_ref[2, z])
            + gravity
        )
        rhs = scale * rhs
        start = (1.0 - RELAXATION) * press + rhs
        for name, coupling, beside in zip(names, couplings, besides):
            scaled = scale * coupling
            coup_ref[name, z] = scaled
            start = start + scaled * beside
        rhs_ref[z] = rhs
        gain_ref[z] = scale * mobility
        start_ref[z] = start
        mob_ref[z] = mobility
        before, this = after, following


def slot_bhp(bhp, well_ref, index_ref):
    well_row, well_lane = places(well_ref[...], LANES)
    return live_index(well_ref, index_ref) * well_gather(bhp, well_row, well_lane)


def first_update(
    sums_ref, cell_ref, well_ref, index_ref, start_ref, gain_ref, mob_ref,
    cur_ref, out_ref, xup_ref, xdn_ref, known_ref,
):
    layers, width, lanes = start_ref.shape
    rows = layers * width
    count = lax.axis_size("gx") * lax.axis_size("gy")
    chunk = sums_ref.shape[0] // count
    well_rows = (chunk - 2) // 2
    group = count // well_rows
    my = lax.axis_index("gy")
    part = sums_ref[0:well_rows, :]
    base = sums_ref[well_rows : 2 * well_rows, :]
    for d in range(1, count):
        part = part + sums_ref[d * chunk : d * chunk + well_rows, :]
        base = base + sums_ref[d * chunk + well_rows : d * chunk + 2 * well_rows, :]
    controls = []
    for k in (2 * well_rows, 2 * well_rows + 1):
        total = sums_ref[pl.ds(k, well_rows, stride=group * chunk), :]
        for j in range(1, group):
            total = total + sums_ref[pl.ds(j * chunk + k, well_rows, stride=group * chunk), :]
        controls.append(total)
    mode, target = controls
    bhp = jnp.where(mode < 0.5, target, (part - target) / base)
    known_ref[0] = mode
    known_ref[1] = target
    known_ref[2] = base
    row, lane = places(cell_ref[...], lanes)
    well_row, well_lane = places(well_ref[...], LANES)
    push = cell_scatter(slot_bhp(bhp, well_ref, index_ref), row, lane, rows, lanes)
    start = start_ref[...].reshape(rows, lanes)
    gain = gain_ref[...].reshape(rows, lanes)
    current = start + gain * push
    cur_ref[...] = current.reshape(layers, width, lanes)
    xup_ref[...] = cur_ref[:, width - 1, :]
    xdn_ref[...] = cur_ref[:, 0, :]
    (at_cell,) = cell_gather([mob_ref[...].reshape(rows, lanes) * current], row, lane)
    (part,) = well_scatter([live_index(well_ref, index_ref) * at_cell], well_row, well_lane, well_rows)
    both = jnp.concatenate([half.astype(BF16) for half in halves(current)], axis=1)
    pick_row, pick_lane = iota((2 * EDGE, 2 * lanes), 0), lax.rem(iota((2 * EDGE, 2 * lanes), 1), lanes)
    rims = nt(
        ones_of(((pick_row == 0) & (pick_lane == lanes - 1)) | ((pick_row == 1) & (pick_lane == 0))), both
    )
    pieces = rows // LANES
    split = [
        jnp.concatenate([rims[r : r + 1, i * LANES : (i + 1) * LANES] for i in range(pieces)], axis=0)
        for r in range(2)
    ]
    height = well_rows + pieces
    ends = lax.axis_size("gy")
    for d in range(count):
        out_ref[d * height : d * height + well_rows, :] = part
        out_ref[d * height + well_rows : (d + 1) * height, :] = jnp.where(
            d % ends > my, split[0], split[1]
        )


def last_update(
    sums_ref, known_ref, cell_ref, well_ref, index_ref, cur_ref, coup_ref, rhs_ref, gain_ref,
    xup_ref, xdn_ref, out_ref, bhp_ref, push_ref, side_ref,
):
    layers, width, lanes = cur_ref.shape
    rows = layers * width
    count = lax.axis_size("gx") * lax.axis_size("gy")
    height = sums_ref.shape[0] // count
    well_rows = known_ref.shape[1]
    pieces = height - well_rows
    me = lax.axis_index(AXES)
    part = sums_ref[0:well_rows, :]
    for d in range(1, count):
        part = part + sums_ref[d * height : d * height + well_rows, :]
    bhp = jnp.where(known_ref[0] < 0.5, known_ref[1], (part - known_ref[1]) / known_ref[2])
    owned = bhp_ref.shape[1]
    group = LANES // owned
    line = jnp.sum(
        jnp.where(iota(bhp.shape, 0) == me // group, bhp, 0.0), axis=0, keepdims=True
    )
    line = pltpu.roll(line, lax.rem(LANES - lax.rem(me, group) * owned, LANES), 1)
    bhp_ref[...] = line[:, :owned]
    row, lane = places(cell_ref[...], lanes)
    push_ref[...] = cell_scatter(slot_bhp(bhp, well_ref, index_ref), row, lane, rows, lanes)
    strips = []
    for beside in (jnp.maximum(me - 1, 0), jnp.minimum(me + 1, count - 1)):
        strips.append(
            jnp.concatenate(
                [sums_ref[pl.ds(beside * height + well_rows + i, 1), :] for i in range(pieces)], axis=1
            )
        )
    side_ref[...] = upright(strips, lanes)
    sub = iota((width, lanes), 0)
    along = iota((width, lanes), 1)
    for z in range(layers):
        here = slice(z * width, (z + 1) * width)
        current = cur_ref[z]
        side = side_ref[here, :]
        besides = [
            jnp.where(sub == width - 1, xdn_ref[z : z + 1, :], pltpu.roll(current, width - 1, 0)),
            jnp.where(sub == 0, xup_ref[z : z + 1, :], pltpu.roll(current, 1, 0)),
            jnp.where(along == lanes - 1, pltpu.roll(side, lanes - 2, 1), pltpu.roll(current, lanes - 1, 1)),
            jnp.where(along == 0, side, pltpu.roll(current, 1, 1)),
            cur_ref[z + 1] if z + 1 < layers else None,
            cur_ref[z - 1] if z > 0 else None,
        ]
        total = (1.0 - RELAXATION) * current + rhs_ref[z] + gain_ref[z] * push_ref[here, :]
        for i, beside in enumerate(besides):
            if beside is not None:
                total = total + coup_ref[i, z] * beside
        out_ref[z] = total


def call(kernel, out_shapes, args, scratch=(), flops=1_000_000):
    shapes = [jax.ShapeDtypeStruct(s, F32) for s in out_shapes]
    return pl.pallas_call(
        kernel,
        out_shape=shapes,
        in_specs=[pl.BlockSpec(memory_space=pltpu.VMEM)] * len(args),
        out_specs=[pl.BlockSpec(memory_space=pltpu.VMEM)] * len(shapes),
        scratch_shapes=[pltpu.VMEM(s, F32) for s in scratch],
        compiler_params=pltpu.CompilerParams(vmem_limit_bytes=32 * 1024 * 1024),
        cost_estimate=pl.CostEstimate(flops=flops, bytes_accessed=4_000_000, transcendentals=0),
    )(*args)


def everyone(rows, count):
    height = rows.shape[0] // count
    swapped = lax.all_to_all(rows.reshape(count, height, 1, LANES), AXES, 0, 0, tiled=True)
    return swapped.reshape(rows.shape)


def shifted(up, down, axis):
    count = lax.axis_size(axis)
    return (
        lax.ppermute(up, axis, [(i, i + 1) for i in range(count - 1)]),
        lax.ppermute(down, axis, [(i + 1, i) for i in range(count - 1)]),
    )


def body(
    pressure, saturation, permeability, pore_volume, cell_depth, residual, upstream_flags,
    perf_cell, perf_well, perf_index, well_mode, well_target,
):
    layers, width, lanes = pressure.shape
    rows = layers * width
    count = lax.axis_size("gx") * lax.axis_size("gy")
    owned = well_mode.shape[0]
    well_rows = owned * count // LANES
    chunk = 2 * well_rows + 2
    (sums,) = call(
        first_wells,
        [(count * chunk, LANES)],
        [pressure, saturation, perf_cell, perf_well, perf_index, well_mode[None], well_target[None]],
    )
    gathered = everyone(sums, count)
    xup, xdn, yup, ydn = call(
        pack,
        [(PLANES * layers, lanes)] * 2 + [(EDGE, rows)] * 2,
        [sums[:8], pressure, saturation, permeability, cell_depth, upstream_flags],
    )
    xup, xdn = shifted(xup, xdn, "gx")
    yup, ydn = shifted(yup, ydn, "gy")
    grid = (layers, width, lanes)
    coup, rhs, gain, start, mobility = call(
        main_terms,
        [(6,) + grid, grid, grid, grid, grid],
        [
            pressure, saturation, permeability, pore_volume, cell_depth, residual, upstream_flags,
            perf_cell, perf_well, perf_index, xup, xdn, yup, ydn,
        ],
        [(rows, PLANES * lanes), (rows, lanes)],
    )
    pieces = rows // LANES
    current, sums, xup, xdn, known = call(
        first_update,
        [grid, (count * (well_rows + pieces), LANES), (layers, lanes), (layers, lanes), (3, well_rows, LANES)],
        [gathered, perf_cell, perf_well, perf_index, start, gain, mobility],
    )
    gathered = everyone(sums, count)
    xup, xdn = shifted(xup, xdn, "gx")
    out, bhp = call(
        last_update,
        [grid, (1, owned)],
        [gathered, known, perf_cell, perf_well, perf_index, current, coup, rhs, gain, xup, xdn],
        [(rows, lanes), (rows, lanes)],
    )
    return out, bhp[0]


def solution(mesh):
    return jax.shard_map(
        body,
        mesh=mesh,
        in_specs=(
            P(None, "gx", "gy"),
            P(None, None, "gx", "gy"),
            P(None, None, "gx", "gy"),
            P(None, "gx", "gy"),
            P(None, "gx", "gy"),
            P(None, None, "gx", "gy"),
            P(None, "gx", "gy"),
            P(("gx", "gy"), None),
            P(("gx", "gy"), None),
            P(("gx", "gy"), None),
            P(("gx", "gy")),
            P(("gx", "gy")),
        ),
        out_specs=(P(None, "gx", "gy"), P(("gx", "gy"))),
        check_vma=False,
    )
```

time: 253 us -> 52.8 us (0.21)
  blocking collectives: 120 us -> 0 us
  other arithmetic: 62 us -> 0 us
  local copies, waits for them, and re-layouts: 45.4 us -> 7.59 us
  Pallas kernels: 0 us -> 8.39 us
  waiting for transfers between devices: 0.02 us -> 7.27 us
  starting transfers between devices: 21.1 us -> 28.1 us
    psum x2 -> x0, blocking collectives: 78.9 us -> none  [body(): reduced = lax.psum(partial_value, ('gx', 'gy'))]
    scatter-add x6 -> x0, other arithmetic: 42.8 us -> none  [the longest x2 15.4 us: body(): jax.ops.segment_sum(perf_factor * at_perf, well_ids, num_segments=wells_c...]
    all_gather x1 -> x0, blocking collectives: 41.1 us -> none  [body(): lax.all_gather(jnp.stack((well_mode.astype(jnp.float32), well_target)), (...]
    gather x5 -> x0, local copies, waits for them, and re-layouts: 32.4 us -> none  [the longest x2 16.7 us: body(): at_perf = current.reshape(-1)[perf_slots]]
    all_to_all x0 -> x2, starting transfers between devices: none -> 15.1 us  [everyone(): lax.all_to_all(rows.reshape(count, height, 1, LANES), AXES, 0, 0, tiled=T...]
    add x3 -> x0, other arithmetic: 11 us -> none  [the longest x2 8.95 us: body(): current + RELAXATION * (rhs_base + well_rhs - total_diag * current + coup...]
    pallas_call x0 -> x5, Pallas kernels: none -> 8.39 us  [call(): pl.pallas_call(kernel, out_shape=shapes, in_specs=[pl.BlockSpec(memory_sp...]
    ppermute x8 -> x6, starting transfers between devices: 21.1 us -> 13 us  [the longest x3 9.13 us: shifted(): lax.ppermute(up, axis, [(i, i + 1) for i in range(count - 1)])]
  transfers between devices with their start and end apart: 8 -> 8, of which waited for: 0 -> 2; matrix products, arithmetic and copies ran while one was open for 32% -> 1% of each run, Pallas kernels for 0% -> 6%
where the time goes in v1:
time: 52.8 us; the launch traced here: 52.2 us
  starting transfers between devices  28.1 us (53%)
  Pallas kernels  8.39 us (16%)
  local copies, waits for them, and re-layouts  7.59 us (14%)
  waiting for transfers between devices  7.27 us (14%)
  between operations  0.8 us (2%)
    all_to_all x2, starting transfers between devices, everyone(): lax.all_to_all(rows.reshape(count, height, 1, LANES), AXES, 0, 0, tiled=T...  15.1 us
    ppermute x3, starting transfers between devices, shifted(): lax.ppermute(up, axis, [(i, i + 1) for i in range(count - 1)])  9.13 us
    pallas_call x5, Pallas kernels, call(): pl.pallas_call(kernel, out_shape=shapes, in_specs=[pl.BlockSpec(memory_sp...  8.39 us
    ppermute x3, waiting for transfers between devices, shifted(): lax.ppermute(down, axis, [(i + 1, i) for i in range(count - 1)])  7.21 us
    unnamed x38, local copies, waits for them, and re-layouts  6.91 us
    ppermute x3, starting transfers between devices, shifted(): lax.ppermute(down, axis, [(i + 1, i) for i in range(count - 1)])  3.88 us
  transfers between devices with their start and end apart: 8, of which 2 were waited for; matrix products, arithmetic and copies ran while one was open for 1% of the time, Pallas kernels for 6%

profile of v1, /device:TPU:0, one launch (start us, length us, event | category | flops | bytes accessed | tf_op | source)
XLA Modules:
  0.0 52.2 jit_solution(3977148197948579100)
XLA Ops:
  0.6 0.0 copy-start
  0.6 1.0 %copy-done = f32[2,12,32,128]{3,2,1,0:T(8,128)S(1)} copy-done((f32[2,12,32,128]{3,2,1,0:T(8,128)S(1)}, f32[2,12,32,128]{3,2,1,0:T(8,128)}, u32[]{:S(2)}) %copy-start) | copy-done | bytes 393240
  1.6 0.0 copy-start.3
  1.6 0.9 %copy-done.3 = f32[12,32,128]{2,1,0:T(8,128)S(1)} copy-done((f32[12,32,128]{2,1,0:T(8,128)S(1)}, f32[12,32,128]{2,1,0:T(8,128)}, u32[]{:S(2)}) %copy-start.3) | copy-done | bytes 196632
  2.6 0.0 copy-start.11
  2.6 0.7 %copy-done.11 = s32[1,1024]{1,0:T(1,128)S(1)} copy-done((s32[1,1024]{1,0:T(1,128)S(1)}, s32[1,1024]{1,0:T(1,128)}, u32[]{:S(2)}) %copy-start.11) | copy-done | bytes 4120
  3.2 0.0 copy-start.13
  3.2 0.7 %copy-done.13 = s32[1,1024]{1,0:T(1,128)S(1)} copy-done((s32[1,1024]{1,0:T(1,128)S(1)}, s32[1,1024]{1,0:T(1,128)}, u32[]{:S(2)}) %copy-start.13) | copy-done | bytes 4120
  3.9 0.0 copy-start.15
  3.9 0.7 %copy-done.15 = f32[1,1024]{1,0:T(1,128)S(1)} copy-done((f32[1,1024]{1,0:T(1,128)S(1)}, f32[1,1024]{1,0:T(1,128)}, u32[]{:S(2)}) %copy-start.15) | copy-done | bytes 4120
  4.6 0.0 copy-start.17
  4.6 0.7 %copy-done.17 = s32[32]{0:T(128)S(1)} copy-done((s32[32]{0:T(128)S(1)}, s32[32]{0:T(128)}, u32[]{:S(2)}) %copy-start.17) | copy-done | bytes 152
  5.3 0.0 copy-start.18
  5.3 0.7 %copy-done.18 = f32[32]{0:T(128)S(1)} copy-done((f32[32]{0:T(128)S(1)}, f32[32]{0:T(128)}, u32[]{:S(2)}) %copy-start.18) | copy-done | bytes 152
  5.9 0.0 copy-start.1
  5.9 0.0 copy-start.2
  5.9 0.0 copy-start.4
  5.9 0.0 copy-start.5
  5.9 1.7 %shard_map.131 = f32[576,128]{1,0:T(8,128)} custom-call(f32[12,32,128]{2,1,0:T(8,128)S(1)} %copy-done.3, f32[2,12,32,128]{3,2,1,0:T(8,128)S(1)} %copy-done, s32[1,1024]{1,0:T(1,128)S(1)} %copy-done.11, s32[1,1024]{1,0:T(1,128)S(1)} %copy-done.13, f32[1,1024]{1,0:T(1,128)S(1)} %copy-done.15, s32[1,32]{1,0:T(1,128)S(1)} %bitcast.9, f32[1,32]{1,0:T(1,128)S(1)} %bitcast.10), custom_call_target="tpu_custom_call" | custom-call | flops 1000000 | bytes 4000000 | tf_op jit(solution)/shard_map/pallas_call | solution.py:445
  7.7 0.0 copy-start.12
  7.7 0.0 copy-start.14
  7.7 0.0 copy-start.16
  7.7 7.3 %all-to-all-start = ((f32[32,18,1,128]{3,2,1,0:T(1,128)}), f32[32,18,1,128]{3,2,1,0:T(1,128)S(1)}, u32[]{:S(2)}, u32[]{:S(2)}) async-start(f32[32,18,1,128]{3,2,1,0:T(1,128)} %bitcast.2), calls=%async_computation | async-start | bytes 589824 | tf_op jit(solution)/shard_map/all_to_all | solution.py:458
  15.0 0.7 %slice.4.after_ref = f32[8,128]{1,0:T(8,128)S(1)} slice(f32[576,128]{1,0:T(8,128)} %shard_map.131), slice={[0:8], [0:128]} | slice | bytes 8192 | tf_op jit(solution)/shard_map/slice | solution.py:489
  15.7 0.0 copy-done.1
  15.7 0.0 copy-done.2
  15.7 0.0 copy-done.4
  15.7 0.0 copy-done.5
  15.7 0.0 copy-start.6
  15.7 0.9 %copy-done.6 = s32[12,32,128]{2,1,0:T(8,128)S(1)} copy-done((s32[12,32,128]{2,1,0:T(8,128)S(1)}, s32[12,32,128]{2,1,0:T(8,128)}, u32[]{:S(2)}) %copy-start.6) | copy-done | bytes 196632
  16.6 0.0 copy-start.7
  16.6 0.0 copy-start.8
  16.6 0.5 shard_map.132
  17.1 3.7 %collective-permute-start = (f32[72,128]{1,0:T(8,128)S(1)}, f32[72,128]{1,0:T(8,128)S(1)}, u32[]{:S(2)}, u32[]{:S(2)}) collective-permute-start(f32[72,128]{1,0:T(8,128)S(1)} %get-tuple-element.18), channel_id=1, source_target_pairs={{0,4},{4,8},{8,12},{12,16},{16,20},{20,24},{24,28},{1,5},{5,9},{9,... | collective-permute-start | bytes 110600 | tf_op jit(solution)/shard_map/ppermute | solution.py:465
  20.8 1.3 %collective-permute-start.1 = (f32[72,128]{1,0:T(8,128)S(1)}, f32[72,128]{1,0:T(8,128)S(1)}, u32[]{:S(2)}, u32[]{:S(2)}) collective-permute-start(f32[72,128]{1,0:T(8,128)S(1)} %get-tuple-element.19), channel_id=1, source_target_pairs={{4,0},{8,4},{12,8},{16,12},{20,16},{24,20},{28,24},{5,1},{9,5},{13... | collective-permute-start | bytes 110600 | tf_op jit(solution)/shard_map/ppermute | solution.py:466
  22.1 1.8 %collective-permute-start.2 = (f32[8,384]{1,0:T(8,128)S(1)}, f32[8,384]{1,0:T(8,128)S(1)}, u32[]{:S(2)}, u32[]{:S(2)}) collective-permute-start(f32[8,384]{1,0:T(8,128)S(1)} %get-tuple-element.20), channel_id=1, source_target_pairs={{0,1},{1,2},{2,3},{4,5},{5,6},{6,7},{8,9},{9,10},{10,11},{12,13},{... | collective-permute-start | bytes 36872 | tf_op jit(solution)/shard_map/ppermute | solution.py:465
  23.9 1.3 %collective-permute-start.3 = (f32[8,384]{1,0:T(8,128)S(1)}, f32[8,384]{1,0:T(8,128)S(1)}, u32[]{:S(2)}, u32[]{:S(2)}) collective-permute-start(f32[8,384]{1,0:T(8,128)S(1)} %get-tuple-element.21), channel_id=1, source_target_pairs={{1,0},{2,1},{3,2},{5,4},{6,5},{7,6},{9,8},{10,9},{11,10},{13,12},{... | collective-permute-start | bytes 36872 | tf_op jit(solution)/shard_map/ppermute | solution.py:466
  25.2 0.0 collective-permute-done.2.yup_ref
  25.2 3.0 %collective-permute-done.3.ydn_ref = f32[8,384]{1,0:T(8,128)S(1)} collective-permute-done((f32[8,384]{1,0:T(8,128)S(1)}, f32[8,384]{1,0:T(8,128)S(1)}, u32[]{:S(2)}, u32[]{:S(2)}) %collective-permute-start.3) | collective-permute-done | bytes 12320 | tf_op jit(solution)/shard_map/ppermute | solution.py:466
  28.2 0.0 collective-permute-done.xup_ref
  28.2 0.0 collective-permute-done.1.xdn_ref
  28.2 0.0 copy-done.12
  28.2 0.0 copy-done.14
  28.2 0.0 copy-done.16
  28.2 0.0 copy-done.7
  28.2 0.0 copy-done.8
  28.2 2.6 %shard_map.133 = (f32[6,12,32,128]{3,2,1,0:T(8,128)S(1)}, f32[12,32,128]{2,1,0:T(8,128)S(1)}, f32[12,32,128]{2,1,0:T(8,128)S(1)}, f32[12,32,128]{2,1,0:T(8,128)S(1)}, f32[12,32,128]{2,1,0:T(8,128)S(1)}) custom-call(f32[12,32,128]{2,1,0:T(8,128)S(1)} %copy-done.4, f32[2,12,32,128]{3,2,1,0:T(8,128)S(1)} %copy-done.1, f32[3,12,32,128]{3,2,1,0:T(8,128)S(1)} %copy-done.2, ...), custom_call_target="tpu_custom_call" | custom-call | flops 1000000 | bytes 4000000 | tf_op jit(solution)/shard_map/pallas_call | solution.py:445
  30.8 0.0 copy-start.9
  30.9 0.7 %copy-done.9 = f32[12,32,128]{2,1,0:T(8,128)} copy-done((f32[12,32,128]{2,1,0:T(8,128)}, f32[12,32,128]{2,1,0:T(8,128)S(1)}, u32[]{:S(2)}) %copy-start.9) | copy-done | bytes 196632
  31.5 0.0 all-to-all-done
  31.5 0.0 copy-start.10
  31.5 2.2 %shard_map.134 = (f32[12,32,128]{2,1,0:T(8,128)S(1)}, f32[352,128]{1,0:T(8,128)}, f32[12,128]{1,0:T(8,128)S(1)}, f32[12,128]{1,0:T(8,128)S(1)}, f32[3,8,128]{2,1,0:T(8,128)S(1)}) custom-call(f32[576,128]{1,0:T(8,128)S(1)} %bitcast.7, s32[1,1024]{1,0:T(1,128)S(1)} %copy-done.12, s32[1,1024]{1,0:T(1,128)S(1)} %copy-done.14, f32[1,1024]{1,0:T(1,128)S(1)} %copy-done.16, ...), custom_call_target="tpu_custom_call" | custom-call | flops 1000000 | bytes 4000000 | tf_op jit(solution)/shard_map/pallas_call | solution.py:445
  33.7 7.8 %all-to-all-start.1 = ((f32[32,11,1,128]{3,2,1,0:T(1,128)}), f32[32,11,1,128]{3,2,1,0:T(1,128)S(1)}, u32[]{:S(2)}, u32[]{:S(2)}) async-start(f32[32,11,1,128]{3,2,1,0:T(1,128)} %bitcast.4), calls=%async_computation.1 | async-start | bytes 360448 | tf_op jit(solution)/shard_map/all_to_all | solution.py:458
  41.5 3.7 %collective-permute-start.4 = (f32[12,128]{1,0:T(8,128)S(1)}, f32[12,128]{1,0:T(8,128)S(1)}, u32[]{:S(2)}, u32[]{:S(2)}) collective-permute-start(f32[12,128]{1,0:T(8,128)S(1)} %get-tuple-element.30), channel_id=1, source_target_pairs={{0,4},{4,8},{8,12},{12,16},{16,20},{20,24},{24,28},{1,5},{5,9},{9,... | collective-permute-start | bytes 18440 | tf_op jit(solution)/shard_map/ppermute | solution.py:465
  45.2 1.3 %collective-permute-start.5 = (f32[12,128]{1,0:T(8,128)S(1)}, f32[12,128]{1,0:T(8,128)S(1)}, u32[]{:S(2)}, u32[]{:S(2)}) collective-permute-start(f32[12,128]{1,0:T(8,128)S(1)} %get-tuple-element.31), channel_id=1, source_target_pairs={{4,0},{8,4},{12,8},{16,12},{20,16},{24,20},{28,24},{5,1},{9,5},{13... | collective-permute-start | bytes 18440 | tf_op jit(solution)/shard_map/ppermute | solution.py:466
  46.5 0.0 collective-permute-done.4.xup_ref
  46.6 4.2 %collective-permute-done.5.xdn_ref = f32[12,128]{1,0:T(8,128)S(1)} collective-permute-done((f32[12,128]{1,0:T(8,128)S(1)}, f32[12,128]{1,0:T(8,128)S(1)}, u32[]{:S(2)}, u32[]{:S(2)}) %collective-permute-start.5) | collective-permute-done | bytes 6176 | tf_op jit(solution)/shard_map/ppermute | solution.py:466
  50.8 0.0 all-to-all-done.1
  50.8 0.0 copy-done.10
  50.8 1.4 %shard_map.135 = (f32[12,32,128]{2,1,0:T(8,128)}, f32[1,32]{1,0:T(1,128)}) custom-call(f32[352,128]{1,0:T(8,128)S(1)} %bitcast.8, f32[3,8,128]{2,1,0:T(8,128)S(1)} %get-tuple-element.26.known_ref, s32[1,1024]{1,0:T(1,128)S(1)} %copy-done.12, s32[1,1024]{1,0:T(1,128)S(1)} %copy-done.14, f32[1,1024]{1,0:T(1,128)S(1)} %copy-done.16, ...), custom_call_target="tpu_custom_call" | custom-call | flops 1000000 | bytes 4000000 | tf_op jit(solution)/shard_map/pallas_call | solution.py:445
Async XLA Ops:
  0.6 1.0 %copy-start = (f32[2,12,32,128]{3,2,1,0:T(8,128)S(1)}, f32[2,12,32,128]{3,2,1,0:T(8,128)}, u32[]{:S(2)}) copy-start(f32[2,12,32,128]{3,2,1,0:T(8,128)} %sat_ref.5) | copy-start | bytes 1179652
  1.6 0.9 %copy-start.3 = (f32[12,32,128]{2,1,0:T(8,128)S(1)}, f32[12,32,128]{2,1,0:T(8,128)}, u32[]{:S(2)}) copy-start(f32[12,32,128]{2,1,0:T(8,128)} %press_ref.5) | copy-start | bytes 589828
  2.6 0.7 %copy-start.11 = (s32[1,1024]{1,0:T(1,128)S(1)}, s32[1,1024]{1,0:T(1,128)}, u32[]{:S(2)}) copy-start(s32[1,1024]{1,0:T(1,128)} %cell_ref.7) | copy-start | bytes 12292
  3.2 0.7 %copy-start.13 = (s32[1,1024]{1,0:T(1,128)S(1)}, s32[1,1024]{1,0:T(1,128)}, u32[]{:S(2)}) copy-start(s32[1,1024]{1,0:T(1,128)} %well_ref.7) | copy-start | bytes 12292
  3.9 0.7 %copy-start.15 = (f32[1,1024]{1,0:T(1,128)S(1)}, f32[1,1024]{1,0:T(1,128)}, u32[]{:S(2)}) copy-start(f32[1,1024]{1,0:T(1,128)} %index_ref.7) | copy-start | bytes 12292
  4.6 0.7 %copy-start.17 = (s32[32]{0:T(128)S(1)}, s32[32]{0:T(128)}, u32[]{:S(2)}) copy-start(s32[32]{0:T(128)} %param.22) | copy-start | bytes 388
  5.3 0.7 %copy-start.18 = (f32[32]{0:T(128)S(1)}, f32[32]{0:T(128)}, u32[]{:S(2)}) copy-start(f32[32]{0:T(128)} %param.23) | copy-start | bytes 388
  5.9 9.7 %copy-start.1 = (f32[2,12,32,128]{3,2,1,0:T(8,128)S(1)}, f32[2,12,32,128]{3,2,1,0:T(8,128)}, u32[]{:S(2)}) copy-start(f32[2,12,32,128]{3,2,1,0:T(8,128)} %sat_ref.5) | copy-start | bytes 1179652
  5.9 9.7 %copy-start.2 = (f32[3,12,32,128]{3,2,1,0:T(8,128)S(1)}, f32[3,12,32,128]{3,2,1,0:T(8,128)}, u32[]{:S(2)}) copy-start(f32[3,12,32,128]{3,2,1,0:T(8,128)} %perm_ref.3) | copy-start | bytes 1769476
  5.9 9.7 %copy-start.4 = (f32[12,32,128]{2,1,0:T(8,128)S(1)}, f32[12,32,128]{2,1,0:T(8,128)}, u32[]{:S(2)}) copy-start(f32[12,32,128]{2,1,0:T(8,128)} %press_ref.5) | copy-start | bytes 589828
  5.9 9.7 %copy-start.5 = (f32[12,32,128]{2,1,0:T(8,128)S(1)}, f32[12,32,128]{2,1,0:T(8,128)}, u32[]{:S(2)}) copy-start(f32[12,32,128]{2,1,0:T(8,128)} %depth_ref.3) | copy-start | bytes 589828
  7.7 20.5 %copy-start.12 = (s32[1,1024]{1,0:T(1,128)S(1)}, s32[1,1024]{1,0:T(1,128)}, u32[]{:S(2)}) copy-start(s32[1,1024]{1,0:T(1,128)} %cell_ref.7) | copy-start | bytes 12292
  7.7 20.5 %copy-start.14 = (s32[1,1024]{1,0:T(1,128)S(1)}, s32[1,1024]{1,0:T(1,128)}, u32[]{:S(2)}) copy-start(s32[1,1024]{1,0:T(1,128)} %well_ref.7) | copy-start | bytes 12292
  7.7 20.5 %copy-start.16 = (f32[1,1024]{1,0:T(1,128)S(1)}, f32[1,1024]{1,0:T(1,128)}, u32[]{:S(2)}) copy-start(f32[1,1024]{1,0:T(1,128)} %index_ref.7) | copy-start | bytes 12292
  7.7 23.8 %all-to-all-start = ((f32[32,18,1,128]{3,2,1,0:T(1,128)}), f32[32,18,1,128]{3,2,1,0:T(1,128)S(1)}, u32[]{:S(2)}, u32[]{:S(2)}) async-start(f32[32,18,1,128]{3,2,1,0:T(1,128)} %bitcast.2), calls=%async_computation | async-start | bytes 589824 | tf_op jit(solution)/shard_map/all_to_all | solution.py:458
  15.7 0.9 %copy-start.6 = (s32[12,32,128]{2,1,0:T(8,128)S(1)}, s32[12,32,128]{2,1,0:T(8,128)}, u32[]{:S(2)}) copy-start(s32[12,32,128]{2,1,0:T(8,128)} %flag_ref.3) | copy-start | bytes 589828
  16.6 11.6 %copy-start.7 = (f32[3,12,32,128]{3,2,1,0:T(8,128)S(1)}, f32[3,12,32,128]{3,2,1,0:T(8,128)}, u32[]{:S(2)}) copy-start(f32[3,12,32,128]{3,2,1,0:T(8,128)} %res_ref.1) | copy-start | bytes 1769476
  16.6 11.6 %copy-start.8 = (f32[12,32,128]{2,1,0:T(8,128)S(1)}, f32[12,32,128]{2,1,0:T(8,128)}, u32[]{:S(2)}) copy-start(f32[12,32,128]{2,1,0:T(8,128)} %pore_ref.1) | copy-start | bytes 589828
  17.1 11.1 %collective-permute-start = (f32[72,128]{1,0:T(8,128)S(1)}, f32[72,128]{1,0:T(8,128)S(1)}, u32[]{:S(2)}, u32[]{:S(2)}) collective-permute-start(f32[72,128]{1,0:T(8,128)S(1)} %get-tuple-element.18), channel_id=1, source_target_pairs={{0,4},{4,8},{8,12},{12,16},{16,20},{20,24},{24,28},{1,5},{5,9},{9,... | collective-permute-start | bytes 110600 | tf_op jit(solution)/shard_map/ppermute | solution.py:465
  20.8 7.4 %collective-permute-start.1 = (f32[72,128]{1,0:T(8,128)S(1)}, f32[72,128]{1,0:T(8,128)S(1)}, u32[]{:S(2)}, u32[]{:S(2)}) collective-permute-start(f32[72,128]{1,0:T(8,128)S(1)} %get-tuple-element.19), channel_id=1, source_target_pairs={{4,0},{8,4},{12,8},{16,12},{20,16},{24,20},{28,24},{5,1},{9,5},{13... | collective-permute-start | bytes 110600 | tf_op jit(solution)/shard_map/ppermute | solution.py:466
  22.1 3.1 %collective-permute-start.2 = (f32[8,384]{1,0:T(8,128)S(1)}, f32[8,384]{1,0:T(8,128)S(1)}, u32[]{:S(2)}, u32[]{:S(2)}) collective-permute-start(f32[8,384]{1,0:T(8,128)S(1)} %get-tuple-element.20), channel_id=1, source_target_pairs={{0,1},{1,2},{2,3},{4,5},{5,6},{6,7},{8,9},{9,10},{10,11},{12,13},{... | collective-permute-start | bytes 36872 | tf_op jit(solution)/shard_map/ppermute | solution.py:465
  23.9 4.3 %collective-permute-start.3 = (f32[8,384]{1,0:T(8,128)S(1)}, f32[8,384]{1,0:T(8,128)S(1)}, u32[]{:S(2)}, u32[]{:S(2)}) collective-permute-start(f32[8,384]{1,0:T(8,128)S(1)} %get-tuple-element.21), channel_id=1, source_target_pairs={{1,0},{2,1},{3,2},{5,4},{6,5},{7,6},{9,8},{10,9},{11,10},{13,12},{... | collective-permute-start | bytes 36872 | tf_op jit(solution)/shard_map/ppermute | solution.py:466
  30.8 0.7 %copy-start.9 = (f32[12,32,128]{2,1,0:T(8,128)}, f32[12,32,128]{2,1,0:T(8,128)S(1)}, u32[]{:S(2)}) copy-start(f32[12,32,128]{2,1,0:T(8,128)S(1)} %get-tuple-element.29.rhs_ref) | copy-start | bytes 589828
  31.5 19.2 %copy-start.10 = (f32[12,32,128]{2,1,0:T(8,128)S(1)}, f32[12,32,128]{2,1,0:T(8,128)}, u32[]{:S(2)}) copy-start(f32[12,32,128]{2,1,0:T(8,128)} %copy-done.9) | copy-start | bytes 589828
  33.7 17.1 %all-to-all-start.1 = ((f32[32,11,1,128]{3,2,1,0:T(1,128)}), f32[32,11,1,128]{3,2,1,0:T(1,128)S(1)}, u32[]{:S(2)}, u32[]{:S(2)}) async-start(f32[32,11,1,128]{3,2,1,0:T(1,128)} %bitcast.4), calls=%async_computation.1 | async-start | bytes 360448 | tf_op jit(solution)/shard_map/all_to_all | solution.py:458
  41.5 5.0 %collective-permute-start.4 = (f32[12,128]{1,0:T(8,128)S(1)}, f32[12,128]{1,0:T(8,128)S(1)}, u32[]{:S(2)}, u32[]{:S(2)}) collective-permute-start(f32[12,128]{1,0:T(8,128)S(1)} %get-tuple-element.30), channel_id=1, source_target_pairs={{0,4},{4,8},{8,12},{12,16},{16,20},{20,24},{24,28},{1,5},{5,9},{9,... | collective-permute-start | bytes 18440 | tf_op jit(solution)/shard_map/ppermute | solution.py:465
  45.2 5.5 %collective-permute-start.5 = (f32[12,128]{1,0:T(8,128)S(1)}, f32[12,128]{1,0:T(8,128)S(1)}, u32[]{:S(2)}, u32[]{:S(2)}) collective-permute-start(f32[12,128]{1,0:T(8,128)S(1)} %get-tuple-element.31), channel_id=1, source_target_pairs={{4,0},{8,4},{12,8},{16,12},{20,16},{24,20},{28,24},{5,1},{9,5},{13... | collective-permute-start | bytes 18440 | tf_op jit(solution)/shard_map/ppermute | solution.py:466

commit v2 on v1

--- a/solution.py
+++ b/solution.py
@@ -13,6 +13,7 @@
 RELAXATION = 0.8
 LANES = 128
 PLANES = 6
+FIELDS = 7
 EDGE = 8
 
 F32 = jnp.float32
@@ -114,7 +115,22 @@
     return jnp.where(well_ref[...] >= 0, index_ref[...], 0.0)
 
 
-def first_wells(press_ref, sat_ref, cell_ref, well_ref, index_ref, mode_ref, target_ref, out_ref):
+def fetch(sources, holds, sems):
+    copies = [
+        pltpu.make_async_copy(source, hold, sems.at[i])
+        for i, (source, hold) in enumerate(zip(sources, holds))
+    ]
+    for copy in copies:
+        copy.start()
+    return copies
+
+
+def first_wells(*refs):
+    count = (len(refs) - 2) // 2
+    sources, out_ref, holds, sems = refs[:count], refs[count], refs[count + 1 : -1], refs[-1]
+    for copy in fetch(sources, holds, sems):
+        copy.wait()
+    press_ref, sat_ref, cell_ref, well_ref, index_ref, mode_ref, target_ref = holds
     layers, width, lanes = press_ref.shape
     rows = layers * width
     owned = mode_ref.shape[1]
@@ -147,14 +163,36 @@
     return out_ref.shape[0] // count
 
 
-def pack(after_ref, press_ref, sat_ref, perm_ref, depth_ref, flag_ref, xup_ref, xdn_ref, yup_ref, ydn_ref):
+def is_even(axis):
+    return lax.rem(lax.axis_index(axis), 2) == 0
+
+
+def pack(
+    after_ref, press_ref, sat_ref, perm_ref, depth_ref, source_ref, xa_ref, xb_ref, ya_ref, yb_ref, flag_ref, sem
+):
     layers, width, lanes = press_ref.shape
     rows = layers * width
-    flags = flag_ref[...]
-    bit_y = lax.bitwise_and(lax.shift_right_logical(flags, 1), 1).astype(F32)
+    copy = pltpu.make_async_copy(source_ref, flag_ref, sem)
+    copy.start()
+    pick_row, pick_lane = iota((2 * EDGE, 2 * lanes), 0), lax.rem(iota((2 * EDGE, 2 * lanes), 1), lanes)
+
+    def rim(i, plane):
+        both = jnp.concatenate([part.astype(BF16) for part in halves(plane.reshape(rows, lanes))], axis=1)
+        pick = ones_of(
+            ((pick_row == i) & (pick_lane == lanes - 1)) | ((pick_row == EDGE + i) & (pick_lane == 0))
+        )
+        return nt(pick, both)
+
+    total = rim(0, press_ref[...])
+    for i, plane in enumerate([sat_ref[0], sat_ref[1], perm_ref[1], depth_ref[...]]):
+        total = total + rim(i + 1, plane)
+    copy.wait()
+    bit_y = lax.bitwise_and(lax.shift_right_logical(flag_ref[...], 1), 1).astype(F32)
+    total = total + rim(PLANES - 1, bit_y)
     last = width - 1
-    for edge, out_ref in ((last, xup_ref), (0, xdn_ref)):
-        fields = [
+    x_even, y_even = is_even("gx"), is_even("gy")
+    ends = [
+        [
             press_ref[:, edge, :],
             sat_ref[0, :, edge, :],
             sat_ref[1, :, edge, :],
@@ -162,19 +200,13 @@
             depth_ref[:, edge, :],
             lax.bitwise_and(flag_ref[:, edge, :], 1).astype(F32),
         ]
-        for i, field in enumerate(fields):
-            out_ref[i * layers : (i + 1) * layers, :] = field
-    planes = [press_ref[...], sat_ref[0], sat_ref[1], perm_ref[1], depth_ref[...], bit_y]
-    pick_row, pick_lane = iota((2 * EDGE, 2 * lanes), 0), lax.rem(iota((2 * EDGE, 2 * lanes), 1), lanes)
-    total = jnp.zeros((2 * EDGE, rows), F32)
-    for i, plane in enumerate(planes):
-        both = jnp.concatenate([part.astype(BF16) for part in halves(plane.reshape(rows, lanes))], axis=1)
-        pick = ones_of(
-            ((pick_row == i) & (pick_lane == lanes - 1)) | ((pick_row == EDGE + i) & (pick_lane == 0))
-        )
-        total = total + nt(pick, both)
-    yup_ref[...] = total[:EDGE]
-    ydn_ref[...] = total[EDGE:]
+        for edge in (last, 0)
+    ]
+    for i, (high, low) in enumerate(zip(*ends)):
+        xa_ref[i * layers : (i + 1) * layers, :] = jnp.where(x_even, high, low)
+        xb_ref[i * layers : (i + 1) * layers, :] = jnp.where(x_even, low, high)
+    ya_ref[...] = jnp.where(y_even, total[:EDGE], total[EDGE:])
+    yb_ref[...] = jnp.where(y_even, total[EDGE:], total[:EDGE])
 
 
 def upright(rows_list, lanes):
@@ -188,17 +220,25 @@
     return [transmit * jnp.where(first_up, a, b) for a, b in zip(mob, mob_next)]
 
 
-def main_terms(
-    press_ref, sat_ref, perm_ref, pore_ref, depth_ref, res_ref, flag_ref, cell_ref, well_ref, index_ref,
-    xup_ref, xdn_ref, yup_ref, ydn_ref,
-    coup_ref, rhs_ref, gain_ref, start_ref, mob_ref,
-    side_ref, share_ref,
-):
+def main_terms(*refs):
+    sources, refs, sems = refs[:FIELDS], refs[FIELDS:-1], refs[-1]
+    refs, holds = refs[:-FIELDS], refs[-FIELDS:]
+    press_ref, sat_ref, perm_ref, pore_ref, depth_ref, res_ref, flag_ref = holds
+    copies = fetch(sources, holds, sems)
+    (
+        sums_ref, cell_ref, well_ref, index_ref, xa_ref, xb_ref, ya_ref, yb_ref,
+        cur_ref, out_ref, oxa_ref, oxb_ref, known_ref, coup_ref, rhs_ref, gain_ref,
+        start_ref, mob_ref, side_ref, share_ref, xup_ref, xdn_ref,
+    ) = refs
     layers, width, lanes = press_ref.shape
     rows = layers * width
     row, lane = places(cell_ref[...], lanes)
     share_ref[...] = cell_scatter(live_index(well_ref, index_ref), row, lane, rows, lanes)
-    stand = upright([yup_ref[...], ydn_ref[...]], lanes)
+    x_even, y_even = is_even("gx"), is_even("gy")
+    xup_ref[...] = jnp.where(x_even, xb_ref[...], xa_ref[...])
+    xdn_ref[...] = jnp.where(x_even, xa_ref[...], xb_ref[...])
+    ya, yb = ya_ref[...], yb_ref[...]
+    stand = upright([jnp.where(y_even, yb, ya), jnp.where(y_even, ya, yb)], lanes)
     stand = jnp.concatenate([part.astype(BF16) for part in halves(stand)], axis=1)
     wide = (2 * lanes, PLANES * lanes)
     from_lane = lax.rem(iota(wide, 0), lanes)
@@ -210,6 +250,8 @@
             | ((from_lane == to_plane + EDGE) & (to_lane == lanes - 1))
         ),
     )
+    for copy in copies:
+        copy.wait()
     sub = iota((width, lanes), 0)
     along = iota((width, lanes), 1)
     x_first, x_last = sub == 0, sub == width - 1
@@ -323,6 +365,10 @@
         start_ref[z] = start
         mob_ref[z] = mobility
         before, this = after, following
+    first_update(
+        sums_ref, cell_ref, well_ref, index_ref, start_ref, gain_ref, mob_ref,
+        cur_ref, out_ref, oxa_ref, oxb_ref, known_ref,
+    )
 
 
 def slot_bhp(bhp, well_ref, index_ref):
@@ -332,7 +378,7 @@
 
 def first_update(
     sums_ref, cell_ref, well_ref, index_ref, start_ref, gain_ref, mob_ref,
-    cur_ref, out_ref, xup_ref, xdn_ref, known_ref,
+    cur_ref, out_ref, xa_ref, xb_ref, known_ref,
 ):
     layers, width, lanes = start_ref.shape
     rows = layers * width
@@ -364,8 +410,10 @@
     gain = gain_ref[...].reshape(rows, lanes)
     current = start + gain * push
     cur_ref[...] = current.reshape(layers, width, lanes)
-    xup_ref[...] = cur_ref[:, width - 1, :]
-    xdn_ref[...] = cur_ref[:, 0, :]
+    x_even = is_even("gx")
+    high, low = cur_ref[:, width - 1, :], cur_ref[:, 0, :]
+    xa_ref[...] = jnp.where(x_even, high, low)
+    xb_ref[...] = jnp.where(x_even, low, high)
     (at_cell,) = cell_gather([mob_ref[...].reshape(rows, lanes) * current], row, lane)
     (part,) = well_scatter([live_index(well_ref, index_ref) * at_cell], well_row, well_lane, well_rows)
     both = jnp.concatenate([half.astype(BF16) for half in halves(current)], axis=1)
@@ -389,7 +437,7 @@
 
 def last_update(
     sums_ref, known_ref, cell_ref, well_ref, index_ref, cur_ref, coup_ref, rhs_ref, gain_ref,
-    xup_ref, xdn_ref, out_ref, bhp_ref, push_ref, side_ref,
+    xa_ref, xb_ref, out_ref, bhp_ref, push_ref, side_ref, xup_ref, xdn_ref,
 ):
     layers, width, lanes = cur_ref.shape
     rows = layers * width
@@ -419,6 +467,9 @@
             )
         )
     side_ref[...] = upright(strips, lanes)
+    x_even = is_even("gx")
+    xup_ref[...] = jnp.where(x_even, xb_ref[...], xa_ref[...])
+    xdn_ref[...] = jnp.where(x_even, xa_ref[...], xb_ref[...])
     sub = iota((width, lanes), 0)
     along = iota((width, lanes), 1)
     for z in range(layers):
@@ -440,16 +491,21 @@
         out_ref[z] = total
 
 
-def call(kernel, out_shapes, args, scratch=(), flops=1_000_000):
-    shapes = [jax.ShapeDtypeStruct(s, F32) for s in out_shapes]
+def call(kernel, out_shapes, args, scratch=(), spaces=None, vmem=24):
+    shapes = [jax.ShapeDtypeStruct(shape, F32) for shape in out_shapes]
+    spaces = spaces or [pltpu.VMEM] * len(args)
+    args = [
+        pltpu.with_memory_space_constraint(arg, space) if space is pltpu.HBM else arg
+        for arg, space in zip(args, spaces)
+    ]
     return pl.pallas_call(
         kernel,
         out_shape=shapes,
-        in_specs=[pl.BlockSpec(memory_space=pltpu.VMEM)] * len(args),
+        in_specs=[pl.BlockSpec(memory_space=space) for space in spaces],
         out_specs=[pl.BlockSpec(memory_space=pltpu.VMEM)] * len(shapes),
-        scratch_shapes=[pltpu.VMEM(s, F32) for s in scratch],
-        compiler_params=pltpu.CompilerParams(vmem_limit_bytes=32 * 1024 * 1024),
-        cost_estimate=pl.CostEstimate(flops=flops, bytes_accessed=4_000_000, transcendentals=0),
+        scratch_shapes=[pltpu.VMEM(item, F32) if isinstance(item, tuple) else item for item in scratch],
+        compiler_params=pltpu.CompilerParams(vmem_limit_bytes=vmem * 1024 * 1024),
+        cost_estimate=pl.CostEstimate(flops=1_000_000, bytes_accessed=4_000_000, transcendentals=0),
     )(*args)
 
 
@@ -459,12 +515,12 @@
     return swapped.reshape(rows.shape)
 
 
-def shifted(up, down, axis):
+def swapped(first, second, axis):
     count = lax.axis_size(axis)
-    return (
-        lax.ppermute(up, axis, [(i, i + 1) for i in range(count - 1)]),
-        lax.ppermute(down, axis, [(i + 1, i) for i in range(count - 1)]),
-    )
+    pairs = [(i, i ^ 1) for i in range(count) if i ^ 1 < count]
+    others = [(i, i + 1 if i % 2 else i - 1) for i in range(count)]
+    others = [(i, j) for i, j in others if 0 <= j < count]
+    return lax.ppermute(first, axis, pairs), lax.ppermute(second, axis, others)
 
 
 def body(
@@ -477,42 +533,46 @@
     owned = well_mode.shape[0]
     well_rows = owned * count // LANES
     chunk = 2 * well_rows + 2
+    operands = [pressure, saturation, perf_cell, perf_well, perf_index, well_mode[None], well_target[None]]
     (sums,) = call(
         first_wells,
         [(count * chunk, LANES)],
-        [pressure, saturation, perf_cell, perf_well, perf_index, well_mode[None], well_target[None]],
+        operands,
+        [pltpu.VMEM(a.shape, a.dtype) for a in operands] + [pltpu.SemaphoreType.DMA((len(operands),))],
+        [pltpu.HBM] * len(operands),
     )
     gathered = everyone(sums, count)
-    xup, xdn, yup, ydn = call(
+    xa, xb, ya, yb = call(
         pack,
         [(PLANES * layers, lanes)] * 2 + [(EDGE, rows)] * 2,
-        [sums[:8], pressure, saturation, permeability, cell_depth, upstream_flags],
-    )
-    xup, xdn = shifted(xup, xdn, "gx")
-    yup, ydn = shifted(yup, ydn, "gy")
+        [sums, pressure, saturation, permeability, cell_depth, upstream_flags],
+        [pltpu.VMEM(upstream_flags.shape, upstream_flags.dtype), pltpu.SemaphoreType.DMA],
+        [pl.ANY] + [pltpu.VMEM] * 4 + [pltpu.HBM],
+    )
+    xa, xb = swapped(xa, xb, "gx")
+    ya, yb = swapped(ya, yb, "gy")
     grid = (layers, width, lanes)
-    coup, rhs, gain, start, mobility = call(
+    pieces = rows // LANES
+    fields = [pressure, saturation, permeability, pore_volume, cell_depth, residual, upstream_flags]
+    current, sums, xa, xb, known, coup, rhs, gain = call(
         main_terms,
-        [(6,) + grid, grid, grid, grid, grid],
         [
-            pressure, saturation, permeability, pore_volume, cell_depth, residual, upstream_flags,
-            perf_cell, perf_well, perf_index, xup, xdn, yup, ydn,
+            grid, (count * (well_rows + pieces), LANES), (layers, lanes), (layers, lanes), (3, well_rows, LANES),
+            (6,) + grid, grid, grid,
         ],
-        [(rows, PLANES * lanes), (rows, lanes)],
-    )
-    pieces = rows // LANES
-    current, sums, xup, xdn, known = call(
-        first_update,
-        [grid, (count * (well_rows + pieces), LANES), (layers, lanes), (layers, lanes), (3, well_rows, LANES)],
-        [gathered, perf_cell, perf_well, perf_index, start, gain, mobility],
+        fields + [gathered, perf_cell, perf_well, perf_index, xa, xb, ya, yb],
+        [grid, grid, (rows, PLANES * lanes), (rows, lanes), (PLANES * layers, lanes), (PLANES * layers, lanes)]
+        + [pltpu.VMEM(a.shape, a.dtype) for a in fields]
+        + [pltpu.SemaphoreType.DMA((FIELDS,))],
+        [pltpu.HBM] * FIELDS + [pltpu.VMEM] * 8,
     )
     gathered = everyone(sums, count)
-    xup, xdn = shifted(xup, xdn, "gx")
+    xa, xb = swapped(xa, xb, "gx")
     out, bhp = call(
         last_update,
         [grid, (1, owned)],
-        [gathered, known, perf_cell, perf_well, perf_index, current, coup, rhs, gain, xup, xdn],
-        [(rows, lanes), (rows, lanes)],
+        [gathered, known, perf_cell, perf_well, perf_index, current, coup, rhs, gain, xa, xb],
+        [(rows, lanes), (rows, lanes), (layers, lanes), (layers, lanes)],
     )
     return out, bhp[0]
 

time: 52.8 us -> 43.3 us (0.82)
  starting transfers between devices: 28.1 us -> 17.8 us
  local copies, waits for them, and re-layouts: 7.59 us -> 0.04 us
  waiting for transfers between devices: 7.27 us -> 13.2 us
  Pallas kernels: 8.39 us -> 11.1 us
    all_to_all x2, waiting for transfers between devices: 0.01 us -> 10.6 us  [everyone(): lax.all_to_all(rows.reshape(count, height, 1, LANES), AXES, 0, 0, tiled=T...]
    ppermute x6, starting transfers between devices: 13 us -> 5.7 us  [the longest x3 3.74 us: swapped(): lax.ppermute(first, axis, pairs)]
    unnamed x38 -> x14, local copies, waits for them, and re-layouts: 6.91 us -> 0.04 us
    ppermute x6, waiting for transfers between devices: 7.26 us -> 2.64 us  [the longest x3 2.63 us: swapped(): lax.ppermute(first, axis, pairs)]
    all_to_all x2, starting transfers between devices: 15.1 us -> 12 us  [everyone(): lax.all_to_all(rows.reshape(count, height, 1, LANES), AXES, 0, 0, tiled=T...]
    pallas_call x5 -> x4, Pallas kernels: 8.39 us -> 11.1 us  [call(): pl.pallas_call(kernel, out_shape=shapes, in_specs=[pl.BlockSpec(memory_sp...]
    slice x1 -> x0, local copies, waits for them, and re-layouts: 0.68 us -> none  [body(): sums[:8]]
  transfers between devices with their start and end apart: 8 -> 8, of which waited for: 2 -> 5; matrix products, arithmetic and copies ran while one was open for 1% -> 0% of each run, Pallas kernels for 6% -> 3%
where the time goes in v2:
time: 43.3 us; the launch traced here: 42.9 us
  starting transfers between devices  17.8 us (41%)
  waiting for transfers between devices  13.2 us (30%)
  Pallas kernels  11.1 us (26%)
  between operations  0.8 us (2%)
    all_to_all x2, starting transfers between devices, everyone(): lax.all_to_all(rows.reshape(count, height, 1, LANES), AXES, 0, 0, tiled=T...  12 us
    pallas_call x4, Pallas kernels, call(): pl.pallas_call(kernel, out_shape=shapes, in_specs=[pl.BlockSpec(memory_sp...  11.1 us
    all_to_all x2, waiting for transfers between devices, everyone(): lax.all_to_all(rows.reshape(count, height, 1, LANES), AXES, 0, 0, tiled=T...  10.6 us
    ppermute x3, starting transfers between devices, swapped(): lax.ppermute(first, axis, pairs)  3.74 us
    ppermute x3, waiting for transfers between devices, swapped(): lax.ppermute(first, axis, pairs)  2.63 us
    ppermute x3, starting transfers between devices, swapped(): lax.ppermute(second, axis, others)  1.96 us
  transfers between devices with their start and end apart: 8, of which 5 were waited for; matrix products, arithmetic and copies ran while one was open for 0% of the time, Pallas kernels for 3%

profile of v2, /device:TPU:0, one launch (start us, length us, event | category | flops | bytes accessed | tf_op | source)
XLA Modules:
  0.0 42.9 jit_solution(17140325149636420856)
XLA Ops:
  0.6 0.0 copy-start
  0.6 0.0 copy-start.2
  0.7 0.0 copy-start.3
  0.7 0.0 copy-start.1
  0.7 3.0 %shard_map.131.after_ref = f32[576,128]{1,0:T(8,128)} custom-call(f32[12,32,128]{2,1,0:T(8,128)} %refs_0_.3, f32[2,12,32,128]{3,2,1,0:T(8,128)} %refs_1_.3, s32[1,1024]{1,0:T(1,128)} %cell_ref.1, s32[1,1024]{1,0:T(1,128)} %well_ref.1, f32[1,1024]{1,0:T(1,128)} %index_ref.1, s32[1,32]{1,0:T(1,128)} %bitcast.9, f32[1,32]{1,0:T(1,128)} %bitcast.10), custom_call_target="tpu_custom_call" | custom-call | flops 1000000 | bytes 4000000 | tf_op jit(solution)/shard_map/pallas_call | solution.py:501
  3.7 0.0 copy-start.4
  3.7 0.0 copy-start.5
  3.7 0.0 copy-start.6
  3.7 7.3 %all-to-all-start = ((f32[32,18,1,128]{3,2,1,0:T(1,128)}), f32[32,18,1,128]{3,2,1,0:T(1,128)S(1)}, u32[]{:S(2)}, u32[]{:S(2)}) async-start(f32[32,18,1,128]{3,2,1,0:T(1,128)} %bitcast.2), calls=%async_computation | async-start | bytes 589824 | tf_op jit(solution)/shard_map/all_to_all | solution.py:514
  11.0 0.0 copy-done
  11.0 0.0 copy-done.2
  11.1 0.0 copy-done.3
  11.1 0.0 copy-done.1
  11.1 1.1 %shard_map.132 = (f32[72,128]{1,0:T(8,128)S(1)}, f32[72,128]{1,0:T(8,128)S(1)}, f32[8,384]{1,0:T(8,128)S(1)}, f32[8,384]{1,0:T(8,128)S(1)}) custom-call(f32[576,128]{1,0:T(8,128)} %shard_map.131.after_ref, f32[12,32,128]{2,1,0:T(8,128)S(1)} %copy-done.2, f32[2,12,32,128]{3,2,1,0:T(8,128)S(1)} %copy-done, f32[3,12,32,128]{3,2,1,0:T(8,128)S(1)} %copy-done.1, ...), custom_call_target="tpu_custom_call" | custom-call | flops 1000000 | bytes 4000000 | tf_op jit(solution)/shard_map/pallas_call | solution.py:501
  12.2 1.8 %collective-permute-start = (f32[72,128]{1,0:T(8,128)S(1)}, f32[72,128]{1,0:T(8,128)S(1)}, u32[]{:S(2)}, u32[]{:S(2)}) collective-permute-start(f32[72,128]{1,0:T(8,128)S(1)} %get-tuple-element.16), channel_id=1, source_target_pairs={{0,4},{4,0},{8,12},{12,8},{16,20},{20,16},{24,28},{28,24},{1,5},{5... | collective-permute-start | bytes 110600 | tf_op jit(solution)/shard_map/ppermute | solution.py:523
  14.1 0.7 %collective-permute-start.1 = (f32[72,128]{1,0:T(8,128)S(1)}, f32[72,128]{1,0:T(8,128)S(1)}, u32[]{:S(2)}, u32[]{:S(2)}) collective-permute-start(f32[72,128]{1,0:T(8,128)S(1)} %get-tuple-element.17), channel_id=1, source_target_pairs={{4,8},{8,4},{12,16},{16,12},{20,24},{24,20},{5,9},{9,5},{13,17},{1... | collective-permute-start | bytes 110600 | tf_op jit(solution)/shard_map/ppermute | solution.py:523
  14.7 0.1 collective-permute-start.2
  14.8 0.7 %collective-permute-start.3 = (f32[8,384]{1,0:T(8,128)S(1)}, f32[8,384]{1,0:T(8,128)S(1)}, u32[]{:S(2)}, u32[]{:S(2)}) collective-permute-start(f32[8,384]{1,0:T(8,128)S(1)} %get-tuple-element.19), channel_id=1, source_target_pairs={{1,2},{2,1},{5,6},{6,5},{9,10},{10,9},{13,14},{14,13},{17,18},{18,... | collective-permute-start | bytes 36872 | tf_op jit(solution)/shard_map/ppermute | solution.py:523
  15.5 0.5 %collective-permute-done.2.refs_13_ = f32[8,384]{1,0:T(8,128)S(1)} collective-permute-done((f32[8,384]{1,0:T(8,128)S(1)}, f32[8,384]{1,0:T(8,128)S(1)}, u32[]{:S(2)}, u32[]{:S(2)}) %collective-permute-start.2) | collective-permute-done | bytes 12320 | tf_op jit(solution)/shard_map/ppermute | solution.py:523
  16.0 0.0 collective-permute-done.3.refs_14_
  16.0 0.9 %collective-permute-done.refs_11_ = f32[72,128]{1,0:T(8,128)S(1)} collective-permute-done((f32[72,128]{1,0:T(8,128)S(1)}, f32[72,128]{1,0:T(8,128)S(1)}, u32[]{:S(2)}, u32[]{:S(2)}) %collective-permute-start) | collective-permute-done | bytes 36896 | tf_op jit(solution)/shard_map/ppermute | solution.py:523
  16.9 0.0 collective-permute-done.1.refs_12_
  16.9 5.6 %all-to-all-done = f32[32,18,1,128]{3,2,1,0:T(1,128)S(1)} async-done(((f32[32,18,1,128]{3,2,1,0:T(1,128)}), f32[32,18,1,128]{3,2,1,0:T(1,128)S(1)}, u32[]{:S(2)}, u32[]{:S(2)}) %all-to-all-start) | async-done | bytes 294944 | tf_op jit(solution)/shard_map/all_to_all | solution.py:514
  22.4 0.0 copy-done.4
  22.4 0.0 copy-done.5
  22.4 0.0 copy-done.6
  22.4 5.6 %shard_map.133 = (f32[12,32,128]{2,1,0:T(8,128)S(1)}, f32[352,128]{1,0:T(8,128)}, f32[12,128]{1,0:T(8,128)S(1)}, f32[12,128]{1,0:T(8,128)S(1)}, f32[3,8,128]{2,1...) custom-call(f32[12,32,128]{2,1,0:T(8,128)} %refs_0_.3, ...), custom_call_target="tpu_custom_call" | custom-call | flops 1000000 | bytes 4000000 | tf_op jit(solution)/shard_map/pallas_call | solution.py:501
  28.0 4.8 %all-to-all-start.1 = ((f32[32,11,1,128]{3,2,1,0:T(1,128)}), f32[32,11,1,128]{3,2,1,0:T(1,128)S(1)}, u32[]{:S(2)}, u32[]{:S(2)}) async-start(f32[32,11,1,128]{3,2,1,0:T(1,128)} %bitcast.4), calls=%async_computation.1 | async-start | bytes 360448 | tf_op jit(solution)/shard_map/all_to_all | solution.py:514
  32.8 1.8 %collective-permute-start.4 = (f32[12,128]{1,0:T(8,128)S(1)}, f32[12,128]{1,0:T(8,128)S(1)}, u32[]{:S(2)}, u32[]{:S(2)}) collective-permute-start(f32[12,128]{1,0:T(8,128)S(1)} %get-tuple-element.26), channel_id=1, source_target_pairs={{0,4},{4,0},{8,12},{12,8},{16,20},{20,16},{24,28},{28,24},{1,5},{5... | collective-permute-start | bytes 18440 | tf_op jit(solution)/shard_map/ppermute | solution.py:523
  34.6 0.6 %collective-permute-start.5 = (f32[12,128]{1,0:T(8,128)S(1)}, f32[12,128]{1,0:T(8,128)S(1)}, u32[]{:S(2)}, u32[]{:S(2)}) collective-permute-start(f32[12,128]{1,0:T(8,128)S(1)} %get-tuple-element.27), channel_id=1, source_target_pairs={{4,8},{8,4},{12,16},{16,12},{20,24},{24,20},{5,9},{9,5},{13,17},{1... | collective-permute-start | bytes 18440 | tf_op jit(solution)/shard_map/ppermute | solution.py:523
  35.3 1.2 %collective-permute-done.4.xa_ref = f32[12,128]{1,0:T(8,128)S(1)} collective-permute-done((f32[12,128]{1,0:T(8,128)S(1)}, f32[12,128]{1,0:T(8,128)S(1)}, u32[]{:S(2)}, u32[]{:S(2)}) %collective-permute-start.4) | collective-permute-done | bytes 6176 | tf_op jit(solution)/shard_map/ppermute | solution.py:523
  36.5 0.0 collective-permute-done.5.xb_ref
  36.5 5.0 %all-to-all-done.1 = f32[32,11,1,128]{3,2,1,0:T(1,128)S(1)} async-done(((f32[32,11,1,128]{3,2,1,0:T(1,128)}), f32[32,11,1,128]{3,2,1,0:T(1,128)S(1)}, u32[]{:S(2)}, u32[]{:S(2)}) %all-to-all-start.1) | async-done | bytes 180256 | tf_op jit(solution)/shard_map/all_to_all | solution.py:514
  41.5 1.4 %shard_map.134 = (f32[12,32,128]{2,1,0:T(8,128)}, f32[1,32]{1,0:T(1,128)}) custom-call(f32[352,128]{1,0:T(8,128)S(1)} %bitcast.8, f32[3,8,128]{2,1,0:T(8,128)S(1)} %get-tuple-element.21.known_ref, s32[1,1024]{1,0:T(1,128)S(1)} %copy-done.4, s32[1,1024]{1,0:T(1,128)S(1)} %copy-done.5, f32[1,1024]{1,0:T(1,128)S(1)} %copy-done.6, ...), custom_call_target="tpu_custom_call" | custom-call | flops 1000000 | bytes 4000000 | tf_op jit(solution)/shard_map/pallas_call | solution.py:501
Async XLA Ops:
  0.6 10.4 %copy-start = (f32[2,12,32,128]{3,2,1,0:T(8,128)S(1)}, f32[2,12,32,128]{3,2,1,0:T(8,128)}, u32[]{:S(2)}) copy-start(f32[2,12,32,128]{3,2,1,0:T(8,128)} %refs_1_.3) | copy-start | bytes 1179652
  0.6 10.4 %copy-start.2 = (f32[12,32,128]{2,1,0:T(8,128)S(1)}, f32[12,32,128]{2,1,0:T(8,128)}, u32[]{:S(2)}) copy-start(f32[12,32,128]{2,1,0:T(8,128)} %refs_0_.3) | copy-start | bytes 589828
  0.7 10.4 %copy-start.3 = (f32[12,32,128]{2,1,0:T(8,128)S(1)}, f32[12,32,128]{2,1,0:T(8,128)}, u32[]{:S(2)}) copy-start(f32[12,32,128]{2,1,0:T(8,128)} %refs_4_.3) | copy-start | bytes 589828
  0.7 10.4 %copy-start.1 = (f32[3,12,32,128]{3,2,1,0:T(8,128)S(1)}, f32[3,12,32,128]{3,2,1,0:T(8,128)}, u32[]{:S(2)}) copy-start(f32[3,12,32,128]{3,2,1,0:T(8,128)} %refs_2_.3) | copy-start | bytes 1769476
  3.7 18.7 %copy-start.4 = (s32[1,1024]{1,0:T(1,128)S(1)}, s32[1,1024]{1,0:T(1,128)}, u32[]{:S(2)}) copy-start(s32[1,1024]{1,0:T(1,128)} %cell_ref.1) | copy-start | bytes 12292
  3.7 18.7 %copy-start.5 = (s32[1,1024]{1,0:T(1,128)S(1)}, s32[1,1024]{1,0:T(1,128)}, u32[]{:S(2)}) copy-start(s32[1,1024]{1,0:T(1,128)} %well_ref.1) | copy-start | bytes 12292
  3.7 18.7 %copy-start.6 = (f32[1,1024]{1,0:T(1,128)S(1)}, f32[1,1024]{1,0:T(1,128)}, u32[]{:S(2)}) copy-start(f32[1,1024]{1,0:T(1,128)} %index_ref.1) | copy-start | bytes 12292
  3.7 18.7 %all-to-all-start = ((f32[32,18,1,128]{3,2,1,0:T(1,128)}), f32[32,18,1,128]{3,2,1,0:T(1,128)S(1)}, u32[]{:S(2)}, u32[]{:S(2)}) async-start(f32[32,18,1,128]{3,2,1,0:T(1,128)} %bitcast.2), calls=%async_computation | async-start | bytes 589824 | tf_op jit(solution)/shard_map/all_to_all | solution.py:514
  12.2 4.7 %collective-permute-start = (f32[72,128]{1,0:T(8,128)S(1)}, f32[72,128]{1,0:T(8,128)S(1)}, u32[]{:S(2)}, u32[]{:S(2)}) collective-permute-start(f32[72,128]{1,0:T(8,128)S(1)} %get-tuple-element.16), channel_id=1, source_target_pairs={{0,4},{4,0},{8,12},{12,8},{16,20},{20,16},{24,28},{28,24},{1,5},{5... | collective-permute-start | bytes 110600 | tf_op jit(solution)/shard_map/ppermute | solution.py:523
  14.1 2.8 %collective-permute-start.1 = (f32[72,128]{1,0:T(8,128)S(1)}, f32[72,128]{1,0:T(8,128)S(1)}, u32[]{:S(2)}, u32[]{:S(2)}) collective-permute-start(f32[72,128]{1,0:T(8,128)S(1)} %get-tuple-element.17), channel_id=1, source_target_pairs={{4,8},{8,4},{12,16},{16,12},{20,24},{24,20},{5,9},{9,5},{13,17},{1... | collective-permute-start | bytes 110600 | tf_op jit(solution)/shard_map/ppermute | solution.py:523
  14.7 1.2 %collective-permute-start.2 = (f32[8,384]{1,0:T(8,128)S(1)}, f32[8,384]{1,0:T(8,128)S(1)}, u32[]{:S(2)}, u32[]{:S(2)}) collective-permute-start(f32[8,384]{1,0:T(8,128)S(1)} %get-tuple-element.18), channel_id=1, source_target_pairs={{0,1},{1,0},{2,3},{3,2},{4,5},{5,4},{6,7},{7,6},{8,9},{9,8},{10,11... | collective-permute-start | bytes 36872 | tf_op jit(solution)/shard_map/ppermute | solution.py:523
  14.8 1.2 %collective-permute-start.3 = (f32[8,384]{1,0:T(8,128)S(1)}, f32[8,384]{1,0:T(8,128)S(1)}, u32[]{:S(2)}, u32[]{:S(2)}) collective-permute-start(f32[8,384]{1,0:T(8,128)S(1)} %get-tuple-element.19), channel_id=1, source_target_pairs={{1,2},{2,1},{5,6},{6,5},{9,10},{10,9},{13,14},{14,13},{17,18},{18,... | collective-permute-start | bytes 36872 | tf_op jit(solution)/shard_map/ppermute | solution.py:523
  28.0 13.5 %all-to-all-start.1 = ((f32[32,11,1,128]{3,2,1,0:T(1,128)}), f32[32,11,1,128]{3,2,1,0:T(1,128)S(1)}, u32[]{:S(2)}, u32[]{:S(2)}) async-start(f32[32,11,1,128]{3,2,1,0:T(1,128)} %bitcast.4), calls=%async_computation.1 | async-start | bytes 360448 | tf_op jit(solution)/shard_map/all_to_all | solution.py:514
  32.8 3.7 %collective-permute-start.4 = (f32[12,128]{1,0:T(8,128)S(1)}, f32[12,128]{1,0:T(8,128)S(1)}, u32[]{:S(2)}, u32[]{:S(2)}) collective-permute-start(f32[12,128]{1,0:T(8,128)S(1)} %get-tuple-element.26), channel_id=1, source_target_pairs={{0,4},{4,0},{8,12},{12,8},{16,20},{20,16},{24,28},{28,24},{1,5},{5... | collective-permute-start | bytes 18440 | tf_op jit(solution)/shard_map/ppermute | solution.py:523
  34.6 1.9 %collective-permute-start.5 = (f32[12,128]{1,0:T(8,128)S(1)}, f32[12,128]{1,0:T(8,128)S(1)}, u32[]{:S(2)}, u32[]{:S(2)}) collective-permute-start(f32[12,128]{1,0:T(8,128)S(1)} %get-tuple-element.27), channel_id=1, source_target_pairs={{4,8},{8,4},{12,16},{16,12},{20,24},{24,20},{5,9},{9,5},{13,17},{1... | collective-permute-start | bytes 18440 | tf_op jit(solution)/shard_map/ppermute | solution.py:523

commit v3 on v2

v3 whole, which is shorter than its diff:
```python
import jax
import jax.numpy as jnp
from jax import lax
from jax.experimental import pallas as pl
from jax.experimental.pallas import tpu as pltpu
from jax.sharding import PartitionSpec as P

COMP_OIL = 0.2
COMP_WATER = 0.05
GRAV_OIL = 0.4
GRAV_WATER = 0.5
GRAV_GAS = 0.08
RELAXATION = 0.8
LANES = 128
PLANES = 6
INPUTS = 12
PRESS, SAT, PERM, DEPTH, PORE, RES, GRIDS = 0, 1, 3, 6, 7, 8, 11
DIAG, RHS, COUP, MOB, AROUND = 1, 2, 3, 9, 10
CURRENT, SCALE, GAIN = 0, 1, 10
EDGE = 8

F32 = jnp.float32
BF16 = jnp.bfloat16
AXES = ("gx", "gy")


def nn(a, b):
    return lax.dot_general(a, b, (((1,), (0,)), ((), ())), preferred_element_type=F32)


def nt(a, b):
    return lax.dot_general(a, b, (((1,), (1,)), ((), ())), preferred_element_type=F32)


def halves(x):
    high = x.astype(BF16).astype(F32)
    return high, x - high


def iota(shape, dim):
    return lax.broadcasted_iota(jnp.int32, shape, dim)


def hot(index, count):
    return iota((count, index.shape[1]), 0) == index


def ones_of(mask):
    return jnp.where(mask, 1.0, 0.0).astype(BF16)


def bits_of(n):
    assert n & (n - 1) == 0
    return n.bit_length() - 1


def places(index, width):
    return lax.shift_right_arithmetic(index, bits_of(width)), lax.bitwise_and(index, width - 1)


def cell_pick(row, lane, rows, lanes):
    pick = ones_of(hot(lane, lanes))
    return jnp.concatenate([pick, pick], axis=0), hot(row, rows)


def cell_find(field, pick, at_row):
    both = jnp.concatenate([part.astype(BF16) for part in halves(field)], axis=1)
    return jnp.sum(jnp.where(at_row, nn(both, pick), 0.0), axis=0, keepdims=True)


def cell_scatter(value, row, lane, rows, lanes):
    spread = jnp.where(hot(lane, lanes), value, 0.0)
    spread = jnp.concatenate([part.astype(BF16) for part in halves(spread)], axis=0)
    total = nt(ones_of(hot(row, rows)), spread)
    return total[:, :lanes] + total[:, lanes:]


def well_scatter(values, row, lane, rows):
    mine = hot(row, rows)
    stack = []
    for value in values:
        stack.extend(halves(jnp.where(mine, value, 0.0)))
    total = nt(jnp.concatenate(stack, axis=0).astype(BF16), ones_of(hot(lane, LANES)))
    return [
        total[2 * i * rows : (2 * i + 1) * rows] + total[(2 * i + 1) * rows : (2 * i + 2) * rows]
        for i in range(len(values))
    ]


def well_gather(field, row, lane):
    rows = field.shape[0]
    both = jnp.concatenate(halves(field), axis=0).astype(BF16)
    found = nn(both, ones_of(hot(lane, LANES)))
    return jnp.sum(
        jnp.where(hot(row, rows), found[:rows] + found[rows:], 0.0), axis=0, keepdims=True
    )


def total_mobility(sat_water, sat_gas):
    sat_oil = 1.0 - sat_water - sat_gas
    return 0.5 * sat_oil * sat_oil + sat_water * sat_water + 5.0 * (sat_gas * sat_gas)


def phase_mobility(pressure, sat_water, sat_gas):
    sat_oil = 1.0 - sat_water - sat_gas
    b_oil = 1.0 + COMP_OIL * (pressure - 1.0)
    b_water = 1.0 + COMP_WATER * (pressure - 1.0)
    return (
        sat_oil * sat_oil * b_oil * 0.5,
        sat_water * sat_water * b_water,
        sat_gas * sat_gas * pressure * 5.0,
    )


def live_index(well_ref, index_ref):
    return jnp.where(well_ref[...] >= 0, index_ref[...], 0.0)


def fetch(sources, holds, sems):
    copies = [
        pltpu.make_async_copy(source, hold, sems.at[i])
        for i, (source, hold) in enumerate(zip(sources, holds))
    ]
    for copy in copies:
        copy.start()
    return copies


def repeat_out(block_ref, out_ref, sem):
    height = block_ref.shape[0]
    copies = [
        pltpu.make_async_copy(block_ref, out_ref.at[pl.ds(i * height, height)], sem.at[i])
        for i in range(out_ref.shape[0] // height)
    ]
    for copy in copies:
        copy.start()
    return copies


def first_rows(out_ref):
    count = lax.axis_size("gx") * lax.axis_size("gy")
    return out_ref.shape[0] // count


def is_even(axis):
    return lax.rem(lax.axis_index(axis), 2) == 0


def opening(*refs):
    inputs, sems, out_sems = refs[:INPUTS], refs[-2], refs[-1]
    sums_ref, yb_ref, xb_ref, xa_ref, ya_ref, grid_ref, flag_ref = refs[INPUTS : INPUTS + 7]
    cell_ref, well_ref, index_ref, mode_ref, target_ref, block_ref = refs[INPUTS + 7 : -2]
    slot_refs = [cell_ref, well_ref, index_ref, mode_ref, target_ref]
    sat_ref, perm_ref = grid_ref.at[SAT : SAT + 2], grid_ref.at[PERM : PERM + 3]
    holds = slot_refs + [
        sat_ref, grid_ref.at[PRESS], perm_ref, grid_ref.at[DEPTH], flag_ref,
        grid_ref.at[PORE], grid_ref.at[RES : RES + 3],
    ]
    copies = fetch(inputs, holds, sems)
    layers, width, lanes = flag_ref.shape
    rows = layers * width
    owned = mode_ref.shape[1]
    group = LANES // owned
    me = lax.axis_index(AXES)
    for copy in copies[: len(slot_refs)]:
        copy.wait()
    row, lane = places(cell_ref[...], lanes)
    well_row, well_lane = places(well_ref[...], LANES)
    pick, at_row = cell_pick(row, lane, rows, lanes)
    index = live_index(well_ref, index_ref)
    chunk_rows = first_rows(sums_ref)
    here = lax.shift_right_logical(iota((1, LANES), 1), bits_of(owned)) == lax.rem(me, group)
    controls = [
        jnp.where(here, jnp.concatenate([ref[...].astype(F32)] * group, axis=1), 0.0)
        for ref in (mode_ref, target_ref)
    ]
    later = copies[len(slot_refs) :]
    later[0].wait()
    mobility = total_mobility(grid_ref[SAT].reshape(rows, lanes), grid_ref[SAT + 1].reshape(rows, lanes))
    at_mob = cell_find(mobility, pick, at_row)
    later[1].wait()
    at_press = cell_find(mobility * grid_ref[PRESS].reshape(rows, lanes), pick, at_row)
    sums = well_scatter([index * at_press, index * at_mob], well_row, well_lane, (chunk_rows - 2) // 2)
    block = jnp.concatenate(sums + controls, axis=0)
    block_ref[...] = jnp.concatenate([block] * (block_ref.shape[0] // chunk_rows), axis=0)
    outgoing = repeat_out(block_ref, sums_ref, out_sems)
    pick_row, pick_lane = iota((2 * EDGE, 2 * lanes), 0), lax.rem(iota((2 * EDGE, 2 * lanes), 1), lanes)

    def rim(i, plane):
        both = jnp.concatenate([part.astype(BF16) for part in halves(plane.reshape(rows, lanes))], axis=1)
        pick = ones_of(
            ((pick_row == i) & (pick_lane == lanes - 1)) | ((pick_row == EDGE + i) & (pick_lane == 0))
        )
        return nt(pick, both)

    total = rim(0, grid_ref[PRESS]) + rim(1, grid_ref[SAT]) + rim(2, grid_ref[SAT + 1])
    later[2].wait()
    total = total + rim(3, grid_ref[PERM + 1])
    later[3].wait()
    total = total + rim(4, grid_ref[DEPTH])
    later[4].wait()
    bit_y = lax.bitwise_and(lax.shift_right_logical(flag_ref[...], 1), 1).astype(F32)
    total = total + rim(PLANES - 1, bit_y)
    x_even, y_even = is_even("gx"), is_even("gy")
    last = width - 1
    ends = [
        [
            grid_ref[PRESS, :, edge, :],
            grid_ref[SAT, :, edge, :],
            grid_ref[SAT + 1, :, edge, :],
            grid_ref[PERM, :, edge, :],
            grid_ref[DEPTH, :, edge, :],
            lax.bitwise_and(flag_ref[:, edge, :], 1).astype(F32),
        ]
        for edge in (last, 0)
    ]
    for i, (high, low) in enumerate(zip(*ends)):
        xa_ref[i * layers : (i + 1) * layers, :] = jnp.where(x_even, high, low)
        xb_ref[i * layers : (i + 1) * layers, :] = jnp.where(x_even, low, high)
    ya_ref[...] = jnp.where(y_even, total[:EDGE], total[EDGE:])
    yb_ref[...] = jnp.where(y_even, total[EDGE:], total[:EDGE])
    for copy in later[5:] + outgoing:
        copy.wait()


def upright(rows_list, lanes):
    stack = jnp.concatenate(rows_list, axis=0)
    stack = jnp.concatenate([stack, jnp.zeros((lanes - stack.shape[0], stack.shape[1]), F32)], axis=0)
    return jnp.transpose(stack)


def inverse(x):
    guess = pl.reciprocal(x, approx=True)
    return guess * (2.0 - x * guess)


def phase_weights(pressure):
    b_oil = 1.0 + COMP_OIL * (pressure - 1.0)
    b_water = 1.0 + COMP_WATER * (pressure - 1.0)
    whole = inverse(b_oil * b_water * pressure)
    other = pressure * whole
    return b_water * other, b_oil * other, b_oil * b_water * whole


def faces(perm, perm_next, mob, mob_next, first_up):
    transmit = 2.0 * perm * perm_next * inverse(perm + perm_next)
    return [transmit * jnp.where(first_up, a, b) for a, b in zip(mob, mob_next)]


def weighted(weights, flux):
    oil, water, gas = (w * f for w, f in zip(weights, flux))
    return oil + water + gas, GRAV_OIL * oil + GRAV_WATER * water + GRAV_GAS * gas


def outer_face(own, other, own_up):
    mob, mob_other = phase_mobility(*own[:3]), phase_mobility(*other[:3])
    coupling, lift = weighted(phase_weights(own[0]), faces(own[3], other[3], mob, mob_other, own_up))
    return coupling, lift * (own[4] - other[4]), coupling * other[0]


def main_terms(given_ref, after_ref, flag_ref, cell_ref, well_ref, index_ref, grid_ref, share_ref):
    layers, width, lanes = flag_ref.shape
    rows = layers * width
    row, lane = places(cell_ref[...], lanes)
    share_ref[...] = cell_scatter(live_index(well_ref, index_ref), row, lane, rows, lanes)
    x_last = iota((width, lanes), 0) == width - 1
    y_last = iota((width, lanes), 1) == lanes - 1

    def layer(z):
        press = grid_ref[PRESS, z]
        return press, phase_mobility(press, grid_ref[SAT, z], grid_ref[SAT + 1, z])

    this = layer(0)
    before = None
    for z in range(layers):
        press, mob = this
        following = layer(z + 1) if z + 1 < layers else None
        sat_water, sat_gas = grid_ref[SAT, z], grid_ref[SAT + 1, z]
        sat_oil = 1.0 - sat_water - sat_gas
        depth = grid_ref[DEPTH, z]
        flags = flag_ref[z]
        weights = phase_weights(press)
        storage = grid_ref[PORE, z] * (
            sat_oil * COMP_OIL * weights[0] + sat_water * COMP_WATER * weights[1] + sat_gas * weights[2]
        )
        mobility = total_mobility(sat_water, sat_gas)
        diag = storage + mobility * share_ref[z * width : (z + 1) * width, :]
        rhs = storage * press
        for i, weight in enumerate(weights):
            rhs = rhs - weight * grid_ref[RES + i, z]
        around = jnp.zeros_like(press)
        couplings = {}

        def add(name, flux, drop, beside):
            nonlocal diag, rhs, around
            coupling, lift = weighted(weights, flux)
            couplings[name] = coupling
            diag = diag + coupling
            rhs = rhs + lift * drop
            around = around + coupling * beside

        for dim, size, end, bit in ((0, width, x_last, 1), (1, lanes, y_last, 2)):
            perm = grid_ref[PERM + dim, z]
            perm_next = jnp.where(end, 0.0, pltpu.roll(perm, size - 1, dim))
            up = lax.bitwise_and(flags, bit) > 0
            flux = faces(perm, perm_next, mob, [pltpu.roll(a, size - 1, dim) for a in mob], up)
            drop = depth - pltpu.roll(depth, size - 1, dim)
            add(2 * dim, flux, drop, pltpu.roll(press, size - 1, dim))
            add(2 * dim + 1, [pltpu.roll(a, 1, dim) for a in flux], -pltpu.roll(drop, 1, dim), pltpu.roll(press, 1, dim))
        if following is not None:
            up = lax.bitwise_and(flags, 4) > 0
            flux = faces(grid_ref[PERM + 2, z], grid_ref[PERM + 2, z + 1], mob, following[1], up)
            drop = depth - grid_ref[DEPTH, z + 1]
            add(4, flux, drop, following[0])
        if before is not None:
            add(5, before[0], -before[1], before[2])
        if following is not None:
            before = (flux, drop, press)
        for name, coupling in couplings.items():
            grid_ref[COUP + name, z] = coupling
        grid_ref[DIAG, z] = diag
        grid_ref[RHS, z] = rhs
        grid_ref[AROUND, z] = around
        grid_ref[MOB, z] = mobility
        this = following


def slot_bhp(bhp, well_ref, index_ref):
    well_row, well_lane = places(well_ref[...], LANES)
    return live_index(well_ref, index_ref) * well_gather(bhp, well_row, well_lane)


def sides(a, b, axis):
    even = is_even(axis)
    return jnp.where(even, a, b), jnp.where(even, b, a)


def first_update(
    given_ref, sums_ref, cell_ref, well_ref, index_ref,
    own_yb_ref, own_xb_ref, own_xa_ref, own_ya_ref, yb_ref, xb_ref, xa_ref, ya_ref,
    grid_ref, out_ref, oxb_ref, oxa_ref, known_ref, bound_ref, flank_ref,
    side_ref, push_ref, block_ref, sems,
):
    layers, width, lanes = grid_ref.shape[1:]
    rows = layers * width
    (high, low), (nxt, prev) = (
        sides(own_xa_ref[...], own_xb_ref[...], "gx"), sides(xa_ref[...], xb_ref[...], "gx")
    )
    high, low, nxt, prev = (
        [rim[i * layers : (i + 1) * layers] for i in range(PLANES)] for rim in (high, low, nxt, prev)
    )
    for where, edge, terms in (
        (0, width - 1, outer_face(high, nxt, high[5] > 0.5)),
        (1, 0, outer_face(low, prev, prev[5] < 0.5)),
    ):
        bound_ref[where] = terms[0]
        for name, term in zip((DIAG, RHS, AROUND), terms):
            grid_ref[name, :, edge, :] = grid_ref[name, :, edge, :] + term
    (high, low), (nxt, prev) = (
        sides(own_ya_ref[...], own_yb_ref[...], "gy"), sides(ya_ref[...], yb_ref[...], "gy")
    )
    high, low, nxt, prev = ([rim[i : i + 1] for i in range(PLANES)] for rim in (high, low, nxt, prev))
    after = outer_face(high, nxt, high[5] > 0.5)
    behind = outer_face(low, prev, prev[5] < 0.5)
    flank_ref[0:1, :] = after[0]
    flank_ref[1:2, :] = behind[0]
    stand = upright(list(behind + after), lanes)
    stand = jnp.concatenate([part.astype(BF16) for part in halves(stand)], axis=1)
    wide = (2 * lanes, 3 * lanes)
    from_lane = lax.rem(iota(wide, 0), lanes)
    to_plane, to_lane = places(iota(wide, 1), lanes)
    side_ref[...] = nn(
        stand,
        ones_of(
            ((from_lane == to_plane) & (to_lane == 0)) | ((from_lane == to_plane + 3) & (to_lane == lanes - 1))
        ),
    )
    count = lax.axis_size("gx") * lax.axis_size("gy")
    chunk = sums_ref.shape[0] // count
    well_rows = (chunk - 2) // 2
    group = count // well_rows
    my = lax.axis_index("gy")
    part = sums_ref[0:well_rows, :]
    base = sums_ref[well_rows : 2 * well_rows, :]
    for d in range(1, count):
        part = part + sums_ref[d * chunk : d * chunk + well_rows, :]
        base = base + sums_ref[d * chunk + well_rows : d * chunk + 2 * well_rows, :]
    controls = []
    for k in (2 * well_rows, 2 * well_rows + 1):
        total = sums_ref[pl.ds(k, well_rows, stride=group * chunk), :]
        for j in range(1, group):
            total = total + sums_ref[pl.ds(j * chunk + k, well_rows, stride=group * chunk), :]
        controls.append(total)
    mode, target = controls
    bhp = jnp.where(mode < 0.5, target, (part - target) / base)
    known_ref[0] = mode
    known_ref[1] = target
    known_ref[2] = base
    row, lane = places(cell_ref[...], lanes)
    well_row, well_lane = places(well_ref[...], LANES)
    push_ref[...] = cell_scatter(slot_bhp(bhp, well_ref, index_ref), row, lane, rows, lanes)
    for z in range(layers):
        here = slice(z * width, (z + 1) * width)
        diag, rhs, around = (
            grid_ref[name, z] + side_ref[here, i * lanes : (i + 1) * lanes]
            for i, name in enumerate((DIAG, RHS, AROUND))
        )
        scale = RELAXATION * inverse(diag)
        rhs = scale * rhs
        gain = scale * grid_ref[MOB, z]
        current = (1.0 - RELAXATION) * grid_ref[PRESS, z] + rhs + scale * around + gain * push_ref[here, :]
        grid_ref[SCALE, z] = scale
        grid_ref[RHS, z] = rhs
        grid_ref[GAIN, z] = gain
        grid_ref[CURRENT, z] = current
    current = grid_ref[CURRENT].reshape(rows, lanes)
    oxa_ref[...], oxb_ref[...] = sides(
        grid_ref[CURRENT, :, width - 1, :], grid_ref[CURRENT, :, 0, :], "gx"
    )
    at_cell = cell_find(grid_ref[MOB].reshape(rows, lanes) * current, *cell_pick(row, lane, rows, lanes))
    (part,) = well_scatter([live_index(well_ref, index_ref) * at_cell], well_row, well_lane, well_rows)
    both = jnp.concatenate([half.astype(BF16) for half in halves(current)], axis=1)
    pick_row, pick_lane = iota((2 * EDGE, 2 * lanes), 0), lax.rem(iota((2 * EDGE, 2 * lanes), 1), lanes)
    rims = nt(
        ones_of(((pick_row == 0) & (pick_lane == lanes - 1)) | ((pick_row == 1) & (pick_lane == 0))), both
    )
    pieces = rows // LANES
    split = [
        jnp.concatenate([rims[r : r + 1, i * LANES : (i + 1) * LANES] for i in range(pieces)], axis=0)
        for r in range(2)
    ]
    height = well_rows + pieces
    ends = lax.axis_size("gy")
    for i in range(block_ref.shape[0] // height):
        block_ref[i * height : i * height + well_rows, :] = part
        block_ref[i * height + well_rows : (i + 1) * height, :] = jnp.where(
            i % ends > my, split[0], split[1]
        )
    for copy in repeat_out(block_ref, out_ref, sems):
        copy.wait()


def last_update(
    sums_ref, known_ref, cell_ref, well_ref, index_ref, grid_ref, bound_ref, flank_ref, xb_ref, xa_ref,
    out_ref, bhp_ref, push_ref, side_ref,
):
    layers, width, lanes = out_ref.shape
    rows = layers * width
    count = lax.axis_size("gx") * lax.axis_size("gy")
    height = sums_ref.shape[0] // count
    well_rows = known_ref.shape[1]
    pieces = height - well_rows
    me = lax.axis_index(AXES)
    part = sums_ref[0:well_rows, :]
    for d in range(1, count):
        part = part + sums_ref[d * height : d * height + well_rows, :]
    bhp = jnp.where(known_ref[0] < 0.5, known_ref[1], (part - known_ref[1]) / known_ref[2])
    owned = bhp_ref.shape[1]
    group = LANES // owned
    line = jnp.sum(
        jnp.where(iota(bhp.shape, 0) == me // group, bhp, 0.0), axis=0, keepdims=True
    )
    line = pltpu.roll(line, lax.rem(LANES - lax.rem(me, group) * owned, LANES), 1)
    bhp_ref[...] = line[:, :owned]
    row, lane = places(cell_ref[...], lanes)
    push_ref[...] = cell_scatter(slot_bhp(bhp, well_ref, index_ref), row, lane, rows, lanes)
    strips = []
    for beside in (jnp.maximum(me - 1, 0), jnp.minimum(me + 1, count - 1)):
        strips.append(
            jnp.concatenate(
                [sums_ref[pl.ds(beside * height + well_rows + i, 1), :] for i in range(pieces)], axis=1
            )
        )
    side_ref[...] = upright([flank_ref[1:2, :] * strips[0], flank_ref[0:1, :] * strips[1]], lanes)
    along = iota((width, lanes), 1)
    nxt, prev = sides(xa_ref[...], xb_ref[...], "gx")
    for z in range(layers):
        here = slice(z * width, (z + 1) * width)
        current = grid_ref[CURRENT, z]
        side = side_ref[here, :]
        around = jnp.where(along == 0, side, jnp.where(along == lanes - 1, pltpu.roll(side, lanes - 2, 1), 0.0))
        besides = [
            pltpu.roll(current, width - 1, 0),
            pltpu.roll(current, 1, 0),
            pltpu.roll(current, lanes - 1, 1),
            pltpu.roll(current, 1, 1),
            grid_ref[CURRENT, z + 1] if z + 1 < layers else None,
            grid_ref[CURRENT, z - 1] if z > 0 else None,
        ]
        for i, beside in enumerate(besides):
            if beside is not None:
                around = around + grid_ref[COUP + i, z] * beside
        out_ref[z] = (
            (1.0 - RELAXATION) * current
            + grid_ref[RHS, z]
            + grid_ref[GAIN, z] * push_ref[here, :]
            + grid_ref[SCALE, z] * around
        )
    for where, edge, beyond in ((0, width - 1, nxt), (1, 0, prev)):
        out_ref[:, edge, :] = out_ref[:, edge, :] + grid_ref[SCALE, :, edge, :] * (bound_ref[where] * beyond)


def call(kernel, outs, args, scratch=(), spaces=None, out_spaces=None, aliases=None):
    shapes = [jax.ShapeDtypeStruct(item, F32) if isinstance(item, tuple) else item for item in outs]
    spaces = spaces or [pltpu.VMEM] * len(args)
    out_spaces = out_spaces or [pltpu.VMEM] * len(outs)
    args = [
        pltpu.with_memory_space_constraint(arg, space) if space is pltpu.HBM else arg
        for arg, space in zip(args, spaces)
    ]
    return pl.pallas_call(
        kernel,
        out_shape=shapes,
        in_specs=[pl.BlockSpec(memory_space=space) for space in spaces],
        out_specs=[pl.BlockSpec(memory_space=space) for space in out_spaces],
        scratch_shapes=[pltpu.VMEM(item, F32) if isinstance(item, tuple) else item for item in scratch],
        input_output_aliases=aliases or {},
        compiler_params=pltpu.CompilerParams(vmem_limit_bytes=24 * 1024 * 1024),
        cost_estimate=pl.CostEstimate(flops=1_000_000, bytes_accessed=4_000_000, transcendentals=0),
    )(*args)


def whole_tiles(height, step, count):
    chunks = step
    while chunks * height % 8:
        chunks += step
    assert count % chunks == 0
    return chunks * height


def everyone(rows, count):
    height = rows.shape[0] // count
    swapped = lax.all_to_all(rows.reshape(count, height, 1, LANES), AXES, 0, 0, tiled=True)
    return swapped.reshape(rows.shape)


def to_pair(block, axis):
    count = lax.axis_size(axis)
    return lax.ppermute(block, axis, [(i, i ^ 1) for i in range(count) if i ^ 1 < count])


def to_other(block, axis):
    count = lax.axis_size(axis)
    ends = [(i, i + 1 if i % 2 else i - 1) for i in range(count)]
    return lax.ppermute(block, axis, [(i, j) for i, j in ends if 0 <= j < count])


def body(
    pressure, saturation, permeability, pore_volume, cell_depth, residual, upstream_flags,
    perf_cell, perf_well, perf_index, well_mode, well_target,
):
    layers, width, lanes = pressure.shape
    rows = layers * width
    count = lax.axis_size("gx") * lax.axis_size("gy")
    owned = well_mode.shape[0]
    well_rows = owned * count // LANES
    chunk = 2 * well_rows + 2
    grid = (layers, width, lanes)
    slots = [perf_cell, perf_well, perf_index]
    operands = slots + [
        well_mode[None], well_target[None], saturation, pressure, permeability, cell_depth,
        upstream_flags, pore_volume, residual,
    ]
    height = whole_tiles(chunk, 1, count)
    sums, yb, xb, xa, ya, given, flags = call(
        opening,
        [
            (count * chunk, LANES), (EDGE, rows), (PLANES * layers, lanes), (PLANES * layers, lanes),
            (EDGE, rows), (GRIDS,) + grid, jax.ShapeDtypeStruct(grid, upstream_flags.dtype),
        ],
        operands,
        [pltpu.VMEM(a.shape, a.dtype) for a in operands[:5]]
        + [(height, LANES), pltpu.SemaphoreType.DMA((INPUTS,))]
        + [pltpu.SemaphoreType.DMA((count * chunk // height,))],
        [pltpu.HBM] * INPUTS,
        [pltpu.HBM] + [pltpu.VMEM] * 6,
    )
    rims = [yb, xb, xa, ya]
    rims = rims + [to_other(yb, "gy"), to_other(xb, "gx"), to_pair(xa, "gx"), to_pair(ya, "gy")]
    gathered = everyone(sums, count)
    (given,) = call(
        main_terms,
        [(GRIDS,) + grid],
        [given, sums, flags] + slots,
        [(rows, lanes)],
        [pltpu.VMEM, pl.ANY] + [pltpu.VMEM] * 4,
        None,
        {0: 0},
    )
    chunk = well_rows + rows // LANES
    height = whole_tiles(chunk, lax.axis_size("gy"), count)
    given, sums, xb, xa, known, bound, flank = call(
        first_update,
        [
            (GRIDS,) + grid, (count * chunk, LANES), (layers, lanes), (layers, lanes), (3, well_rows, LANES),
            (2, layers, lanes), (EDGE, rows),
        ],
        [given, gathered] + slots + rims,
        [
            (rows, 3 * lanes), (rows, lanes), (height, LANES),
            pltpu.SemaphoreType.DMA((count * chunk // height,)),
        ],
        None,
        [pltpu.VMEM, pltpu.HBM] + [pltpu.VMEM] * 5,
        {0: 0},
    )
    gathered = everyone(sums, count)
    xb = to_other(xb, "gx")
    xa = to_pair(xa, "gx")
    out, bhp = call(
        last_update,
        [grid, (1, owned)],
        [gathered, known] + slots + [given, bound, flank, xb, xa],
        [(rows, lanes), (rows, lanes)],
    )
    return out, bhp[0]


def solution(mesh):
    return jax.shard_map(
        body,
        mesh=mesh,
        in_specs=(
            P(None, "gx", "gy"),
            P(None, None, "gx", "gy"),
            P(None, None, "gx", "gy"),
            P(None, "gx", "gy"),
            P(None, "gx", "gy"),
            P(None, None, "gx", "gy"),
            P(None, "gx", "gy"),
            P(("gx", "gy"), None),
            P(("gx", "gy"), None),
            P(("gx", "gy"), None),
            P(("gx", "gy")),
            P(("gx", "gy")),
        ),
        out_specs=(P(None, "gx", "gy"), P(("gx", "gy"))),
        check_vma=False,
    )
```

time: 43.3 us -> 39 us (0.901)
  waiting for transfers between devices: 13.2 us -> 4.27 us
  starting transfers between devices: 17.8 us -> 24.7 us
  Pallas kernels: 11.1 us -> 8.94 us
    ppermute x6, starting transfers between devices: 5.7 us -> 14 us  [the longest x3 12 us: to_pair(): lax.ppermute(block, axis, [(i, i ^ 1) for i in range(count) if i ^ 1 < co...]
    all_to_all x2, waiting for transfers between devices: 10.6 us -> 2.62 us  [everyone(): lax.all_to_all(rows.reshape(count, height, 1, LANES), AXES, 0, 0, tiled=T...]
    pallas_call x4, Pallas kernels: 11.1 us -> 8.94 us  [call(): pl.pallas_call(kernel, out_shape=shapes, in_specs=[pl.BlockSpec(memory_sp...]
    all_to_all x2, starting transfers between devices: 12 us -> 10.7 us  [everyone(): lax.all_to_all(rows.reshape(count, height, 1, LANES), AXES, 0, 0, tiled=T...]
    ppermute x6, waiting for transfers between devices: 2.64 us -> 1.65 us  [the longest x3 1.64 us: to_pair(): lax.ppermute(block, axis, [(i, i ^ 1) for i in range(count) if i ^ 1 < co...]
  transfers between devices with their start and end apart: 8 -> 8, of which waited for: 5 -> 3; matrix products, arithmetic and copies ran while one was open for 0% -> 0% of each run, Pallas kernels for 3% -> 5%
where the time goes in v3:
time: 39 us; the launch traced here: 38.7 us
  starting transfers between devices  24.7 us (63%)
  Pallas kernels  8.94 us (23%)
  waiting for transfers between devices  4.27 us (11%)
  between operations  0.76 us (2%)
    ppermute x3, starting transfers between devices, to_pair(): lax.ppermute(block, axis, [(i, i ^ 1) for i in range(count) if i ^ 1 < co...  12 us
    all_to_all x2, starting transfers between devices, everyone(): lax.all_to_all(rows.reshape(count, height, 1, LANES), AXES, 0, 0, tiled=T...  10.7 us
    pallas_call x4, Pallas kernels, call(): pl.pallas_call(kernel, out_shape=shapes, in_specs=[pl.BlockSpec(memory_sp...  8.94 us
    all_to_all x2, waiting for transfers between devices, everyone(): lax.all_to_all(rows.reshape(count, height, 1, LANES), AXES, 0, 0, tiled=T...  2.62 us
    ppermute x3, starting transfers between devices, to_other(): lax.ppermute(block, axis, [(i, j) for i, j in ends if 0 <= j < count])  1.98 us
    ppermute x3, waiting for transfers between devices, to_pair(): lax.ppermute(block, axis, [(i, i ^ 1) for i in range(count) if i ^ 1 < co...  1.64 us
  transfers between devices with their start and end apart: 8, of which 3 were waited for; matrix products, arithmetic and copies ran while one was open for 0% of the time, Pallas kernels for 5%

profile of v3, /device:TPU:0, one launch (start us, length us, event | category | flops | bytes accessed | tf_op | source)
XLA Modules:
  0.0 38.7 jit_solution(6079403151893424392)
XLA Ops:
  0.6 0.0 copy-start.2
  0.6 0.0 copy-start.1
  0.7 0.0 copy-start
  0.7 3.1 %shard_map.131 = (f32[576,128]{1,0:T(8,128)}, f32[8,384]{1,0:T(8,128)S(1)}, f32[72,128]{1,0:T(8,128)S(1)}, f32[72,128]{1,0:T(8,128)S(1)}, f32[8,384]{1,0:T(8,128...) custom-call(s32[1,1024]{1,0:T(1,128)} %cell_ref.5, s32[1,1024]{1,0:T(1,128)} %well_ref.5, ...), custom_call_target="tpu_custom_call" | custom-call | flops 1000000 | bytes 4000000 | tf_op jit(solution)/shard_map/pallas_call | solution.py:511
  3.8 7.3 %all-to-all-start = ((f32[32,18,1,128]{3,2,1,0:T(1,128)}), f32[32,18,1,128]{3,2,1,0:T(1,128)S(1)}, u32[]{:S(2)}, u32[]{:S(2)}) async-start(f32[32,18,1,128]{3,2,1,0:T(1,128)} %bitcast.2), calls=%async_computation | async-start | bytes 589824 | tf_op jit(solution)/shard_map/all_to_all | solution.py:533
  11.1 0.7 %collective-permute-start.1 = (f32[72,128]{1,0:T(8,128)S(1)}, f32[72,128]{1,0:T(8,128)S(1)}, u32[]{:S(2)}, u32[]{:S(2)}) collective-permute-start(f32[72,128]{1,0:T(8,128)S(1)} %get-tuple-element.22.own_xb_ref), channel_id=1, source_target_pairs={{4,8},{8,4},{12,16},{16,12},{20,24},{24,20},{5,9},{9,5},{13,17},{1... | collective-permute-start | bytes 110600 | tf_op jit(solution)/shard_map/ppermute | solution.py:545
  11.8 4.5 %collective-permute-start.2 = (f32[72,128]{1,0:T(8,128)S(1)}, f32[72,128]{1,0:T(8,128)S(1)}, u32[]{:S(2)}, u32[]{:S(2)}) collective-permute-start(f32[72,128]{1,0:T(8,128)S(1)} %get-tuple-element.23.own_xa_ref), channel_id=1, source_target_pairs={{0,4},{4,0},{8,12},{12,8},{16,20},{20,16},{24,28},{28,24},{1,5},{5... | collective-permute-start | bytes 110600 | tf_op jit(solution)/shard_map/ppermute | solution.py:539
  16.3 0.7 %collective-permute-start = (f32[8,384]{1,0:T(8,128)S(1)}, f32[8,384]{1,0:T(8,128)S(1)}, u32[]{:S(2)}, u32[]{:S(2)}) collective-permute-start(f32[8,384]{1,0:T(8,128)S(1)} %get-tuple-element.21.own_yb_ref), channel_id=1, source_target_pairs={{1,2},{2,1},{5,6},{6,5},{9,10},{10,9},{13,14},{14,13},{17,18},{18,... | collective-permute-start | bytes 36872 | tf_op jit(solution)/shard_map/ppermute | solution.py:545
  17.0 2.9 %collective-permute-start.3 = (f32[8,384]{1,0:T(8,128)S(1)}, f32[8,384]{1,0:T(8,128)S(1)}, u32[]{:S(2)}, u32[]{:S(2)}) collective-permute-start(f32[8,384]{1,0:T(8,128)S(1)} %get-tuple-element.24.own_ya_ref), channel_id=1, source_target_pairs={{0,1},{1,0},{2,3},{3,2},{4,5},{5,4},{6,7},{7,6},{8,9},{9,8},{10,11... | collective-permute-start | bytes 36872 | tf_op jit(solution)/shard_map/ppermute | solution.py:539
  19.9 0.0 copy-done.2
  19.9 0.0 copy-done.1
  19.9 0.0 copy-done
  19.9 1.8 %shard_map.132.given_ref = f32[11,12,32,128]{3,2,1,0:T(8,128)S(1)} custom-call(f32[11,12,32,128]{3,2,1,0:T(8,128)S(1)} %get-tuple-element.18.given_ref, f32[576,128]{1,0:T(8,128)} %get-tuple-element.19.after_ref, s32[12,32,128]{2,1,0:T(8,128)S(1)} %get-tuple-element.20.flag_ref, s32[1,1024]{1,0:T(1,128)S(1)} %copy-done, ...), custom_call_target="tpu_custom_call", output_to_operand_aliasing={{}: (0, {})} | custom-call | flops 1000000 | bytes 4000000 | tf_op jit(solution)/shard_map/pallas_call | solution.py:511
  21.7 0.0 collective-permute-done.yb_ref
  21.7 0.0 collective-permute-done.3.ya_ref
  21.8 0.0 collective-permute-done.1.xb_ref
  21.8 0.0 collective-permute-done.2.xa_ref
  21.8 0.8 %all-to-all-done = f32[32,18,1,128]{3,2,1,0:T(1,128)S(1)} async-done(((f32[32,18,1,128]{3,2,1,0:T(1,128)}), f32[32,18,1,128]{3,2,1,0:T(1,128)S(1)}, u32[]{:S(2)}, u32[]{:S(2)}) %all-to-all-start) | async-done | bytes 294944 | tf_op jit(solution)/shard_map/all_to_all | solution.py:533
  22.5 2.6 %shard_map.133 = (f32[11,12,32,128]{3,2,1,0:T(8,128)S(1)}, f32[352,128]{1,0:T(8,128)}, f32[12,128]{1,0:T(8,128)S(1)}, f32[12,128]{1,0:T(8,128)S(1)}, f32[3,8,128...) custom-call(f32[11,12,32,128]{3,2,1,0:T(8,128)S(1)} %shard_map.132.given_re, ...), custom_call_target="tpu_custom_call", output_to_operand_aliasing={{0}: (0, {})} | custom-call | flops 1000000 | bytes 4000000 | tf_op jit(solution)/shard_map/pallas_call | solution.py:511
  25.1 3.4 %all-to-all-start.1 = ((f32[32,11,1,128]{3,2,1,0:T(1,128)}), f32[32,11,1,128]{3,2,1,0:T(1,128)S(1)}, u32[]{:S(2)}, u32[]{:S(2)}) async-start(f32[32,11,1,128]{3,2,1,0:T(1,128)} %bitcast.4), calls=%async_computation.1 | async-start | bytes 360448 | tf_op jit(solution)/shard_map/all_to_all | solution.py:533
  28.6 0.7 %collective-permute-start.4 = (f32[12,128]{1,0:T(8,128)S(1)}, f32[12,128]{1,0:T(8,128)S(1)}, u32[]{:S(2)}, u32[]{:S(2)}) collective-permute-start(f32[12,128]{1,0:T(8,128)S(1)} %get-tuple-element.30), channel_id=1, source_target_pairs={{4,8},{8,4},{12,16},{16,12},{20,24},{24,20},{5,9},{9,5},{13,17},{1... | collective-permute-start | bytes 18440 | tf_op jit(solution)/shard_map/ppermute | solution.py:545
  29.2 4.5 %collective-permute-start.5 = (f32[12,128]{1,0:T(8,128)S(1)}, f32[12,128]{1,0:T(8,128)S(1)}, u32[]{:S(2)}, u32[]{:S(2)}) collective-permute-start(f32[12,128]{1,0:T(8,128)S(1)} %get-tuple-element.31), channel_id=1, source_target_pairs={{0,4},{4,0},{8,12},{12,8},{16,20},{20,16},{24,28},{28,24},{1,5},{5... | collective-permute-start | bytes 18440 | tf_op jit(solution)/shard_map/ppermute | solution.py:539
  33.8 0.0 collective-permute-done.4.xb_ref
  33.8 1.6 %collective-permute-done.5.xa_ref = f32[12,128]{1,0:T(8,128)S(1)} collective-permute-done((f32[12,128]{1,0:T(8,128)S(1)}, f32[12,128]{1,0:T(8,128)S(1)}, u32[]{:S(2)}, u32[]{:S(2)}) %collective-permute-start.5) | collective-permute-done | bytes 6176 | tf_op jit(solution)/shard_map/ppermute | solution.py:539
  35.4 1.9 %all-to-all-done.1 = f32[32,11,1,128]{3,2,1,0:T(1,128)S(1)} async-done(((f32[32,11,1,128]{3,2,1,0:T(1,128)}), f32[32,11,1,128]{3,2,1,0:T(1,128)S(1)}, u32[]{:S(2)}, u32[]{:S(2)}) %all-to-all-start.1) | async-done | bytes 180256 | tf_op jit(solution)/shard_map/all_to_all | solution.py:533
  37.3 1.4 %shard_map.134 = (f32[12,32,128]{2,1,0:T(8,128)}, f32[1,32]{1,0:T(1,128)}) custom-call(f32[352,128]{1,0:T(8,128)S(1)} %bitcast.8, f32[3,8,128]{2,1,0:T(8,128)S(1)} %get-tuple-element.26.known_ref, s32[1,1024]{1,0:T(1,128)S(1)} %copy-done, s32[1,1024]{1,0:T(1,128)S(1)} %copy-done.1, f32[1,1024]{1,0:T(1,128)S(1)} %copy-done.2, ...), custom_call_target="tpu_custom_call" | custom-call | flops 1000000 | bytes 4000000 | tf_op jit(solution)/shard_map/pallas_call | solution.py:511
Async XLA Ops:
  0.6 19.3 %copy-start.2 = (f32[1,1024]{1,0:T(1,128)S(1)}, f32[1,1024]{1,0:T(1,128)}, u32[]{:S(2)}) copy-start(f32[1,1024]{1,0:T(1,128)} %index_ref.5) | copy-start | bytes 12292
  0.6 19.3 %copy-start.1 = (s32[1,1024]{1,0:T(1,128)S(1)}, s32[1,1024]{1,0:T(1,128)}, u32[]{:S(2)}) copy-start(s32[1,1024]{1,0:T(1,128)} %well_ref.5) | copy-start | bytes 12292
  0.7 19.2 %copy-start = (s32[1,1024]{1,0:T(1,128)S(1)}, s32[1,1024]{1,0:T(1,128)}, u32[]{:S(2)}) copy-start(s32[1,1024]{1,0:T(1,128)} %cell_ref.5) | copy-start | bytes 12292
  3.8 18.7 %all-to-all-start = ((f32[32,18,1,128]{3,2,1,0:T(1,128)}), f32[32,18,1,128]{3,2,1,0:T(1,128)S(1)}, u32[]{:S(2)}, u32[]{:S(2)}) async-start(f32[32,18,1,128]{3,2,1,0:T(1,128)} %bitcast.2), calls=%async_computation | async-start | bytes 589824 | tf_op jit(solution)/shard_map/all_to_all | solution.py:533
  11.1 10.6 %collective-permute-start.1 = (f32[72,128]{1,0:T(8,128)S(1)}, f32[72,128]{1,0:T(8,128)S(1)}, u32[]{:S(2)}, u32[]{:S(2)}) collective-permute-start(f32[72,128]{1,0:T(8,128)S(1)} %get-tuple-element.22.own_xb_ref), channel_id=1, source_target_pairs={{4,8},{8,4},{12,16},{16,12},{20,24},{24,20},{5,9},{9,5},{13,17},{1... | collective-permute-start | bytes 110600 | tf_op jit(solution)/shard_map/ppermute | solution.py:545
  11.8 10.0 %collective-permute-start.2 = (f32[72,128]{1,0:T(8,128)S(1)}, f32[72,128]{1,0:T(8,128)S(1)}, u32[]{:S(2)}, u32[]{:S(2)}) collective-permute-start(f32[72,128]{1,0:T(8,128)S(1)} %get-tuple-element.23.own_xa_ref), channel_id=1, source_target_pairs={{0,4},{4,0},{8,12},{12,8},{16,20},{20,16},{24,28},{28,24},{1,5},{5... | collective-permute-start | bytes 110600 | tf_op jit(solution)/shard_map/ppermute | solution.py:539
  16.3 5.4 %collective-permute-start = (f32[8,384]{1,0:T(8,128)S(1)}, f32[8,384]{1,0:T(8,128)S(1)}, u32[]{:S(2)}, u32[]{:S(2)}) collective-permute-start(f32[8,384]{1,0:T(8,128)S(1)} %get-tuple-element.21.own_yb_ref), channel_id=1, source_target_pairs={{1,2},{2,1},{5,6},{6,5},{9,10},{10,9},{13,14},{14,13},{17,18},{18,... | collective-permute-start | bytes 36872 | tf_op jit(solution)/shard_map/ppermute | solution.py:545
  17.0 4.7 %collective-permute-start.3 = (f32[8,384]{1,0:T(8,128)S(1)}, f32[8,384]{1,0:T(8,128)S(1)}, u32[]{:S(2)}, u32[]{:S(2)}) collective-permute-start(f32[8,384]{1,0:T(8,128)S(1)} %get-tuple-element.24.own_ya_ref), channel_id=1, source_target_pairs={{0,1},{1,0},{2,3},{3,2},{4,5},{5,4},{6,7},{7,6},{8,9},{9,8},{10,11... | collective-permute-start | bytes 36872 | tf_op jit(solution)/shard_map/ppermute | solution.py:539
  25.1 12.2 %all-to-all-start.1 = ((f32[32,11,1,128]{3,2,1,0:T(1,128)}), f32[32,11,1,128]{3,2,1,0:T(1,128)S(1)}, u32[]{:S(2)}, u32[]{:S(2)}) async-start(f32[32,11,1,128]{3,2,1,0:T(1,128)} %bitcast.4), calls=%async_computation.1 | async-start | bytes 360448 | tf_op jit(solution)/shard_map/all_to_all | solution.py:533
  28.6 5.2 %collective-permute-start.4 = (f32[12,128]{1,0:T(8,128)S(1)}, f32[12,128]{1,0:T(8,128)S(1)}, u32[]{:S(2)}, u32[]{:S(2)}) collective-permute-start(f32[12,128]{1,0:T(8,128)S(1)} %get-tuple-element.30), channel_id=1, source_target_pairs={{4,8},{8,4},{12,16},{16,12},{20,24},{24,20},{5,9},{9,5},{13,17},{1... | collective-permute-start | bytes 18440 | tf_op jit(solution)/shard_map/ppermute | solution.py:545
  29.2 6.2 %collective-permute-start.5 = (f32[12,128]{1,0:T(8,128)S(1)}, f32[12,128]{1,0:T(8,128)S(1)}, u32[]{:S(2)}, u32[]{:S(2)}) collective-permute-start(f32[12,128]{1,0:T(8,128)S(1)} %get-tuple-element.31), channel_id=1, source_target_pairs={{0,4},{4,0},{8,12},{12,8},{16,20},{20,16},{24,28},{28,24},{1,5},{5... | collective-permute-start | bytes 18440 | tf_op jit(solution)/shard_map/ppermute | solution.py:539

commit v4 on v3

--- a/solution.py
+++ b/solution.py
@@ -149,7 +149,7 @@
 def opening(*refs):
     inputs, sems, out_sems = refs[:INPUTS], refs[-2], refs[-1]
     sums_ref, yb_ref, xb_ref, xa_ref, ya_ref, grid_ref, flag_ref = refs[INPUTS : INPUTS + 7]
-    cell_ref, well_ref, index_ref, mode_ref, target_ref, block_ref = refs[INPUTS + 7 : -2]
+    cell_ref, well_ref, index_ref, mode_ref, target_ref, block_ref, lying_ref = refs[INPUTS + 7 : -2]
     slot_refs = [cell_ref, well_ref, index_ref, mode_ref, target_ref]
     sat_ref, perm_ref = grid_ref.at[SAT : SAT + 2], grid_ref.at[PERM : PERM + 3]
     holds = slot_refs + [
@@ -184,24 +184,33 @@
     block = jnp.concatenate(sums + controls, axis=0)
     block_ref[...] = jnp.concatenate([block] * (block_ref.shape[0] // chunk_rows), axis=0)
     outgoing = repeat_out(block_ref, sums_ref, out_sems)
-    pick_row, pick_lane = iota((2 * EDGE, 2 * lanes), 0), lax.rem(iota((2 * EDGE, 2 * lanes), 1), lanes)
-
-    def rim(i, plane):
-        both = jnp.concatenate([part.astype(BF16) for part in halves(plane.reshape(rows, lanes))], axis=1)
-        pick = ones_of(
-            ((pick_row == i) & (pick_lane == lanes - 1)) | ((pick_row == EDGE + i) & (pick_lane == 0))
-        )
-        return nt(pick, both)
-
-    total = rim(0, grid_ref[PRESS]) + rim(1, grid_ref[SAT]) + rim(2, grid_ref[SAT + 1])
+    pair = lax.shift_right_logical(iota((rows, lanes), 1), 1)
+
+    def rim(total, i, plane):
+        return jnp.where(pair == i, pltpu.roll(plane.reshape(rows, lanes), 2 * i + 1, 1), total)
+
+    total = rim(jnp.zeros((rows, lanes), F32), 0, grid_ref[PRESS])
+    total = rim(rim(total, 1, grid_ref[SAT]), 2, grid_ref[SAT + 1])
     later[2].wait()
-    total = total + rim(3, grid_ref[PERM + 1])
+    total = rim(total, 3, grid_ref[PERM + 1])
     later[3].wait()
-    total = total + rim(4, grid_ref[DEPTH])
+    total = rim(total, 4, grid_ref[DEPTH])
     later[4].wait()
     bit_y = lax.bitwise_and(lax.shift_right_logical(flag_ref[...], 1), 1).astype(F32)
-    total = total + rim(PLANES - 1, bit_y)
+    total = rim(total, PLANES - 1, bit_y)
+    pieces = [
+        (i * 2 * EDGE, jnp.transpose(total[i * LANES : (i + 1) * LANES])[: 2 * EDGE])
+        for i in range(rows // LANES)
+    ]
+    for first, piece in pieces:
+        lying_ref[first : first + 2 * EDGE, :] = piece
+    high, low = (
+        jnp.concatenate([lying_ref[pl.ds(first + k, EDGE, stride=2), :] for first, _ in pieces], axis=1)
+        for k in range(2)
+    )
     x_even, y_even = is_even("gx"), is_even("gy")
+    ya_ref[...] = jnp.where(y_even, high, low)
+    yb_ref[...] = jnp.where(y_even, low, high)
     last = width - 1
     ends = [
         [
@@ -217,8 +226,6 @@
     for i, (high, low) in enumerate(zip(*ends)):
         xa_ref[i * layers : (i + 1) * layers, :] = jnp.where(x_even, high, low)
         xb_ref[i * layers : (i + 1) * layers, :] = jnp.where(x_even, low, high)
-    ya_ref[...] = jnp.where(y_even, total[:EDGE], total[EDGE:])
-    yb_ref[...] = jnp.where(y_even, total[EDGE:], total[:EDGE])
     for copy in later[5:] + outgoing:
         copy.wait()
 
@@ -335,6 +342,12 @@
     return jnp.where(even, a, b), jnp.where(even, b, a)
 
 
+def close_ends(nxt, prev, axis):
+    me = lax.axis_index(axis)
+    nxt[3] = jnp.where(me < lax.axis_size(axis) - 1, nxt[3], 0.0)
+    prev[3] = jnp.where(me > 0, prev[3], 0.0)
+
+
 def first_update(
     given_ref, sums_ref, cell_ref, well_ref, index_ref,
     own_yb_ref, own_xb_ref, own_xa_ref, own_ya_ref, yb_ref, xb_ref, xa_ref, ya_ref,
@@ -349,6 +362,7 @@
     high, low, nxt, prev = (
         [rim[i * layers : (i + 1) * layers] for i in range(PLANES)] for rim in (high, low, nxt, prev)
     )
+    close_ends(nxt, prev, "gx")
     for where, edge, terms in (
         (0, width - 1, outer_face(high, nxt, high[5] > 0.5)),
         (1, 0, outer_face(low, prev, prev[5] < 0.5)),
@@ -360,6 +374,7 @@
         sides(own_ya_ref[...], own_yb_ref[...], "gy"), sides(ya_ref[...], yb_ref[...], "gy")
     )
     high, low, nxt, prev = ([rim[i : i + 1] for i in range(PLANES)] for rim in (high, low, nxt, prev))
+    close_ends(nxt, prev, "gy")
     after = outer_face(high, nxt, high[5] > 0.5)
     behind = outer_face(low, prev, prev[5] < 0.5)
     flank_ref[0:1, :] = after[0]
@@ -536,13 +551,24 @@
 
 def to_pair(block, axis):
     count = lax.axis_size(axis)
-    return lax.ppermute(block, axis, [(i, i ^ 1) for i in range(count) if i ^ 1 < count])
+    assert count % 2 == 0
+    return lax.ppermute(block, axis, [(i, i ^ 1) for i in range(count)])
 
 
 def to_other(block, axis):
-    count = lax.axis_size(axis)
-    ends = [(i, i + 1 if i % 2 else i - 1) for i in range(count)]
-    return lax.ppermute(block, axis, [(i, j) for i, j in ends if 0 <= j < count])
+    sizes = {name: lax.axis_size(name) for name in AXES}
+    moves = []
+    for gx in range(sizes["gx"]):
+        for gy in range(sizes["gy"]):
+            there = {"gx": gx, "gy": gy}
+            away = there[axis] + (1 if there[axis] % 2 else -1)
+            if 0 <= away < sizes[axis]:
+                there[axis] = away
+            else:
+                cross = "gy" if axis == "gx" else "gx"
+                there[cross] ^= 1
+            moves.append((gx * sizes["gy"] + gy, there["gx"] * sizes["gy"] + there["gy"]))
+    return lax.ppermute(block, AXES, moves)
 
 
 def body(
@@ -570,7 +596,7 @@
         ],
         operands,
         [pltpu.VMEM(a.shape, a.dtype) for a in operands[:5]]
-        + [(height, LANES), pltpu.SemaphoreType.DMA((INPUTS,))]
+        + [(height, LANES), (2 * EDGE * (rows // LANES), LANES), pltpu.SemaphoreType.DMA((INPUTS,))]
         + [pltpu.SemaphoreType.DMA((count * chunk // height,))],
         [pltpu.HBM] * INPUTS,
         [pltpu.HBM] + [pltpu.VMEM] * 6,

time: 39 us -> 38.1 us (0.977)
  starting transfers between devices: 24.7 us -> 18 us
  waiting for transfers between devices: 4.27 us -> 10.2 us
    ppermute x6, starting transfers between devices: 14 us -> 8.09 us  [the longest x3 7.52 us: to_pair(): return lax.ppermute(block, axis, [(i, i ^ 1) for i in range(count)])]
    all_to_all x2, waiting for transfers between devices: 2.62 us -> 8.07 us  [everyone(): lax.all_to_all(rows.reshape(count, height, 1, LANES), AXES, 0, 0, tiled=T...]
    all_to_all x2, starting transfers between devices: 10.7 us -> 9.9 us  [everyone(): lax.all_to_all(rows.reshape(count, height, 1, LANES), AXES, 0, 0, tiled=T...]
    ppermute x6, waiting for transfers between devices: 1.65 us -> 2.11 us  [the longest x3 1.73 us: to_pair(): return lax.ppermute(block, axis, [(i, i ^ 1) for i in range(count)])]
  transfers between devices with their start and end apart: 8 -> 8, of which waited for: 3 -> 4; matrix products, arithmetic and copies ran while one was open for 0% -> 0% of each run, Pallas kernels for 5% -> 5%
where the time goes in v4:
time: 38.1 us; the launch traced here: 37.7 us
  starting transfers between devices  18 us (47%)
  waiting for transfers between devices  10.2 us (27%)
  Pallas kernels  8.84 us (23%)
  between operations  0.71 us (2%)
    all_to_all x2, starting transfers between devices, everyone(): lax.all_to_all(rows.reshape(count, height, 1, LANES), AXES, 0, 0, tiled=T...  9.9 us
    pallas_call x4, Pallas kernels, call(): pl.pallas_call(kernel, out_shape=shapes, in_specs=[pl.BlockSpec(memory_sp...  8.84 us
    all_to_all x2, waiting for transfers between devices, everyone(): lax.all_to_all(rows.reshape(count, height, 1, LANES), AXES, 0, 0, tiled=T...  8.07 us
    ppermute x3, starting transfers between devices, to_pair(): return lax.ppermute(block, axis, [(i, i ^ 1) for i in range(count)])  7.52 us
    ppermute x3, waiting for transfers between devices, to_pair(): return lax.ppermute(block, axis, [(i, i ^ 1) for i in range(count)])  1.73 us
  transfers between devices with their start and end apart: 8, of which 4 were waited for; matrix products, arithmetic and copies ran while one was open for 0% of the time, Pallas kernels for 5%

profile of v4, /device:TPU:0, one launch (start us, length us, event | category | flops | bytes accessed | tf_op | source)
XLA Modules:
  0.0 37.7 jit_solution(12773849196998671011)
XLA Ops:
  0.6 0.0 copy-start.2
  0.6 0.0 copy-start.1
  0.7 0.0 copy-start
  0.7 3.0 %shard_map.131 = (f32[576,128]{1,0:T(8,128)}, f32[8,384]{1,0:T(8,128)S(1)}, f32[72,128]{1,0:T(8,128)S(1)}, f32[72,128]{1,0:T(8,128)S(1)}, f32[8,384]{1,0:T(8,128...) custom-call(s32[1,1024]{1,0:T(1,128)} %cell_ref.5, s32[1,1024]{1,0:T(1,128)} %well_ref.5, ...), custom_call_target="tpu_custom_call" | custom-call | flops 1000000 | bytes 4000000 | tf_op jit(solution)/shard_map/pallas_call | solution.py:526
  3.7 7.3 %all-to-all-start = ((f32[32,18,1,128]{3,2,1,0:T(1,128)}), f32[32,18,1,128]{3,2,1,0:T(1,128)S(1)}, u32[]{:S(2)}, u32[]{:S(2)}) async-start(f32[32,18,1,128]{3,2,1,0:T(1,128)} %bitcast.2), calls=%async_computation | async-start | bytes 589824 | tf_op jit(solution)/shard_map/all_to_all | solution.py:548
  11.0 0.3 collective-permute-start.1
  11.3 3.0 %collective-permute-start.2 = (f32[72,128]{1,0:T(8,128)S(1)}, f32[72,128]{1,0:T(8,128)S(1)}, u32[]{:S(2)}, u32[]{:S(2)}) collective-permute-start(f32[72,128]{1,0:T(8,128)S(1)} %get-tuple-element.23.own_xa_ref), channel_id=1, source_target_pairs={{0,4},{4,0},{8,12},{12,8},{16,20},{20,16},{24,28},{28,24},{1,5},{5... | collective-permute-start | bytes 110600 | tf_op jit(solution)/shard_map/ppermute | solution.py:555
  14.3 0.0 collective-permute-start
  14.4 1.5 %collective-permute-start.3 = (f32[8,384]{1,0:T(8,128)S(1)}, f32[8,384]{1,0:T(8,128)S(1)}, u32[]{:S(2)}, u32[]{:S(2)}) collective-permute-start(f32[8,384]{1,0:T(8,128)S(1)} %get-tuple-element.24.own_ya_ref), channel_id=1, source_target_pairs={{0,1},{1,0},{2,3},{3,2},{4,5},{5,4},{6,7},{7,6},{8,9},{9,8},{10,11... | collective-permute-start | bytes 36872 | tf_op jit(solution)/shard_map/ppermute | solution.py:555
  15.9 0.0 copy-done.2
  15.9 0.0 copy-done.1
  15.9 0.0 copy-done
  15.9 1.8 %shard_map.132.given_ref = f32[11,12,32,128]{3,2,1,0:T(8,128)S(1)} custom-call(f32[11,12,32,128]{3,2,1,0:T(8,128)S(1)} %get-tuple-element.18.given_ref, f32[576,128]{1,0:T(8,128)} %get-tuple-element.19.after_ref, s32[12,32,128]{2,1,0:T(8,128)S(1)} %get-tuple-element.20.flag_ref, s32[1,1024]{1,0:T(1,128)S(1)} %copy-done, ...), custom_call_target="tpu_custom_call", output_to_operand_aliasing={{}: (0, {})} | custom-call | flops 1000000 | bytes 4000000 | tf_op jit(solution)/shard_map/pallas_call | solution.py:526
  17.7 0.4 collective-permute-done.yb_ref
  18.1 0.0 collective-permute-done.3.ya_ref
  18.1 0.0 collective-permute-done.1.xb_ref
  18.1 0.0 collective-permute-done.2.xa_ref
  18.1 4.3 %all-to-all-done = f32[32,18,1,128]{3,2,1,0:T(1,128)S(1)} async-done(((f32[32,18,1,128]{3,2,1,0:T(1,128)}), f32[32,18,1,128]{3,2,1,0:T(1,128)S(1)}, u32[]{:S(2)}, u32[]{:S(2)}) %all-to-all-start) | async-done | bytes 294944 | tf_op jit(solution)/shard_map/all_to_all | solution.py:548
  22.4 2.6 %shard_map.133 = (f32[11,12,32,128]{3,2,1,0:T(8,128)S(1)}, f32[352,128]{1,0:T(8,128)}, f32[12,128]{1,0:T(8,128)S(1)}, f32[12,128]{1,0:T(8,128)S(1)}, f32[3,8,128...) custom-call(f32[11,12,32,128]{3,2,1,0:T(8,128)S(1)} %shard_map.132.given_re, ...), custom_call_target="tpu_custom_call", output_to_operand_aliasing={{0}: (0, {})} | custom-call | flops 1000000 | bytes 4000000 | tf_op jit(solution)/shard_map/pallas_call | solution.py:526
  25.0 2.6 %all-to-all-start.1 = ((f32[32,11,1,128]{3,2,1,0:T(1,128)}), f32[32,11,1,128]{3,2,1,0:T(1,128)S(1)}, u32[]{:S(2)}, u32[]{:S(2)}) async-start(f32[32,11,1,128]{3,2,1,0:T(1,128)} %bitcast.4), calls=%async_computation.1 | async-start | bytes 360448 | tf_op jit(solution)/shard_map/all_to_all | solution.py:548
  27.6 0.2 collective-permute-start.4
  27.9 3.0 %collective-permute-start.5 = (f32[12,128]{1,0:T(8,128)S(1)}, f32[12,128]{1,0:T(8,128)S(1)}, u32[]{:S(2)}, u32[]{:S(2)}) collective-permute-start(f32[12,128]{1,0:T(8,128)S(1)} %get-tuple-element.31), channel_id=1, source_target_pairs={{0,4},{4,0},{8,12},{12,8},{16,20},{20,16},{24,28},{28,24},{1,5},{5... | collective-permute-start | bytes 18440 | tf_op jit(solution)/shard_map/ppermute | solution.py:555
  30.9 0.0 collective-permute-done.4.xb_ref
  30.9 1.7 %collective-permute-done.5.xa_ref = f32[12,128]{1,0:T(8,128)S(1)} collective-permute-done((f32[12,128]{1,0:T(8,128)S(1)}, f32[12,128]{1,0:T(8,128)S(1)}, u32[]{:S(2)}, u32[]{:S(2)}) %collective-permute-start.5) | collective-permute-done | bytes 6176 | tf_op jit(solution)/shard_map/ppermute | solution.py:555
  32.6 3.8 %all-to-all-done.1 = f32[32,11,1,128]{3,2,1,0:T(1,128)S(1)} async-done(((f32[32,11,1,128]{3,2,1,0:T(1,128)}), f32[32,11,1,128]{3,2,1,0:T(1,128)S(1)}, u32[]{:S(2)}, u32[]{:S(2)}) %all-to-all-start.1) | async-done | bytes 180256 | tf_op jit(solution)/shard_map/all_to_all | solution.py:548
  36.4 1.4 %shard_map.134 = (f32[12,32,128]{2,1,0:T(8,128)}, f32[1,32]{1,0:T(1,128)}) custom-call(f32[352,128]{1,0:T(8,128)S(1)} %bitcast.8, f32[3,8,128]{2,1,0:T(8,128)S(1)} %get-tuple-element.26.known_ref, s32[1,1024]{1,0:T(1,128)S(1)} %copy-done, s32[1,1024]{1,0:T(1,128)S(1)} %copy-done.1, f32[1,1024]{1,0:T(1,128)S(1)} %copy-done.2, ...), custom_call_target="tpu_custom_call" | custom-call | flops 1000000 | bytes 4000000 | tf_op jit(solution)/shard_map/pallas_call | solution.py:526
Async XLA Ops:
  0.6 15.3 %copy-start.2 = (f32[1,1024]{1,0:T(1,128)S(1)}, f32[1,1024]{1,0:T(1,128)}, u32[]{:S(2)}) copy-start(f32[1,1024]{1,0:T(1,128)} %index_ref.5) | copy-start | bytes 12292
  0.6 15.3 %copy-start.1 = (s32[1,1024]{1,0:T(1,128)S(1)}, s32[1,1024]{1,0:T(1,128)}, u32[]{:S(2)}) copy-start(s32[1,1024]{1,0:T(1,128)} %well_ref.5) | copy-start | bytes 12292
  0.7 15.3 %copy-start = (s32[1,1024]{1,0:T(1,128)S(1)}, s32[1,1024]{1,0:T(1,128)}, u32[]{:S(2)}) copy-start(s32[1,1024]{1,0:T(1,128)} %cell_ref.5) | copy-start | bytes 12292
  3.7 18.7 %all-to-all-start = ((f32[32,18,1,128]{3,2,1,0:T(1,128)}), f32[32,18,1,128]{3,2,1,0:T(1,128)S(1)}, u32[]{:S(2)}, u32[]{:S(2)}) async-start(f32[32,18,1,128]{3,2,1,0:T(1,128)} %bitcast.2), calls=%async_computation | async-start | bytes 589824 | tf_op jit(solution)/shard_map/all_to_all | solution.py:548
  11.0 7.1 %collective-permute-start.1 = (f32[72,128]{1,0:T(8,128)S(1)}, f32[72,128]{1,0:T(8,128)S(1)}, u32[]{:S(2)}, u32[]{:S(2)}) collective-permute-start(f32[72,128]{1,0:T(8,128)S(1)} %get-tuple-element.22.own_xb_ref), channel_id=1, source_target_pairs={{0,1},{1,0},{2,3},{3,2},{4,8},{5,9},{6,10},{7,11},{8,4},{9,5},{10,... | collective-permute-start | bytes 110600 | tf_op jit(solution)/shard_map/ppermute | solution.py:571
  11.3 6.8 %collective-permute-start.2 = (f32[72,128]{1,0:T(8,128)S(1)}, f32[72,128]{1,0:T(8,128)S(1)}, u32[]{:S(2)}, u32[]{:S(2)}) collective-permute-start(f32[72,128]{1,0:T(8,128)S(1)} %get-tuple-element.23.own_xa_ref), channel_id=1, source_target_pairs={{0,4},{4,0},{8,12},{12,8},{16,20},{20,16},{24,28},{28,24},{1,5},{5... | collective-permute-start | bytes 110600 | tf_op jit(solution)/shard_map/ppermute | solution.py:555
  14.3 3.8 %collective-permute-start = (f32[8,384]{1,0:T(8,128)S(1)}, f32[8,384]{1,0:T(8,128)S(1)}, u32[]{:S(2)}, u32[]{:S(2)}) collective-permute-start(f32[8,384]{1,0:T(8,128)S(1)} %get-tuple-element.21.own_yb_ref), channel_id=1, source_target_pairs={{0,4},{1,2},{2,1},{3,7},{4,0},{5,6},{6,5},{7,3},{8,12},{9,10},{10,... | collective-permute-start | bytes 36872 | tf_op jit(solution)/shard_map/ppermute | solution.py:571
  14.4 3.8 %collective-permute-start.3 = (f32[8,384]{1,0:T(8,128)S(1)}, f32[8,384]{1,0:T(8,128)S(1)}, u32[]{:S(2)}, u32[]{:S(2)}) collective-permute-start(f32[8,384]{1,0:T(8,128)S(1)} %get-tuple-element.24.own_ya_ref), channel_id=1, source_target_pairs={{0,1},{1,0},{2,3},{3,2},{4,5},{5,4},{6,7},{7,6},{8,9},{9,8},{10,11... | collective-permute-start | bytes 36872 | tf_op jit(solution)/shard_map/ppermute | solution.py:555
  25.0 11.3 %all-to-all-start.1 = ((f32[32,11,1,128]{3,2,1,0:T(1,128)}), f32[32,11,1,128]{3,2,1,0:T(1,128)S(1)}, u32[]{:S(2)}, u32[]{:S(2)}) async-start(f32[32,11,1,128]{3,2,1,0:T(1,128)} %bitcast.4), calls=%async_computation.1 | async-start | bytes 360448 | tf_op jit(solution)/shard_map/all_to_all | solution.py:548
  27.6 3.2 %collective-permute-start.4 = (f32[12,128]{1,0:T(8,128)S(1)}, f32[12,128]{1,0:T(8,128)S(1)}, u32[]{:S(2)}, u32[]{:S(2)}) collective-permute-start(f32[12,128]{1,0:T(8,128)S(1)} %get-tuple-element.30), channel_id=1, source_target_pairs={{0,1},{1,0},{2,3},{3,2},{4,8},{5,9},{6,10},{7,11},{8,4},{9,5},{10,... | collective-permute-start | bytes 18440 | tf_op jit(solution)/shard_map/ppermute | solution.py:571
  27.9 4.7 %collective-permute-start.5 = (f32[12,128]{1,0:T(8,128)S(1)}, f32[12,128]{1,0:T(8,128)S(1)}, u32[]{:S(2)}, u32[]{:S(2)}) collective-permute-start(f32[12,128]{1,0:T(8,128)S(1)} %get-tuple-element.31), channel_id=1, source_target_pairs={{0,4},{4,0},{8,12},{12,8},{16,20},{20,16},{24,28},{28,24},{1,5},{5... | collective-permute-start | bytes 18440 | tf_op jit(solution)/shard_map/ppermute | solution.py:555

commit v5 on v4

--- a/solution.py
+++ b/solution.py
@@ -348,11 +348,9 @@
     prev[3] = jnp.where(me > 0, prev[3], 0.0)
 
 
-def first_update(
-    given_ref, sums_ref, cell_ref, well_ref, index_ref,
-    own_yb_ref, own_xb_ref, own_xa_ref, own_ya_ref, yb_ref, xb_ref, xa_ref, ya_ref,
-    grid_ref, out_ref, oxb_ref, oxa_ref, known_ref, bound_ref, flank_ref,
-    side_ref, push_ref, block_ref, sems,
+def outer_terms(
+    given_ref, own_yb_ref, own_xb_ref, own_xa_ref, own_ya_ref, yb_ref, xb_ref, xa_ref, ya_ref,
+    grid_ref, bound_ref, flank_ref, side_ref,
 ):
     layers, width, lanes = grid_ref.shape[1:]
     rows = layers * width
@@ -390,6 +388,26 @@
             ((from_lane == to_plane) & (to_lane == 0)) | ((from_lane == to_plane + 3) & (to_lane == lanes - 1))
         ),
     )
+    for z in range(layers):
+        here = slice(z * width, (z + 1) * width)
+        diag, rhs, around = (
+            grid_ref[name, z] + side_ref[here, i * lanes : (i + 1) * lanes]
+            for i, name in enumerate((DIAG, RHS, AROUND))
+        )
+        scale = RELAXATION * inverse(diag)
+        rhs = scale * rhs
+        grid_ref[CURRENT, z] = (1.0 - RELAXATION) * grid_ref[PRESS, z] + rhs + scale * around
+        grid_ref[SCALE, z] = scale
+        grid_ref[RHS, z] = rhs
+        grid_ref[GAIN, z] = scale * grid_ref[MOB, z]
+
+
+def first_update(
+    given_ref, sums_ref, cell_ref, well_ref, index_ref,
+    grid_ref, out_ref, yb_ref, xb_ref, xa_ref, ya_ref, known_ref, block_ref, sems,
+):
+    layers, width, lanes = grid_ref.shape[1:]
+    rows = layers * width
     count = lax.axis_size("gx") * lax.axis_size("gy")
     chunk = sums_ref.shape[0] // count
     well_rows = (chunk - 2) // 2
@@ -413,58 +431,55 @@
     known_ref[2] = base
     row, lane = places(cell_ref[...], lanes)
     well_row, well_lane = places(well_ref[...], LANES)
-    push_ref[...] = cell_scatter(slot_bhp(bhp, well_ref, index_ref), row, lane, rows, lanes)
-    for z in range(layers):
-        here = slice(z * width, (z + 1) * width)
-        diag, rhs, around = (
-            grid_ref[name, z] + side_ref[here, i * lanes : (i + 1) * lanes]
-            for i, name in enumerate((DIAG, RHS, AROUND))
-        )
-        scale = RELAXATION * inverse(diag)
-        rhs = scale * rhs
-        gain = scale * grid_ref[MOB, z]
-        current = (1.0 - RELAXATION) * grid_ref[PRESS, z] + rhs + scale * around + gain * push_ref[here, :]
-        grid_ref[SCALE, z] = scale
-        grid_ref[RHS, z] = rhs
-        grid_ref[GAIN, z] = gain
-        grid_ref[CURRENT, z] = current
-    current = grid_ref[CURRENT].reshape(rows, lanes)
-    oxa_ref[...], oxb_ref[...] = sides(
+    push = cell_scatter(slot_bhp(bhp, well_ref, index_ref), row, lane, rows, lanes)
+    current = grid_ref[CURRENT].reshape(rows, lanes) + grid_ref[GAIN].reshape(rows, lanes) * push
+    grid_ref[CURRENT] = current.reshape(layers, width, lanes)
+    xa_ref[...], xb_ref[...] = sides(
         grid_ref[CURRENT, :, width - 1, :], grid_ref[CURRENT, :, 0, :], "gx"
     )
     at_cell = cell_find(grid_ref[MOB].reshape(rows, lanes) * current, *cell_pick(row, lane, rows, lanes))
     (part,) = well_scatter([live_index(well_ref, index_ref) * at_cell], well_row, well_lane, well_rows)
+    block_ref[...] = jnp.concatenate([part] * (block_ref.shape[0] // well_rows), axis=0)
+    outgoing = repeat_out(block_ref, out_ref, sems)
     both = jnp.concatenate([half.astype(BF16) for half in halves(current)], axis=1)
     pick_row, pick_lane = iota((2 * EDGE, 2 * lanes), 0), lax.rem(iota((2 * EDGE, 2 * lanes), 1), lanes)
     rims = nt(
         ones_of(((pick_row == 0) & (pick_lane == lanes - 1)) | ((pick_row == 1) & (pick_lane == 0))), both
     )
-    pieces = rows // LANES
-    split = [
-        jnp.concatenate([rims[r : r + 1, i * LANES : (i + 1) * LANES] for i in range(pieces)], axis=0)
-        for r in range(2)
-    ]
-    height = well_rows + pieces
-    ends = lax.axis_size("gy")
-    for i in range(block_ref.shape[0] // height):
-        block_ref[i * height : i * height + well_rows, :] = part
-        block_ref[i * height + well_rows : (i + 1) * height, :] = jnp.where(
-            i % ends > my, split[0], split[1]
-        )
-    for copy in repeat_out(block_ref, out_ref, sems):
+    ya_ref[...], yb_ref[...] = sides(rims[0:1], rims[1:2], "gy")
+    for copy in outgoing:
         copy.wait()
 
 
+def inner_terms(after_ref, grid_ref, out_ref):
+    layers, width, lanes = out_ref.shape
+    for z in range(layers):
+        current = grid_ref[CURRENT, z]
+        besides = [
+            pltpu.roll(current, width - 1, 0),
+            pltpu.roll(current, 1, 0),
+            pltpu.roll(current, lanes - 1, 1),
+            pltpu.roll(current, 1, 1),
+        ]
+        around = grid_ref[COUP, z] * besides[0]
+        for i in range(1, 4):
+            around = around + grid_ref[COUP + i, z] * besides[i]
+        if z + 1 < layers:
+            around = around + grid_ref[COUP + 4, z] * grid_ref[CURRENT, z + 1]
+        if z > 0:
+            around = around + grid_ref[COUP + 5, z] * grid_ref[CURRENT, z - 1]
+        out_ref[z] = (1.0 - RELAXATION) * current + grid_ref[RHS, z] + grid_ref[SCALE, z] * around
+
+
 def last_update(
-    sums_ref, known_ref, cell_ref, well_ref, index_ref, grid_ref, bound_ref, flank_ref, xb_ref, xa_ref,
-    out_ref, bhp_ref, push_ref, side_ref,
+    sums_ref, known_ref, cell_ref, well_ref, index_ref, grid_ref, inner_ref, bound_ref, flank_ref,
+    yb_ref, xb_ref, xa_ref, ya_ref, out_ref, bhp_ref, push_ref, side_ref,
 ):
     layers, width, lanes = out_ref.shape
     rows = layers * width
     count = lax.axis_size("gx") * lax.axis_size("gy")
     height = sums_ref.shape[0] // count
     well_rows = known_ref.shape[1]
-    pieces = height - well_rows
     me = lax.axis_index(AXES)
     part = sums_ref[0:well_rows, :]
     for d in range(1, count):
@@ -479,38 +494,15 @@
     bhp_ref[...] = line[:, :owned]
     row, lane = places(cell_ref[...], lanes)
     push_ref[...] = cell_scatter(slot_bhp(bhp, well_ref, index_ref), row, lane, rows, lanes)
-    strips = []
-    for beside in (jnp.maximum(me - 1, 0), jnp.minimum(me + 1, count - 1)):
-        strips.append(
-            jnp.concatenate(
-                [sums_ref[pl.ds(beside * height + well_rows + i, 1), :] for i in range(pieces)], axis=1
-            )
-        )
-    side_ref[...] = upright([flank_ref[1:2, :] * strips[0], flank_ref[0:1, :] * strips[1]], lanes)
+    nxt, prev = sides(ya_ref[...], yb_ref[...], "gy")
+    side_ref[...] = upright([flank_ref[1:2, :] * prev, flank_ref[0:1, :] * nxt], lanes)
     along = iota((width, lanes), 1)
     nxt, prev = sides(xa_ref[...], xb_ref[...], "gx")
     for z in range(layers):
         here = slice(z * width, (z + 1) * width)
-        current = grid_ref[CURRENT, z]
         side = side_ref[here, :]
-        around = jnp.where(along == 0, side, jnp.where(along == lanes - 1, pltpu.roll(side, lanes - 2, 1), 0.0))
-        besides = [
-            pltpu.roll(current, width - 1, 0),
-            pltpu.roll(current, 1, 0),
-            pltpu.roll(current, lanes - 1, 1),
-            pltpu.roll(current, 1, 1),
-            grid_ref[CURRENT, z + 1] if z + 1 < layers else None,
-            grid_ref[CURRENT, z - 1] if z > 0 else None,
-        ]
-        for i, beside in enumerate(besides):
-            if beside is not None:
-                around = around + grid_ref[COUP + i, z] * beside
-        out_ref[z] = (
-            (1.0 - RELAXATION) * current
-            + grid_ref[RHS, z]
-            + grid_ref[GAIN, z] * push_ref[here, :]
-            + grid_ref[SCALE, z] * around
-        )
+        side = jnp.where(along == 0, side, jnp.where(along == lanes - 1, pltpu.roll(side, lanes - 2, 1), 0.0))
+        out_ref[z] = inner_ref[z] + grid_ref[GAIN, z] * push_ref[here, :] + grid_ref[SCALE, z] * side
     for where, edge, beyond in ((0, width - 1, nxt), (1, 0, prev)):
         out_ref[:, edge, :] = out_ref[:, edge, :] + grid_ref[SCALE, :, edge, :] * (bound_ref[where] * beyond)
 
@@ -613,30 +605,33 @@
         None,
         {0: 0},
     )
-    chunk = well_rows + rows // LANES
-    height = whole_tiles(chunk, lax.axis_size("gy"), count)
-    given, sums, xb, xa, known, bound, flank = call(
+    given, bound, flank = call(
+        outer_terms,
+        [(GRIDS,) + grid, (2, layers, lanes), (EDGE, rows)],
+        [given] + rims,
+        [(rows, 3 * lanes)],
+        aliases={0: 0},
+    )
+    height = whole_tiles(well_rows, min(8, count), count)
+    given, sums, yb, xb, xa, ya, known = call(
         first_update,
         [
-            (GRIDS,) + grid, (count * chunk, LANES), (layers, lanes), (layers, lanes), (3, well_rows, LANES),
-            (2, layers, lanes), (EDGE, rows),
+            (GRIDS,) + grid, (count * well_rows, LANES), (1, rows), (layers, lanes), (layers, lanes), (1, rows),
+            (3, well_rows, LANES),
         ],
-        [given, gathered] + slots + rims,
-        [
-            (rows, 3 * lanes), (rows, lanes), (height, LANES),
-            pltpu.SemaphoreType.DMA((count * chunk // height,)),
-        ],
+        [given, gathered] + slots,
+        [(height, LANES), pltpu.SemaphoreType.DMA((count * well_rows // height,))],
         None,
         [pltpu.VMEM, pltpu.HBM] + [pltpu.VMEM] * 5,
         {0: 0},
     )
     gathered = everyone(sums, count)
-    xb = to_other(xb, "gx")
-    xa = to_pair(xa, "gx")
+    rims = [to_other(yb, "gy"), to_other(xb, "gx"), to_pair(xa, "gx"), to_pair(ya, "gy")]
+    (inner,) = call(inner_terms, [grid], [sums, given], (), [pl.ANY, pltpu.VMEM])
     out, bhp = call(
         last_update,
         [grid, (1, owned)],
-        [gathered, known] + slots + [given, bound, flank, xb, xa],
+        [gathered, known] + slots + [given, inner, bound, flank] + rims,
         [(rows, lanes), (rows, lanes)],
     )
     return out, bhp[0]

time: 38.1 us -> 37.2 us (0.976)
  waiting for transfers between devices: 10.2 us -> 7.28 us
  starting transfers between devices: 18 us -> 19.8 us
    all_to_all x2, waiting for transfers between devices: 8.07 us -> 5.07 us  [everyone(): lax.all_to_all(rows.reshape(count, height, 1, LANES), AXES, 0, 0, tiled=T...]
    ppermute x3 -> x4, waiting for transfers between devices: 0.38 us -> 2.2 us  [to_other(): return lax.ppermute(block, AXES, moves)]
    ppermute x3 -> x4, waiting for transfers between devices: 1.73 us -> 0.01 us  [to_pair(): return lax.ppermute(block, axis, [(i, i ^ 1) for i in range(count)])]
    ppermute x3 -> x4, starting transfers between devices: 7.52 us -> 9.06 us  [to_pair(): return lax.ppermute(block, axis, [(i, i ^ 1) for i in range(count)])]
    pallas_call x4 -> x6, Pallas kernels: 8.84 us -> 9.12 us  [call(): pl.pallas_call(kernel, out_shape=shapes, in_specs=[pl.BlockSpec(memory_sp...]
  transfers between devices with their start and end apart: 8 -> 10, of which waited for: 4 -> 4; matrix products, arithmetic and copies ran while one was open for 0% -> 0% of each run, Pallas kernels for 5% -> 7%
where the time goes in v5:
time: 37.2 us; the launch traced here: 37 us
  starting transfers between devices  19.8 us (53%)
  Pallas kernels  9.12 us (25%)
  waiting for transfers between devices  7.28 us (20%)
  between operations  0.73 us (2%)
    all_to_all x2, starting transfers between devices, everyone(): lax.all_to_all(rows.reshape(count, height, 1, LANES), AXES, 0, 0, tiled=T...  10.1 us
    pallas_call x6, Pallas kernels, call(): pl.pallas_call(kernel, out_shape=shapes, in_specs=[pl.BlockSpec(memory_sp...  9.12 us
    ppermute x4, starting transfers between devices, to_pair(): return lax.ppermute(block, axis, [(i, i ^ 1) for i in range(count)])  9.06 us
    all_to_all x2, waiting for transfers between devices, everyone(): lax.all_to_all(rows.reshape(count, height, 1, LANES), AXES, 0, 0, tiled=T...  5.07 us
    ppermute x4, waiting for transfers between devices, to_other(): return lax.ppermute(block, AXES, moves)  2.2 us
  transfers between devices with their start and end apart: 10, of which 4 were waited for; matrix products, arithmetic and copies ran while one was open for 0% of the time, Pallas kernels for 7%

profile of v5, /device:TPU:0, one launch (start us, length us, event | category | flops | bytes accessed | tf_op | source)
XLA Modules:
  0.0 37.0 jit_solution(16346092121199539233)
XLA Ops:
  0.6 0.0 copy-start.2
  0.6 0.0 copy-start.1
  0.7 0.0 copy-start
  0.7 3.0 %shard_map.131 = (f32[576,128]{1,0:T(8,128)}, f32[8,384]{1,0:T(8,128)S(1)}, f32[72,128]{1,0:T(8,128)S(1)}, f32[72,128]{1,0:T(8,128)S(1)}, f32[8,384]{1,0:T(8,128...) custom-call(s32[1,1024]{1,0:T(1,128)} %cell_ref.5, s32[1,1024]{1,0:T(1,128)} %well_ref.5, ...), custom_call_target="tpu_custom_call" | custom-call | flops 1000000 | bytes 4000000 | tf_op jit(solution)/shard_map/pallas_call | solution.py:518
  3.7 7.3 %all-to-all-start = ((f32[32,18,1,128]{3,2,1,0:T(1,128)}), f32[32,18,1,128]{3,2,1,0:T(1,128)S(1)}, u32[]{:S(2)}, u32[]{:S(2)}) async-start(f32[32,18,1,128]{3,2,1,0:T(1,128)} %bitcast.2), calls=%async_computation | async-start | bytes 589824 | tf_op jit(solution)/shard_map/all_to_all | solution.py:540
  11.0 0.3 collective-permute-start.1
  11.3 3.0 %collective-permute-start.2 = (f32[72,128]{1,0:T(8,128)S(1)}, f32[72,128]{1,0:T(8,128)S(1)}, u32[]{:S(2)}, u32[]{:S(2)}) collective-permute-start(f32[72,128]{1,0:T(8,128)S(1)} %get-tuple-element.26.own_xa_ref), channel_id=1, source_target_pairs={{0,4},{4,0},{8,12},{12,8},{16,20},{20,16},{24,28},{28,24},{1,5},{5... | collective-permute-start | bytes 110600 | tf_op jit(solution)/shard_map/ppermute | solution.py:547
  14.3 0.0 collective-permute-start
  14.4 1.5 %collective-permute-start.3 = (f32[8,384]{1,0:T(8,128)S(1)}, f32[8,384]{1,0:T(8,128)S(1)}, u32[]{:S(2)}, u32[]{:S(2)}) collective-permute-start(f32[8,384]{1,0:T(8,128)S(1)} %get-tuple-element.27.own_ya_ref), channel_id=1, source_target_pairs={{0,1},{1,0},{2,3},{3,2},{4,5},{5,4},{6,7},{7,6},{8,9},{9,8},{10,11... | collective-permute-start | bytes 36872 | tf_op jit(solution)/shard_map/ppermute | solution.py:547
  15.9 0.0 copy-done.2
  15.9 0.0 copy-done.1
  15.9 0.0 copy-done
  15.9 1.8 %shard_map.132.given_ref = f32[11,12,32,128]{3,2,1,0:T(8,128)S(1)} custom-call(f32[11,12,32,128]{3,2,1,0:T(8,128)S(1)} %get-tuple-element.21.given_ref, f32[576,128]{1,0:T(8,128)} %get-tuple-element.22.after_ref, s32[12,32,128]{2,1,0:T(8,128)S(1)} %get-tuple-element.23.flag_ref, s32[1,1024]{1,0:T(1,128)S(1)} %copy-done, ...), custom_call_target="tpu_custom_call", output_to_operand_aliasing={{}: (0, {})} | custom-call | flops 1000000 | bytes 4000000 | tf_op jit(solution)/shard_map/pallas_call | solution.py:518
  17.7 0.4 %collective-permute-done.yb_ref = f32[8,384]{1,0:T(8,128)S(1)} collective-permute-done((f32[8,384]{1,0:T(8,128)S(1)}, f32[8,384]{1,0:T(8,128)S(1)}, u32[]{:S(2)}, u32[]{:S(2)}) %collective-permute-start) | collective-permute-done | bytes 12320 | tf_op jit(solution)/shard_map/ppermute | solution.py:563
  18.1 0.0 collective-permute-done.3.ya_ref
  18.1 0.0 collective-permute-done.1.xb_ref
  18.1 0.0 collective-permute-done.2.xa_ref
  18.1 0.5 %shard_map.133 = (f32[11,12,32,128]{3,2,1,0:T(8,128)S(1)}, f32[2,12,128]{2,1,0:T(8,128)S(1)}, f32[8,384]{1,0:T(8,128)S(1)}) custom-call(f32[11,12,32,128]{3,2,1,0:T(8,128)S(1)} %shard_map.132.given_ref, f32[8,384]{1,0:T(8,128)S(1)} %get-tuple-element.24.own_yb_ref, f32[72,128]{1,0:T(8,128)S(1)} %get-tuple-element.25.own_xb_ref, ...), custom_call_target="tpu_custom_call", output_to_operand_aliasing={{0}: (0, {})} | custom-call | flops 1000000 | bytes 4000000 | tf_op jit(solution)/shard_map/pallas_call | solution.py:518
  18.7 3.7 %all-to-all-done = f32[32,18,1,128]{3,2,1,0:T(1,128)S(1)} async-done(((f32[32,18,1,128]{3,2,1,0:T(1,128)}), f32[32,18,1,128]{3,2,1,0:T(1,128)S(1)}, u32[]{:S(2)}, u32[]{:S(2)}) %all-to-all-start) | async-done | bytes 294944 | tf_op jit(solution)/shard_map/all_to_all | solution.py:540
  22.4 2.2 %shard_map.134 = (f32[11,12,32,128]{3,2,1,0:T(8,128)S(1)}, f32[256,128]{1,0:T(8,128)}, f32[1,384]{1,0:T(1,128)S(1)}, f32[12,128]{1,0:T(8,128)S(1)}, f32[12,128]{...) custom-call(f32[11,12,32,128]{3,2,1,0:T(8,128)S(1)} %get-tuple-element.28.given_, ...), custom_call_target="tpu_custom_call", output_to_operand_aliasing={{0}: (0, {})} | custom-call | flops 1000000 | bytes 4000000 | tf_op jit(solution)/shard_map/pallas_call | solution.py:518
  24.6 2.8 %all-to-all-start.1 = ((f32[32,8,1,128]{3,1,2,0:T(8,128)}), f32[32,8,1,128]{3,1,2,0:T(8,128)S(1)}, u32[]{:S(2)}, u32[]{:S(2)}) async-start(f32[32,8,1,128]{3,1,2,0:T(8,128)} %bitcast.5), calls=%async_computation.1 | async-start | bytes 262144 | tf_op jit(solution)/shard_map/all_to_all | solution.py:540
  27.4 0.3 collective-permute-start.5
  27.7 3.0 %collective-permute-start.6 = (f32[12,128]{1,0:T(8,128)S(1)}, f32[12,128]{1,0:T(8,128)S(1)}, u32[]{:S(2)}, u32[]{:S(2)}) collective-permute-start(f32[12,128]{1,0:T(8,128)S(1)} %get-tuple-element.36), channel_id=1, source_target_pairs={{0,4},{4,0},{8,12},{12,8},{16,20},{20,16},{24,28},{28,24},{1,5},{5... | collective-permute-start | bytes 18440 | tf_op jit(solution)/shard_map/ppermute | solution.py:547
  30.7 0.0 collective-permute-start.4
  30.7 1.5 %collective-permute-start.7 = (f32[1,384]{1,0:T(1,128)S(1)}, f32[1,384]{1,0:T(1,128)S(1)}, u32[]{:S(2)}, u32[]{:S(2)}) collective-permute-start(f32[1,384]{1,0:T(1,128)S(1)} %get-tuple-element.37), channel_id=1, source_target_pairs={{0,1},{1,0},{2,3},{3,2},{4,5},{5,4},{6,7},{7,6},{8,9},{9,8},{10,11... | collective-permute-start | bytes 4616 | tf_op jit(solution)/shard_map/ppermute | solution.py:547
  32.3 0.2 shard_map.135.inner_ref
  32.4 1.8 %collective-permute-done.4.yb_ref = f32[1,384]{1,0:T(1,128)S(1)} collective-permute-done((f32[1,384]{1,0:T(1,128)S(1)}, f32[1,384]{1,0:T(1,128)S(1)}, u32[]{:S(2)}, u32[]{:S(2)}) %collective-permute-start.4) | collective-permute-done | bytes 1568 | tf_op jit(solution)/shard_map/ppermute | solution.py:563
  34.3 0.0 collective-permute-done.7.ya_ref
  34.3 0.0 collective-permute-done.5.xb_ref
  34.3 0.0 collective-permute-done.6.xa_ref
  34.3 1.3 %all-to-all-done.1 = f32[32,8,1,128]{3,1,2,0:T(8,128)S(1)} async-done(((f32[32,8,1,128]{3,1,2,0:T(8,128)}), f32[32,8,1,128]{3,1,2,0:T(8,128)S(1)}, u32[]{:S(2)}, u32[]{:S(2)}) %all-to-all-start.1) | async-done | bytes 131104 | tf_op jit(solution)/shard_map/all_to_all | solution.py:540
  35.6 1.4 %shard_map.136 = (f32[12,32,128]{2,1,0:T(8,128)}, f32[1,32]{1,0:T(1,128)}) custom-call(f32[256,128]{1,0:T(8,128)S(1)} %bitcast.10, f32[3,8,128]{2,1,0:T(8,128)S(1)} %get-tuple-element.30.known_ref, s32[1,1024]{1,0:T(1,128)S(1)} %copy-done, s32[1,1024]{1,0:T(1,128)S(1)} %copy-done.1, f32[1,1024]{1,0:T(1,128)S(1)} %copy-done.2, ...), custom_call_target="tpu_custom_call" | custom-call | flops 1000000 | bytes 4000000 | tf_op jit(solution)/shard_map/pallas_call | solution.py:518
Async XLA Ops:
  0.6 15.3 %copy-start.2 = (f32[1,1024]{1,0:T(1,128)S(1)}, f32[1,1024]{1,0:T(1,128)}, u32[]{:S(2)}) copy-start(f32[1,1024]{1,0:T(1,128)} %index_ref.5) | copy-start | bytes 12292
  0.6 15.3 %copy-start.1 = (s32[1,1024]{1,0:T(1,128)S(1)}, s32[1,1024]{1,0:T(1,128)}, u32[]{:S(2)}) copy-start(s32[1,1024]{1,0:T(1,128)} %well_ref.5) | copy-start | bytes 12292
  0.7 15.3 %copy-start = (s32[1,1024]{1,0:T(1,128)S(1)}, s32[1,1024]{1,0:T(1,128)}, u32[]{:S(2)}) copy-start(s32[1,1024]{1,0:T(1,128)} %cell_ref.5) | copy-start | bytes 12292
  3.7 18.7 %all-to-all-start = ((f32[32,18,1,128]{3,2,1,0:T(1,128)}), f32[32,18,1,128]{3,2,1,0:T(1,128)S(1)}, u32[]{:S(2)}, u32[]{:S(2)}) async-start(f32[32,18,1,128]{3,2,1,0:T(1,128)} %bitcast.2), calls=%async_computation | async-start | bytes 589824 | tf_op jit(solution)/shard_map/all_to_all | solution.py:540
  11.0 7.1 %collective-permute-start.1 = (f32[72,128]{1,0:T(8,128)S(1)}, f32[72,128]{1,0:T(8,128)S(1)}, u32[]{:S(2)}, u32[]{:S(2)}) collective-permute-start(f32[72,128]{1,0:T(8,128)S(1)} %get-tuple-element.25.own_xb_ref), channel_id=1, source_target_pairs={{0,1},{1,0},{2,3},{3,2},{4,8},{5,9},{6,10},{7,11},{8,4},{9,5},{10,... | collective-permute-start | bytes 110600 | tf_op jit(solution)/shard_map/ppermute | solution.py:563
  11.3 6.8 %collective-permute-start.2 = (f32[72,128]{1,0:T(8,128)S(1)}, f32[72,128]{1,0:T(8,128)S(1)}, u32[]{:S(2)}, u32[]{:S(2)}) collective-permute-start(f32[72,128]{1,0:T(8,128)S(1)} %get-tuple-element.26.own_xa_ref), channel_id=1, source_target_pairs={{0,4},{4,0},{8,12},{12,8},{16,20},{20,16},{24,28},{28,24},{1,5},{5... | collective-permute-start | bytes 110600 | tf_op jit(solution)/shard_map/ppermute | solution.py:547
  14.3 3.8 %collective-permute-start = (f32[8,384]{1,0:T(8,128)S(1)}, f32[8,384]{1,0:T(8,128)S(1)}, u32[]{:S(2)}, u32[]{:S(2)}) collective-permute-start(f32[8,384]{1,0:T(8,128)S(1)} %get-tuple-element.24.own_yb_ref), channel_id=1, source_target_pairs={{0,4},{1,2},{2,1},{3,7},{4,0},{5,6},{6,5},{7,3},{8,12},{9,10},{10,... | collective-permute-start | bytes 36872 | tf_op jit(solution)/shard_map/ppermute | solution.py:563
  14.4 3.8 %collective-permute-start.3 = (f32[8,384]{1,0:T(8,128)S(1)}, f32[8,384]{1,0:T(8,128)S(1)}, u32[]{:S(2)}, u32[]{:S(2)}) collective-permute-start(f32[8,384]{1,0:T(8,128)S(1)} %get-tuple-element.27.own_ya_ref), channel_id=1, source_target_pairs={{0,1},{1,0},{2,3},{3,2},{4,5},{5,4},{6,7},{7,6},{8,9},{9,8},{10,11... | collective-permute-start | bytes 36872 | tf_op jit(solution)/shard_map/ppermute | solution.py:547
  24.6 11.0 %all-to-all-start.1 = ((f32[32,8,1,128]{3,1,2,0:T(8,128)}), f32[32,8,1,128]{3,1,2,0:T(8,128)S(1)}, u32[]{:S(2)}, u32[]{:S(2)}) async-start(f32[32,8,1,128]{3,1,2,0:T(8,128)} %bitcast.5), calls=%async_computation.1 | async-start | bytes 262144 | tf_op jit(solution)/shard_map/all_to_all | solution.py:540
  27.4 6.9 %collective-permute-start.5 = (f32[12,128]{1,0:T(8,128)S(1)}, f32[12,128]{1,0:T(8,128)S(1)}, u32[]{:S(2)}, u32[]{:S(2)}) collective-permute-start(f32[12,128]{1,0:T(8,128)S(1)} %get-tuple-element.35), channel_id=1, source_target_pairs={{0,1},{1,0},{2,3},{3,2},{4,8},{5,9},{6,10},{7,11},{8,4},{9,5},{10,... | collective-permute-start | bytes 18440 | tf_op jit(solution)/shard_map/ppermute | solution.py:563
  27.7 6.6 %collective-permute-start.6 = (f32[12,128]{1,0:T(8,128)S(1)}, f32[12,128]{1,0:T(8,128)S(1)}, u32[]{:S(2)}, u32[]{:S(2)}) collective-permute-start(f32[12,128]{1,0:T(8,128)S(1)} %get-tuple-element.36), channel_id=1, source_target_pairs={{0,4},{4,0},{8,12},{12,8},{16,20},{20,16},{24,28},{28,24},{1,5},{5... | collective-permute-start | bytes 18440 | tf_op jit(solution)/shard_map/ppermute | solution.py:547
  30.7 3.6 %collective-permute-start.4 = (f32[1,384]{1,0:T(1,128)S(1)}, f32[1,384]{1,0:T(1,128)S(1)}, u32[]{:S(2)}, u32[]{:S(2)}) collective-permute-start(f32[1,384]{1,0:T(1,128)S(1)} %get-tuple-element.34), channel_id=1, source_target_pairs={{0,4},{1,2},{2,1},{3,7},{4,0},{5,6},{6,5},{7,3},{8,12},{9,10},{10,... | collective-permute-start | bytes 4616 | tf_op jit(solution)/shard_map/ppermute | solution.py:563
  30.7 3.6 %collective-permute-start.7 = (f32[1,384]{1,0:T(1,128)S(1)}, f32[1,384]{1,0:T(1,128)S(1)}, u32[]{:S(2)}, u32[]{:S(2)}) collective-permute-start(f32[1,384]{1,0:T(1,128)S(1)} %get-tuple-element.37), channel_id=1, source_target_pairs={{0,1},{1,0},{2,3},{3,2},{4,5},{5,4},{6,7},{7,6},{8,9},{9,8},{10,11... | collective-permute-start | bytes 4616 | tf_op jit(solution)/shard_map/ppermute | solution.py:547

commit v6 on v5

--- a/solution.py
+++ b/solution.py
@@ -13,7 +13,7 @@
 RELAXATION = 0.8
 LANES = 128
 PLANES = 6
-INPUTS = 12
+INPUTS = 10
 PRESS, SAT, PERM, DEPTH, PORE, RES, GRIDS = 0, 1, 3, 6, 7, 8, 11
 DIAG, RHS, COUP, MOB, AROUND = 1, 2, 3, 9, 10
 CURRENT, SCALE, GAIN = 0, 1, 10
@@ -63,9 +63,16 @@
     return jnp.concatenate([pick, pick], axis=0), hot(row, rows)
 
 
-def cell_find(field, pick, at_row):
-    both = jnp.concatenate([part.astype(BF16) for part in halves(field)], axis=1)
-    return jnp.sum(jnp.where(at_row, nn(both, pick), 0.0), axis=0, keepdims=True)
+def cell_find(fields, pick, at_row):
+    rows = at_row.shape[0]
+    both = [
+        jnp.concatenate([part.astype(BF16) for part in halves(field)], axis=1) for field in fields
+    ]
+    found = nn(jnp.concatenate(both, axis=0), pick)
+    return [
+        jnp.sum(jnp.where(at_row, found[i * rows : (i + 1) * rows], 0.0), axis=0, keepdims=True)
+        for i in range(len(fields))
+    ]
 
 
 def cell_scatter(value, row, lane, rows, lanes):
@@ -137,53 +144,68 @@
     return copies
 
 
-def first_rows(out_ref):
-    count = lax.axis_size("gx") * lax.axis_size("gy")
-    return out_ref.shape[0] // count
-
-
 def is_even(axis):
     return lax.rem(lax.axis_index(axis), 2) == 0
 
 
 def opening(*refs):
-    inputs, sems, out_sems = refs[:INPUTS], refs[-2], refs[-1]
-    sums_ref, yb_ref, xb_ref, xa_ref, ya_ref, grid_ref, flag_ref = refs[INPUTS : INPUTS + 7]
-    cell_ref, well_ref, index_ref, mode_ref, target_ref, block_ref, lying_ref = refs[INPUTS + 7 : -2]
-    slot_refs = [cell_ref, well_ref, index_ref, mode_ref, target_ref]
-    sat_ref, perm_ref = grid_ref.at[SAT : SAT + 2], grid_ref.at[PERM : PERM + 3]
-    holds = slot_refs + [
-        sat_ref, grid_ref.at[PRESS], perm_ref, grid_ref.at[DEPTH], flag_ref,
-        grid_ref.at[PORE], grid_ref.at[RES : RES + 3],
+    inputs, sems = refs[:INPUTS], refs[-1]
+    keep_ref, give_ref, grid_ref, flag_ref = refs[INPUTS : INPUTS + 4]
+    cell_ref, well_ref, index_ref = slot_refs = refs[INPUTS + 4 : -1]
+    holds = list(slot_refs) + [
+        grid_ref.at[SAT : SAT + 2], grid_ref.at[PRESS], grid_ref.at[PERM : PERM + 3], grid_ref.at[DEPTH],
+        flag_ref, grid_ref.at[PORE], grid_ref.at[RES : RES + 3],
     ]
     copies = fetch(inputs, holds, sems)
     layers, width, lanes = flag_ref.shape
     rows = layers * width
-    owned = mode_ref.shape[1]
-    group = LANES // owned
-    me = lax.axis_index(AXES)
+    well_rows = keep_ref.shape[0]
     for copy in copies[: len(slot_refs)]:
         copy.wait()
     row, lane = places(cell_ref[...], lanes)
     well_row, well_lane = places(well_ref[...], LANES)
     pick, at_row = cell_pick(row, lane, rows, lanes)
     index = live_index(well_ref, index_ref)
-    chunk_rows = first_rows(sums_ref)
-    here = lax.shift_right_logical(iota((1, LANES), 1), bits_of(owned)) == lax.rem(me, group)
+    later = copies[len(slot_refs) :]
+    later[0].wait()
+    mobility = total_mobility(grid_ref[SAT].reshape(rows, lanes), grid_ref[SAT + 1].reshape(rows, lanes))
+    later[1].wait()
+    press = grid_ref[PRESS].reshape(rows, lanes)
+    at_mob, at_press = cell_find([mobility, mobility * press], pick, at_row)
+    part, base = well_scatter([index * at_press, index * at_mob], well_row, well_lane, well_rows)
+    half = well_rows // 2
+    keep_ref[...], give_ref[...] = sides(
+        jnp.concatenate([part[:half], base[:half]], axis=0),
+        jnp.concatenate([part[half:], base[half:]], axis=0),
+        "gy",
+    )
+    for copy in later[2:]:
+        copy.wait()
+
+
+def sides(a, b, axis):
+    even = is_even(axis)
+    return jnp.where(even, a, b), jnp.where(even, b, a)
+
+
+def pair_sums(
+    keep_ref, given_ref, mode_ref, target_ref, grid_ref, flag_ref,
+    out_ref, yb_ref, xb_ref, xa_ref, ya_ref, lying_ref, block_ref, sems,
+):
+    owned = mode_ref.shape[1]
+    group = LANES // owned
+    here = lax.shift_right_logical(iota((1, LANES), 1), bits_of(owned)) == lax.rem(
+        lax.axis_index(AXES), group
+    )
     controls = [
         jnp.where(here, jnp.concatenate([ref[...].astype(F32)] * group, axis=1), 0.0)
         for ref in (mode_ref, target_ref)
     ]
-    later = copies[len(slot_refs) :]
-    later[0].wait()
-    mobility = total_mobility(grid_ref[SAT].reshape(rows, lanes), grid_ref[SAT + 1].reshape(rows, lanes))
-    at_mob = cell_find(mobility, pick, at_row)
-    later[1].wait()
-    at_press = cell_find(mobility * grid_ref[PRESS].reshape(rows, lanes), pick, at_row)
-    sums = well_scatter([index * at_press, index * at_mob], well_row, well_lane, (chunk_rows - 2) // 2)
-    block = jnp.concatenate(sums + controls, axis=0)
-    block_ref[...] = jnp.concatenate([block] * (block_ref.shape[0] // chunk_rows), axis=0)
-    outgoing = repeat_out(block_ref, sums_ref, out_sems)
+    block = jnp.concatenate([keep_ref[...] + given_ref[...]] + controls, axis=0)
+    block_ref[...] = jnp.concatenate([block] * (block_ref.shape[0] // block.shape[0]), axis=0)
+    copies = repeat_out(block_ref, out_ref, sems)
+    layers, width, lanes = flag_ref.shape
+    rows = layers * width
     pair = lax.shift_right_logical(iota((rows, lanes), 1), 1)
 
     def rim(total, i, plane):
@@ -191,11 +213,8 @@
 
     total = rim(jnp.zeros((rows, lanes), F32), 0, grid_ref[PRESS])
     total = rim(rim(total, 1, grid_ref[SAT]), 2, grid_ref[SAT + 1])
-    later[2].wait()
     total = rim(total, 3, grid_ref[PERM + 1])
-    later[3].wait()
     total = rim(total, 4, grid_ref[DEPTH])
-    later[4].wait()
     bit_y = lax.bitwise_and(lax.shift_right_logical(flag_ref[...], 1), 1).astype(F32)
     total = rim(total, PLANES - 1, bit_y)
     pieces = [
@@ -226,7 +245,7 @@
     for i, (high, low) in enumerate(zip(*ends)):
         xa_ref[i * layers : (i + 1) * layers, :] = jnp.where(x_even, high, low)
         xb_ref[i * layers : (i + 1) * layers, :] = jnp.where(x_even, low, high)
-    for copy in later[5:] + outgoing:
+    for copy in copies:
         copy.wait()
 
 
@@ -337,11 +356,6 @@
     return live_index(well_ref, index_ref) * well_gather(bhp, well_row, well_lane)
 
 
-def sides(a, b, axis):
-    even = is_even(axis)
-    return jnp.where(even, a, b), jnp.where(even, b, a)
-
-
 def close_ends(nxt, prev, axis):
     me = lax.axis_index(axis)
     nxt[3] = jnp.where(me < lax.axis_size(axis) - 1, nxt[3], 0.0)
@@ -410,16 +424,17 @@
     rows = layers * width
     count = lax.axis_size("gx") * lax.axis_size("gy")
     chunk = sums_ref.shape[0] // count
-    well_rows = (chunk - 2) // 2
+    well_rows = chunk - 2
+    half = well_rows // 2
     group = count // well_rows
-    my = lax.axis_index("gy")
-    part = sums_ref[0:well_rows, :]
-    base = sums_ref[well_rows : 2 * well_rows, :]
-    for d in range(1, count):
-        part = part + sums_ref[d * chunk : d * chunk + well_rows, :]
-        base = base + sums_ref[d * chunk + well_rows : d * chunk + 2 * well_rows, :]
+    low, high = sums_ref[0:well_rows, :], sums_ref[chunk : chunk + well_rows, :]
+    for d in range(2, count, 2):
+        low = low + sums_ref[d * chunk : d * chunk + well_rows, :]
+        high = high + sums_ref[(d + 1) * chunk : (d + 1) * chunk + well_rows, :]
+    part = jnp.concatenate([low[:half], high[:half]], axis=0)
+    base = jnp.concatenate([low[half:], high[half:]], axis=0)
     controls = []
-    for k in (2 * well_rows, 2 * well_rows + 1):
+    for k in (well_rows, well_rows + 1):
         total = sums_ref[pl.ds(k, well_rows, stride=group * chunk), :]
         for j in range(1, group):
             total = total + sums_ref[pl.ds(j * chunk + k, well_rows, stride=group * chunk), :]
@@ -437,7 +452,8 @@
     xa_ref[...], xb_ref[...] = sides(
         grid_ref[CURRENT, :, width - 1, :], grid_ref[CURRENT, :, 0, :], "gx"
     )
-    at_cell = cell_find(grid_ref[MOB].reshape(rows, lanes) * current, *cell_pick(row, lane, rows, lanes))
+    mobile = grid_ref[MOB].reshape(rows, lanes) * current
+    (at_cell,) = cell_find([mobile], *cell_pick(row, lane, rows, lanes))
     (part,) = well_scatter([live_index(well_ref, index_ref) * at_cell], well_row, well_lane, well_rows)
     block_ref[...] = jnp.concatenate([part] * (block_ref.shape[0] // well_rows), axis=0)
     outgoing = repeat_out(block_ref, out_ref, sems)
@@ -572,26 +588,35 @@
     count = lax.axis_size("gx") * lax.axis_size("gy")
     owned = well_mode.shape[0]
     well_rows = owned * count // LANES
-    chunk = 2 * well_rows + 2
+    chunk = well_rows + 2
     grid = (layers, width, lanes)
     slots = [perf_cell, perf_well, perf_index]
     operands = slots + [
-        well_mode[None], well_target[None], saturation, pressure, permeability, cell_depth,
-        upstream_flags, pore_volume, residual,
-    ]
-    height = whole_tiles(chunk, 1, count)
-    sums, yb, xb, xa, ya, given, flags = call(
+        saturation, pressure, permeability, cell_depth, upstream_flags, pore_volume, residual
+    ]
+    keep, give, given, flags = call(
         opening,
         [
-            (count * chunk, LANES), (EDGE, rows), (PLANES * layers, lanes), (PLANES * layers, lanes),
-            (EDGE, rows), (GRIDS,) + grid, jax.ShapeDtypeStruct(grid, upstream_flags.dtype),
+            (well_rows, LANES), (well_rows, LANES), (GRIDS,) + grid,
+            jax.ShapeDtypeStruct(grid, upstream_flags.dtype),
         ],
         operands,
-        [pltpu.VMEM(a.shape, a.dtype) for a in operands[:5]]
-        + [(height, LANES), (2 * EDGE * (rows // LANES), LANES), pltpu.SemaphoreType.DMA((INPUTS,))]
-        + [pltpu.SemaphoreType.DMA((count * chunk // height,))],
+        [pltpu.VMEM(a.shape, a.dtype) for a in slots] + [pltpu.SemaphoreType.DMA((INPUTS,))],
         [pltpu.HBM] * INPUTS,
-        [pltpu.HBM] + [pltpu.VMEM] * 6,
+    )
+    height = whole_tiles(chunk, 1, count)
+    sums, yb, xb, xa, ya = call(
+        pair_sums,
+        [
+            (count * chunk, LANES), (EDGE, rows), (PLANES * layers, lanes), (PLANES * layers, lanes), (EDGE, rows),
+        ],
+        [keep, to_pair(give, "gy"), well_mode[None], well_target[None], given, flags],
+        [
+            (2 * EDGE * (rows // LANES), LANES), (height, LANES),
+            pltpu.SemaphoreType.DMA((count * chunk // height,)),
+        ],
+        None,
+        [pltpu.HBM] + [pltpu.VMEM] * 4,
     )
     rims = [yb, xb, xa, ya]
     rims = rims + [to_other(yb, "gy"), to_other(xb, "gx"), to_pair(xa, "gx"), to_pair(ya, "gy")]
@@ -612,7 +637,7 @@
         [(rows, 3 * lanes)],
         aliases={0: 0},
     )
-    height = whole_tiles(well_rows, min(8, count), count)
+    height = whole_tiles(well_rows, count, count)
     given, sums, yb, xb, xa, ya, known = call(
         first_update,
         [

time: 37.2 us -> 36.1 us (0.970)
  waiting for transfers between devices: 7.28 us -> 5.28 us
  starting transfers between devices: 19.8 us -> 20.6 us
    all_to_all x2, waiting for transfers between devices: 5.07 us -> 2.34 us  [everyone(): lax.all_to_all(rows.reshape(count, height, 1, LANES), AXES, 0, 0, tiled=T...]
    ppermute x4 -> x5, waiting for transfers between devices: 0.01 us -> 0.83 us  [to_pair(): return lax.ppermute(block, axis, [(i, i ^ 1) for i in range(count)])]
    ppermute x4 -> x5, starting transfers between devices: 9.06 us -> 9.57 us  [to_pair(): return lax.ppermute(block, axis, [(i, i ^ 1) for i in range(count)])]
    pallas_call x6 -> x7, Pallas kernels: 9.12 us -> 9.24 us  [call(): pl.pallas_call(kernel, out_shape=shapes, in_specs=[pl.BlockSpec(memory_sp...]
  transfers between devices with their start and end apart: 10 -> 11, of which waited for: 4 -> 5; matrix products, arithmetic and copies ran while one was open for 0% -> 0% of each run, Pallas kernels for 7% -> 7%
where the time goes in v6:
time: 36.1 us; the launch traced here: 35.9 us
  starting transfers between devices  20.6 us (57%)
  Pallas kernels  9.24 us (26%)
  waiting for transfers between devices  5.28 us (15%)
  between operations  0.75 us (2%)
    all_to_all x2, starting transfers between devices, everyone(): lax.all_to_all(rows.reshape(count, height, 1, LANES), AXES, 0, 0, tiled=T...  10.3 us
    ppermute x5, starting transfers between devices, to_pair(): return lax.ppermute(block, axis, [(i, i ^ 1) for i in range(count)])  9.57 us
    pallas_call x7, Pallas kernels, call(): pl.pallas_call(kernel, out_shape=shapes, in_specs=[pl.BlockSpec(memory_sp...  9.24 us
    all_to_all x2, waiting for transfers between devices, everyone(): lax.all_to_all(rows.reshape(count, height, 1, LANES), AXES, 0, 0, tiled=T...  2.34 us
    ppermute x4, waiting for transfers between devices, to_other(): return lax.ppermute(block, AXES, moves)  2.1 us
    ppermute x5, waiting for transfers between devices, to_pair(): return lax.ppermute(block, axis, [(i, i ^ 1) for i in range(count)])  0.83 us
  transfers between devices with their start and end apart: 11, of which 5 were waited for; matrix products, arithmetic and copies ran while one was open for 0% of the time, Pallas kernels for 7%

profile of v6, /device:TPU:0, one launch (start us, length us, event | category | flops | bytes accessed | tf_op | source)
XLA Modules:
  0.0 35.9 jit_solution(7907348785551740347)
XLA Ops:
  0.6 0.0 copy-start.2
  0.6 0.0 copy-start.1
  0.7 0.0 copy-start
  0.7 0.0 copy-start.4
  0.7 0.0 copy-start.3
  0.7 2.2 %shard_map.131 = (f32[8,128]{1,0:T(8,128)S(1)}, f32[8,128]{1,0:T(8,128)S(1)}, f32[11,12,32,128]{3,2,1,0:T(8,128)S(1)}, s32[12,32,128]{2,1,0:T(8,128)S(1)}) custom-call(s32[1,1024]{1,0:T(1,128)} %cell_ref.5, s32[1,1024]{1,0:T(1,128)} %well_ref.5, f32[1,1024]{1,0:T(1,128)} %index_ref.5, f32[2,12,32,128]{3,2,1,0:T(8,128)} %refs_3_.1, f32[12,32,128]{2,1,0:T(8,128)} %refs_4_.1, ...), custom_call_target="tpu_custom_call" | custom-call | flops 1000000 | bytes 4000000 | tf_op jit(solution)/shard_map/pallas_call | solution.py:534
  2.8 0.5 %collective-permute-start = (f32[8,128]{1,0:T(8,128)S(1)}, f32[8,128]{1,0:T(8,128)S(1)}, u32[]{:S(2)}, u32[]{:S(2)}) collective-permute-start(f32[8,128]{1,0:T(8,128)S(1)} %get-tuple-element.25), channel_id=1, source_target_pairs={{0,1},{1,0},{2,3},{3,2},{4,5},{5,4},{6,7},{7,6},{8,9},{9,8},{10,11... | collective-permute-start | bytes 12296 | tf_op jit(solution)/shard_map/ppermute | solution.py:563
  3.4 0.8 %collective-permute-done.given_ref = f32[8,128]{1,0:T(8,128)S(1)} collective-permute-done((f32[8,128]{1,0:T(8,128)S(1)}, f32[8,128]{1,0:T(8,128)S(1)}, u32[]{:S(2)}, u32[]{:S(2)}) %collective-permute-start) | collective-permute-done | bytes 4128 | tf_op jit(solution)/shard_map/ppermute | solution.py:563
  4.2 0.0 copy-done.4
  4.2 0.0 copy-done.3
  4.2 1.0 %shard_map.132 = (f32[320,128]{1,0:T(8,128)}, f32[8,384]{1,0:T(8,128)S(1)}, f32[72,128]{1,0:T(8,128)S(1)}, f32[72,128]{1,0:T(8,128)S(1)}, f32[8,384]{1,0:T(8,128)S(1)}) custom-call(f32[8,128]{1,0:T(8,128)S(1)} %get-tuple-element.24.keep_ref, f32[8,128]{1,0:T(8,128)S(1)} %collective-permute-done.given_ref, s32[1,32]{1,0:T(1,128)S(1)} %bitcast.11, ...), custom_call_target="tpu_custom_call" | custom-call | flops 1000000 | bytes 4000000 | tf_op jit(solution)/shard_map/pallas_call | solution.py:534
  5.2 7.2 %all-to-all-start = ((f32[32,10,1,128]{3,2,1,0:T(1,128)}), f32[32,10,1,128]{3,2,1,0:T(1,128)S(1)}, u32[]{:S(2)}, u32[]{:S(2)}) async-start(f32[32,10,1,128]{3,2,1,0:T(1,128)} %bitcast.2), calls=%async_computation | async-start | bytes 327680 | tf_op jit(solution)/shard_map/all_to_all | solution.py:556
  12.4 0.3 collective-permute-start.2
  12.8 3.0 %collective-permute-start.3 = (f32[72,128]{1,0:T(8,128)S(1)}, f32[72,128]{1,0:T(8,128)S(1)}, u32[]{:S(2)}, u32[]{:S(2)}) collective-permute-start(f32[72,128]{1,0:T(8,128)S(1)} %get-tuple-element.30.own_xa_ref), channel_id=1, source_target_pairs={{0,4},{4,0},{8,12},{12,8},{16,20},{20,16},{24,28},{28,24},{1,5},{5... | collective-permute-start | bytes 110600 | tf_op jit(solution)/shard_map/ppermute | solution.py:563
  15.7 0.0 collective-permute-start.1
  15.8 1.5 %collective-permute-start.4 = (f32[8,384]{1,0:T(8,128)S(1)}, f32[8,384]{1,0:T(8,128)S(1)}, u32[]{:S(2)}, u32[]{:S(2)}) collective-permute-start(f32[8,384]{1,0:T(8,128)S(1)} %get-tuple-element.31.own_ya_ref), channel_id=1, source_target_pairs={{0,1},{1,0},{2,3},{3,2},{4,5},{5,4},{6,7},{7,6},{8,9},{9,8},{10,11... | collective-permute-start | bytes 36872 | tf_op jit(solution)/shard_map/ppermute | solution.py:563
  17.3 0.0 copy-done.2
  17.3 0.0 copy-done.1
  17.3 0.0 copy-done
  17.3 1.8 %shard_map.133.given_ref = f32[11,12,32,128]{3,2,1,0:T(8,128)S(1)} custom-call(f32[11,12,32,128]{3,2,1,0:T(8,128)S(1)} %get-tuple-element.23.grid_ref.given_ref, f32[320,128]{1,0:T(8,128)} %get-tuple-element.27.after_ref, s32[12,32,128]{2,1,0:T(8,128)S(1)} %get-tuple-element.26.flag_ref, s32[1,1024]{1,0:T(1,128)S(1)} %copy-done, ...), custom_call_target="tpu_custom_call", output_to_operand_aliasing={{}: (0, {})} | custom-call | flops 1000000 | bytes 4000000 | tf_op jit(solution)/shard_map/pallas_call | solution.py:534
  19.2 0.3 collective-permute-done.1.yb_ref
  19.4 0.0 collective-permute-done.4.ya_ref
  19.4 0.0 collective-permute-done.2.xb_ref
  19.4 0.0 collective-permute-done.3.xa_ref
  19.4 0.5 %shard_map.134 = (f32[11,12,32,128]{3,2,1,0:T(8,128)S(1)}, f32[2,12,128]{2,1,0:T(8,128)S(1)}, f32[8,384]{1,0:T(8,128)S(1)}) custom-call(f32[11,12,32,128]{3,2,1,0:T(8,128)S(1)} %shard_map.133.given_ref, f32[8,384]{1,0:T(8,128)S(1)} %get-tuple-element.28.own_yb_ref, f32[72,128]{1,0:T(8,128)S(1)} %get-tuple-element.29.own_xb_ref, ...), custom_call_target="tpu_custom_call", output_to_operand_aliasing={{0}: (0, {})} | custom-call | flops 1000000 | bytes 4000000 | tf_op jit(solution)/shard_map/pallas_call | solution.py:534
  20.0 1.0 %all-to-all-done = f32[32,10,1,128]{3,2,1,0:T(1,128)S(1)} async-done(((f32[32,10,1,128]{3,2,1,0:T(1,128)}), f32[32,10,1,128]{3,2,1,0:T(1,128)S(1)}, u32[]{:S(2)}, u32[]{:S(2)}) %all-to-all-start) | async-done | bytes 163872 | tf_op jit(solution)/shard_map/all_to_all | solution.py:556
  21.0 2.1 %shard_map.135 = (f32[11,12,32,128]{3,2,1,0:T(8,128)S(1)}, f32[256,128]{1,0:T(8,128)}, f32[1,384]{1,0:T(1,128)S(1)}, f32[12,128]{1,0:T(8,128)S(1)}, f32[12,128]{...) custom-call(f32[11,12,32,128]{3,2,1,0:T(8,128)S(1)} %get-tuple-element.32.given_, ...), custom_call_target="tpu_custom_call", output_to_operand_aliasing={{0}: (0, {})} | custom-call | flops 1000000 | bytes 4000000 | tf_op jit(solution)/shard_map/pallas_call | solution.py:534
  23.2 3.1 %all-to-all-start.1 = ((f32[32,8,1,128]{3,1,2,0:T(8,128)}), f32[32,8,1,128]{3,1,2,0:T(8,128)S(1)}, u32[]{:S(2)}, u32[]{:S(2)}) async-start(f32[32,8,1,128]{3,1,2,0:T(8,128)} %bitcast.5), calls=%async_computation.1 | async-start | bytes 262144 | tf_op jit(solution)/shard_map/all_to_all | solution.py:556
  26.3 0.3 collective-permute-start.6
  26.6 3.0 %collective-permute-start.7 = (f32[12,128]{1,0:T(8,128)S(1)}, f32[12,128]{1,0:T(8,128)S(1)}, u32[]{:S(2)}, u32[]{:S(2)}) collective-permute-start(f32[12,128]{1,0:T(8,128)S(1)} %get-tuple-element.40), channel_id=1, source_target_pairs={{0,4},{4,0},{8,12},{12,8},{16,20},{20,16},{24,28},{28,24},{1,5},{5... | collective-permute-start | bytes 18440 | tf_op jit(solution)/shard_map/ppermute | solution.py:563
  29.6 0.0 collective-permute-start.5
  29.6 1.5 %collective-permute-start.8 = (f32[1,384]{1,0:T(1,128)S(1)}, f32[1,384]{1,0:T(1,128)S(1)}, u32[]{:S(2)}, u32[]{:S(2)}) collective-permute-start(f32[1,384]{1,0:T(1,128)S(1)} %get-tuple-element.41), channel_id=1, source_target_pairs={{0,1},{1,0},{2,3},{3,2},{4,5},{5,4},{6,7},{7,6},{8,9},{9,8},{10,11... | collective-permute-start | bytes 4616 | tf_op jit(solution)/shard_map/ppermute | solution.py:563
  31.2 0.2 shard_map.136.inner_ref
  31.4 1.8 %collective-permute-done.5.yb_ref = f32[1,384]{1,0:T(1,128)S(1)} collective-permute-done((f32[1,384]{1,0:T(1,128)S(1)}, f32[1,384]{1,0:T(1,128)S(1)}, u32[]{:S(2)}, u32[]{:S(2)}) %collective-permute-start.5) | collective-permute-done | bytes 1568 | tf_op jit(solution)/shard_map/ppermute | solution.py:579
  33.2 0.0 collective-permute-done.8.ya_ref
  33.2 0.0 collective-permute-done.6.xb_ref
  33.2 0.0 collective-permute-done.7.xa_ref
  33.2 1.3 %all-to-all-done.1 = f32[32,8,1,128]{3,1,2,0:T(8,128)S(1)} async-done(((f32[32,8,1,128]{3,1,2,0:T(8,128)}), f32[32,8,1,128]{3,1,2,0:T(8,128)S(1)}, u32[]{:S(2)}, u32[]{:S(2)}) %all-to-all-start.1) | async-done | bytes 131104 | tf_op jit(solution)/shard_map/all_to_all | solution.py:556
  34.5 1.4 %shard_map.137 = (f32[12,32,128]{2,1,0:T(8,128)}, f32[1,32]{1,0:T(1,128)}) custom-call(f32[256,128]{1,0:T(8,128)S(1)} %bitcast.10, f32[3,8,128]{2,1,0:T(8,128)S(1)} %get-tuple-element.34.known_ref, s32[1,1024]{1,0:T(1,128)S(1)} %copy-done, s32[1,1024]{1,0:T(1,128)S(1)} %copy-done.1, f32[1,1024]{1,0:T(1,128)S(1)} %copy-done.2, ...), custom_call_target="tpu_custom_call" | custom-call | flops 1000000 | bytes 4000000 | tf_op jit(solution)/shard_map/pallas_call | solution.py:534
Async XLA Ops:
  0.6 16.7 %copy-start.2 = (f32[1,1024]{1,0:T(1,128)S(1)}, f32[1,1024]{1,0:T(1,128)}, u32[]{:S(2)}) copy-start(f32[1,1024]{1,0:T(1,128)} %index_ref.5) | copy-start | bytes 12292
  0.6 16.7 %copy-start.1 = (s32[1,1024]{1,0:T(1,128)S(1)}, s32[1,1024]{1,0:T(1,128)}, u32[]{:S(2)}) copy-start(s32[1,1024]{1,0:T(1,128)} %well_ref.5) | copy-start | bytes 12292
  0.7 16.7 %copy-start = (s32[1,1024]{1,0:T(1,128)S(1)}, s32[1,1024]{1,0:T(1,128)}, u32[]{:S(2)}) copy-start(s32[1,1024]{1,0:T(1,128)} %cell_ref.5) | copy-start | bytes 12292
  0.7 3.5 %copy-start.4 = (f32[32]{0:T(128)S(1)}, f32[32]{0:T(128)}, u32[]{:S(2)}) copy-start(f32[32]{0:T(128)} %param.23) | copy-start | bytes 388
  0.7 3.5 %copy-start.3 = (s32[32]{0:T(128)S(1)}, s32[32]{0:T(128)}, u32[]{:S(2)}) copy-start(s32[32]{0:T(128)} %param.22) | copy-start | bytes 388
  2.8 1.3 %collective-permute-start = (f32[8,128]{1,0:T(8,128)S(1)}, f32[8,128]{1,0:T(8,128)S(1)}, u32[]{:S(2)}, u32[]{:S(2)}) collective-permute-start(f32[8,128]{1,0:T(8,128)S(1)} %get-tuple-element.25), channel_id=1, source_target_pairs={{0,1},{1,0},{2,3},{3,2},{4,5},{5,4},{6,7},{7,6},{8,9},{9,8},{10,11... | collective-permute-start | bytes 12296 | tf_op jit(solution)/shard_map/ppermute | solution.py:563
  5.2 15.8 %all-to-all-start = ((f32[32,10,1,128]{3,2,1,0:T(1,128)}), f32[32,10,1,128]{3,2,1,0:T(1,128)S(1)}, u32[]{:S(2)}, u32[]{:S(2)}) async-start(f32[32,10,1,128]{3,2,1,0:T(1,128)} %bitcast.2), calls=%async_computation | async-start | bytes 327680 | tf_op jit(solution)/shard_map/all_to_all | solution.py:556
  12.4 7.0 %collective-permute-start.2 = (f32[72,128]{1,0:T(8,128)S(1)}, f32[72,128]{1,0:T(8,128)S(1)}, u32[]{:S(2)}, u32[]{:S(2)}) collective-permute-start(f32[72,128]{1,0:T(8,128)S(1)} %get-tuple-element.29.own_xb_ref), channel_id=1, source_target_pairs={{0,1},{1,0},{2,3},{3,2},{4,8},{5,9},{6,10},{7,11},{8,4},{9,5},{10,... | collective-permute-start | bytes 110600 | tf_op jit(solution)/shard_map/ppermute | solution.py:579
  12.8 6.7 %collective-permute-start.3 = (f32[72,128]{1,0:T(8,128)S(1)}, f32[72,128]{1,0:T(8,128)S(1)}, u32[]{:S(2)}, u32[]{:S(2)}) collective-permute-start(f32[72,128]{1,0:T(8,128)S(1)} %get-tuple-element.30.own_xa_ref), channel_id=1, source_target_pairs={{0,4},{4,0},{8,12},{12,8},{16,20},{20,16},{24,28},{28,24},{1,5},{5... | collective-permute-start | bytes 110600 | tf_op jit(solution)/shard_map/ppermute | solution.py:563
  15.7 3.7 %collective-permute-start.1 = (f32[8,384]{1,0:T(8,128)S(1)}, f32[8,384]{1,0:T(8,128)S(1)}, u32[]{:S(2)}, u32[]{:S(2)}) collective-permute-start(f32[8,384]{1,0:T(8,128)S(1)} %get-tuple-element.28.own_yb_ref), channel_id=1, source_target_pairs={{0,4},{1,2},{2,1},{3,7},{4,0},{5,6},{6,5},{7,3},{8,12},{9,10},{10,... | collective-permute-start | bytes 36872 | tf_op jit(solution)/shard_map/ppermute | solution.py:579
  15.8 3.7 %collective-permute-start.4 = (f32[8,384]{1,0:T(8,128)S(1)}, f32[8,384]{1,0:T(8,128)S(1)}, u32[]{:S(2)}, u32[]{:S(2)}) collective-permute-start(f32[8,384]{1,0:T(8,128)S(1)} %get-tuple-element.31.own_ya_ref), channel_id=1, source_target_pairs={{0,1},{1,0},{2,3},{3,2},{4,5},{5,4},{6,7},{7,6},{8,9},{9,8},{10,11... | collective-permute-start | bytes 36872 | tf_op jit(solution)/shard_map/ppermute | solution.py:563
  23.2 11.4 %all-to-all-start.1 = ((f32[32,8,1,128]{3,1,2,0:T(8,128)}), f32[32,8,1,128]{3,1,2,0:T(8,128)S(1)}, u32[]{:S(2)}, u32[]{:S(2)}) async-start(f32[32,8,1,128]{3,1,2,0:T(8,128)} %bitcast.5), calls=%async_computation.1 | async-start | bytes 262144 | tf_op jit(solution)/shard_map/all_to_all | solution.py:556
  26.3 6.9 %collective-permute-start.6 = (f32[12,128]{1,0:T(8,128)S(1)}, f32[12,128]{1,0:T(8,128)S(1)}, u32[]{:S(2)}, u32[]{:S(2)}) collective-permute-start(f32[12,128]{1,0:T(8,128)S(1)} %get-tuple-element.39), channel_id=1, source_target_pairs={{0,1},{1,0},{2,3},{3,2},{4,8},{5,9},{6,10},{7,11},{8,4},{9,5},{10,... | collective-permute-start | bytes 18440 | tf_op jit(solution)/shard_map/ppermute | solution.py:579
  26.6 6.6 %collective-permute-start.7 = (f32[12,128]{1,0:T(8,128)S(1)}, f32[12,128]{1,0:T(8,128)S(1)}, u32[]{:S(2)}, u32[]{:S(2)}) collective-permute-start(f32[12,128]{1,0:T(8,128)S(1)} %get-tuple-element.40), channel_id=1, source_target_pairs={{0,4},{4,0},{8,12},{12,8},{16,20},{20,16},{24,28},{28,24},{1,5},{5... | collective-permute-start | bytes 18440 | tf_op jit(solution)/shard_map/ppermute | solution.py:563
  29.6 3.6 %collective-permute-start.5 = (f32[1,384]{1,0:T(1,128)S(1)}, f32[1,384]{1,0:T(1,128)S(1)}, u32[]{:S(2)}, u32[]{:S(2)}) collective-permute-start(f32[1,384]{1,0:T(1,128)S(1)} %get-tuple-element.38), channel_id=1, source_target_pairs={{0,4},{1,2},{2,1},{3,7},{4,0},{5,6},{6,5},{7,3},{8,12},{9,10},{10,... | collective-permute-start | bytes 4616 | tf_op jit(solution)/shard_map/ppermute | solution.py:579
  29.6 3.6 %collective-permute-start.8 = (f32[1,384]{1,0:T(1,128)S(1)}, f32[1,384]{1,0:T(1,128)S(1)}, u32[]{:S(2)}, u32[]{:S(2)}) collective-permute-start(f32[1,384]{1,0:T(1,128)S(1)} %get-tuple-element.41), channel_id=1, source_target_pairs={{0,1},{1,0},{2,3},{3,2},{4,5},{5,4},{6,7},{7,6},{8,9},{9,8},{10,11... | collective-permute-start | bytes 4616 | tf_op jit(solution)/shard_map/ppermute | solution.py:563

commit v7 on v6

--- a/solution.py
+++ b/solution.py
@@ -194,14 +194,11 @@
 ):
     owned = mode_ref.shape[1]
     group = LANES // owned
-    here = lax.shift_right_logical(iota((1, LANES), 1), bits_of(owned)) == lax.rem(
-        lax.axis_index(AXES), group
-    )
-    controls = [
-        jnp.where(here, jnp.concatenate([ref[...].astype(F32)] * group, axis=1), 0.0)
-        for ref in (mode_ref, target_ref)
-    ]
-    block = jnp.concatenate([keep_ref[...] + given_ref[...]] + controls, axis=0)
+    controls = [mode_ref[...].astype(F32), target_ref[...]]
+    if group > 2:
+        controls.append(jnp.zeros((1, LANES - 2 * owned), F32))
+    controls = jnp.concatenate(controls, axis=1)
+    block = jnp.concatenate([keep_ref[...] + given_ref[...], controls], axis=0)
     block_ref[...] = jnp.concatenate([block] * (block_ref.shape[0] // block.shape[0]), axis=0)
     copies = repeat_out(block_ref, out_ref, sems)
     layers, width, lanes = flag_ref.shape
@@ -418,28 +415,38 @@
 
 def first_update(
     given_ref, sums_ref, cell_ref, well_ref, index_ref,
-    grid_ref, out_ref, yb_ref, xb_ref, xa_ref, ya_ref, known_ref, block_ref, sems,
+    grid_ref, out_ref, yb_ref, xb_ref, xa_ref, ya_ref, known_ref, line_ref, block_ref, sems,
 ):
     layers, width, lanes = grid_ref.shape[1:]
     rows = layers * width
     count = lax.axis_size("gx") * lax.axis_size("gy")
     chunk = sums_ref.shape[0] // count
-    well_rows = chunk - 2
+    well_rows = chunk - 1
     half = well_rows // 2
     group = count // well_rows
-    low, high = sums_ref[0:well_rows, :], sums_ref[chunk : chunk + well_rows, :]
-    for d in range(2, count, 2):
-        low = low + sums_ref[d * chunk : d * chunk + well_rows, :]
-        high = high + sums_ref[(d + 1) * chunk : (d + 1) * chunk + well_rows, :]
+    across = lax.axis_size("gx")
+    low = high = jnp.zeros((well_rows, LANES), F32)
+    for d in range(count):
+        sums = sums_ref[d * chunk : d * chunk + well_rows, :]
+        if d // across % 2:
+            high = high + sums
+        else:
+            low = low + sums
     part = jnp.concatenate([low[:half], high[:half]], axis=0)
     base = jnp.concatenate([low[half:], high[half:]], axis=0)
-    controls = []
-    for k in (well_rows, well_rows + 1):
-        total = sums_ref[pl.ds(k, well_rows, stride=group * chunk), :]
-        for j in range(1, group):
-            total = total + sums_ref[pl.ds(j * chunk + k, well_rows, stride=group * chunk), :]
-        controls.append(total)
-    mode, target = controls
+    owned = LANES // group
+    place = lax.shift_right_logical(iota((well_rows, LANES), 1), bits_of(owned))
+    mode = target = jnp.zeros((well_rows, LANES), F32)
+    for j in range(group):
+        for r in range(well_rows // across):
+            first = (r * group + j) * across * chunk + well_rows
+            line_ref[pl.ds(r, across, stride=well_rows // across), :] = sums_ref[
+                pl.ds(first, across, stride=chunk), :
+            ]
+        line = line_ref[...]
+        mode = jnp.where(place == j, pltpu.roll(line, j * owned, 1) if j else line, mode)
+        shift = (j - 1) % group * owned
+        target = jnp.where(place == j, pltpu.roll(line, shift, 1) if shift else line, target)
     bhp = jnp.where(mode < 0.5, target, (part - target) / base)
     known_ref[0] = mode
     known_ref[1] = target
@@ -553,7 +560,7 @@
 
 def everyone(rows, count):
     height = rows.shape[0] // count
-    swapped = lax.all_to_all(rows.reshape(count, height, 1, LANES), AXES, 0, 0, tiled=True)
+    swapped = lax.all_to_all(rows.reshape(count, height, 1, LANES), AXES[::-1], 0, 0, tiled=True)
     return swapped.reshape(rows.shape)
 
 
@@ -588,7 +595,7 @@
     count = lax.axis_size("gx") * lax.axis_size("gy")
     owned = well_mode.shape[0]
     well_rows = owned * count // LANES
-    chunk = well_rows + 2
+    chunk = well_rows + 1
     grid = (layers, width, lanes)
     slots = [perf_cell, perf_well, perf_index]
     operands = slots + [
@@ -645,7 +652,7 @@
             (3, well_rows, LANES),
         ],
         [given, gathered] + slots,
-        [(height, LANES), pltpu.SemaphoreType.DMA((count * well_rows // height,))],
+        [(well_rows, LANES), (height, LANES), pltpu.SemaphoreType.DMA((count * well_rows // height,))],
         None,
         [pltpu.VMEM, pltpu.HBM] + [pltpu.VMEM] * 5,
         {0: 0},

time: 36.1 us -> 35.6 us (0.986)
  waiting for transfers between devices: 5.28 us -> 4.04 us
  starting transfers between devices: 20.6 us -> 21.2 us
    all_to_all x2, waiting for transfers between devices: 2.34 us -> 1.02 us  [everyone(): lax.all_to_all(rows.reshape(count, height, 1, LANES), AXES[::-1], 0, 0, t...]
    all_to_all x2, starting transfers between devices: 10.3 us -> 10.9 us  [everyone(): lax.all_to_all(rows.reshape(count, height, 1, LANES), AXES[::-1], 0, 0, t...]
where the time goes in v7:
time: 35.6 us; the launch traced here: 35.3 us
  starting transfers between devices  21.2 us (60%)
  Pallas kernels  9.3 us (26%)
  waiting for transfers between devices  4.04 us (11%)
  between operations  0.75 us (2%)
    all_to_all x2, starting transfers between devices, everyone(): lax.all_to_all(rows.reshape(count, height, 1, LANES), AXES[::-1], 0, 0, t...  10.9 us
    ppermute x5, starting transfers between devices, to_pair(): return lax.ppermute(block, axis, [(i, i ^ 1) for i in range(count)])  9.57 us
    pallas_call x7, Pallas kernels, call(): pl.pallas_call(kernel, out_shape=shapes, in_specs=[pl.BlockSpec(memory_sp...  9.3 us
    ppermute x4, waiting for transfers between devices, to_other(): return lax.ppermute(block, AXES, moves)  2.19 us
    all_to_all x2, waiting for transfers between devices, everyone(): lax.all_to_all(rows.reshape(count, height, 1, LANES), AXES[::-1], 0, 0, t...  1.02 us
    ppermute x5, waiting for transfers between devices, to_pair(): return lax.ppermute(block, axis, [(i, i ^ 1) for i in range(count)])  0.83 us
  transfers between devices with their start and end apart: 11, of which 5 were waited for; matrix products, arithmetic and copies ran while one was open for 0% of the time, Pallas kernels for 7%

profile of v7, /device:TPU:0, one launch (start us, length us, event | category | flops | bytes accessed | tf_op | source)
XLA Modules:
  0.0 35.3 jit_solution(2254127738611752643)
XLA Ops:
  0.6 0.0 copy-start.2
  0.6 0.0 copy-start.1
  0.7 0.0 copy-start
  0.7 0.0 copy-start.4
  0.7 0.0 copy-start.3
  0.7 2.2 %shard_map.131 = (f32[8,128]{1,0:T(8,128)S(1)}, f32[8,128]{1,0:T(8,128)S(1)}, f32[11,12,32,128]{3,2,1,0:T(8,128)S(1)}, s32[12,32,128]{2,1,0:T(8,128)S(1)}) custom-call(s32[1,1024]{1,0:T(1,128)} %cell_ref.5, s32[1,1024]{1,0:T(1,128)} %well_ref.5, f32[1,1024]{1,0:T(1,128)} %index_ref.5, f32[2,12,32,128]{3,2,1,0:T(8,128)} %refs_3_.1, f32[12,32,128]{2,1,0:T(8,128)} %refs_4_.1, ...), custom_call_target="tpu_custom_call" | custom-call | flops 1000000 | bytes 4000000 | tf_op jit(solution)/shard_map/pallas_call | solution.py:541
  2.8 0.5 %collective-permute-start = (f32[8,128]{1,0:T(8,128)S(1)}, f32[8,128]{1,0:T(8,128)S(1)}, u32[]{:S(2)}, u32[]{:S(2)}) collective-permute-start(f32[8,128]{1,0:T(8,128)S(1)} %get-tuple-element.25), channel_id=1, source_target_pairs={{0,1},{1,0},{2,3},{3,2},{4,5},{5,4},{6,7},{7,6},{8,9},{9,8},{10,11... | collective-permute-start | bytes 12296 | tf_op jit(solution)/shard_map/ppermute | solution.py:570
  3.4 0.8 %collective-permute-done.given_ref = f32[8,128]{1,0:T(8,128)S(1)} collective-permute-done((f32[8,128]{1,0:T(8,128)S(1)}, f32[8,128]{1,0:T(8,128)S(1)}, u32[]{:S(2)}, u32[]{:S(2)}) %collective-permute-start) | collective-permute-done | bytes 4128 | tf_op jit(solution)/shard_map/ppermute | solution.py:570
  4.2 0.0 copy-done.4
  4.2 0.0 copy-done.3
  4.2 1.1 %shard_map.132 = (f32[288,128]{1,0:T(8,128)}, f32[8,384]{1,0:T(8,128)S(1)}, f32[72,128]{1,0:T(8,128)S(1)}, f32[72,128]{1,0:T(8,128)S(1)}, f32[8,384]{1,0:T(8,128)S(1)}) custom-call(f32[8,128]{1,0:T(8,128)S(1)} %get-tuple-element.24.keep_ref, f32[8,128]{1,0:T(8,128)S(1)} %collective-permute-done.given_ref, s32[1,32]{1,0:T(1,128)S(1)} %bitcast.11, ...), custom_call_target="tpu_custom_call" | custom-call | flops 1000000 | bytes 4000000 | tf_op jit(solution)/shard_map/pallas_call | solution.py:541
  5.3 7.2 %all-to-all-start = ((f32[32,9,1,128]{3,2,1,0:T(1,128)}), f32[32,9,1,128]{3,2,1,0:T(1,128)S(1)}, u32[]{:S(2)}, u32[]{:S(2)}) async-start(f32[32,9,1,128]{3,2,1,0:T(1,128)} %bitcast.2), calls=%async_computation | async-start | bytes 294912 | tf_op jit(solution)/shard_map/all_to_all | solution.py:563
  12.5 0.3 collective-permute-start.2
  12.8 3.0 %collective-permute-start.3 = (f32[72,128]{1,0:T(8,128)S(1)}, f32[72,128]{1,0:T(8,128)S(1)}, u32[]{:S(2)}, u32[]{:S(2)}) collective-permute-start(f32[72,128]{1,0:T(8,128)S(1)} %get-tuple-element.30.own_xa_ref), channel_id=1, source_target_pairs={{0,4},{4,0},{8,12},{12,8},{16,20},{20,16},{24,28},{28,24},{1,5},{5... | collective-permute-start | bytes 110600 | tf_op jit(solution)/shard_map/ppermute | solution.py:570
  15.8 0.0 collective-permute-start.1
  15.8 1.5 %collective-permute-start.4 = (f32[8,384]{1,0:T(8,128)S(1)}, f32[8,384]{1,0:T(8,128)S(1)}, u32[]{:S(2)}, u32[]{:S(2)}) collective-permute-start(f32[8,384]{1,0:T(8,128)S(1)} %get-tuple-element.31.own_ya_ref), channel_id=1, source_target_pairs={{0,1},{1,0},{2,3},{3,2},{4,5},{5,4},{6,7},{7,6},{8,9},{9,8},{10,11... | collective-permute-start | bytes 36872 | tf_op jit(solution)/shard_map/ppermute | solution.py:570
  17.3 0.0 copy-done.2
  17.4 0.0 copy-done.1
  17.4 0.0 copy-done
  17.4 1.8 %shard_map.133.given_ref = f32[11,12,32,128]{3,2,1,0:T(8,128)S(1)} custom-call(f32[11,12,32,128]{3,2,1,0:T(8,128)S(1)} %get-tuple-element.23.grid_ref.given_ref, f32[288,128]{1,0:T(8,128)} %get-tuple-element.27.after_ref, s32[12,32,128]{2,1,0:T(8,128)S(1)} %get-tuple-element.26.flag_ref, s32[1,1024]{1,0:T(1,128)S(1)} %copy-done, ...), custom_call_target="tpu_custom_call", output_to_operand_aliasing={{}: (0, {})} | custom-call | flops 1000000 | bytes 4000000 | tf_op jit(solution)/shard_map/pallas_call | solution.py:541
  19.2 0.3 collective-permute-done.1.yb_ref
  19.5 0.0 collective-permute-done.4.ya_ref
  19.5 0.0 collective-permute-done.2.xb_ref
  19.5 0.0 collective-permute-done.3.xa_ref
  19.5 0.5 %shard_map.134 = (f32[11,12,32,128]{3,2,1,0:T(8,128)S(1)}, f32[2,12,128]{2,1,0:T(8,128)S(1)}, f32[8,384]{1,0:T(8,128)S(1)}) custom-call(f32[11,12,32,128]{3,2,1,0:T(8,128)S(1)} %shard_map.133.given_ref, f32[8,384]{1,0:T(8,128)S(1)} %get-tuple-element.28.own_yb_ref, f32[72,128]{1,0:T(8,128)S(1)} %get-tuple-element.29.own_xb_ref, ...), custom_call_target="tpu_custom_call", output_to_operand_aliasing={{0}: (0, {})} | custom-call | flops 1000000 | bytes 4000000 | tf_op jit(solution)/shard_map/pallas_call | solution.py:541
  20.1 0.2 all-to-all-done
  20.3 2.2 %shard_map.135 = (f32[11,12,32,128]{3,2,1,0:T(8,128)S(1)}, f32[256,128]{1,0:T(8,128)}, f32[1,384]{1,0:T(1,128)S(1)}, f32[12,128]{1,0:T(8,128)S(1)}, f32[12,128]{...) custom-call(f32[11,12,32,128]{3,2,1,0:T(8,128)S(1)} %get-tuple-element.32.given_, ...), custom_call_target="tpu_custom_call", output_to_operand_aliasing={{0}: (0, {})} | custom-call | flops 1000000 | bytes 4000000 | tf_op jit(solution)/shard_map/pallas_call | solution.py:541
  22.5 3.7 %all-to-all-start.1 = ((f32[32,8,1,128]{3,1,2,0:T(8,128)}), f32[32,8,1,128]{3,1,2,0:T(8,128)S(1)}, u32[]{:S(2)}, u32[]{:S(2)}) async-start(f32[32,8,1,128]{3,1,2,0:T(8,128)} %bitcast.5), calls=%async_computation.1 | async-start | bytes 262144 | tf_op jit(solution)/shard_map/all_to_all | solution.py:563
  26.2 0.3 collective-permute-start.6
  26.5 3.0 %collective-permute-start.7 = (f32[12,128]{1,0:T(8,128)S(1)}, f32[12,128]{1,0:T(8,128)S(1)}, u32[]{:S(2)}, u32[]{:S(2)}) collective-permute-start(f32[12,128]{1,0:T(8,128)S(1)} %get-tuple-element.40), channel_id=1, source_target_pairs={{0,4},{4,0},{8,12},{12,8},{16,20},{20,16},{24,28},{28,24},{1,5},{5... | collective-permute-start | bytes 18440 | tf_op jit(solution)/shard_map/ppermute | solution.py:570
  29.5 0.0 collective-permute-start.5
  29.6 1.5 %collective-permute-start.8 = (f32[1,384]{1,0:T(1,128)S(1)}, f32[1,384]{1,0:T(1,128)S(1)}, u32[]{:S(2)}, u32[]{:S(2)}) collective-permute-start(f32[1,384]{1,0:T(1,128)S(1)} %get-tuple-element.41), channel_id=1, source_target_pairs={{0,1},{1,0},{2,3},{3,2},{4,5},{5,4},{6,7},{7,6},{8,9},{9,8},{10,11... | collective-permute-start | bytes 4616 | tf_op jit(solution)/shard_map/ppermute | solution.py:570
  31.1 0.2 shard_map.136.inner_ref
  31.3 1.9 %collective-permute-done.5.yb_ref = f32[1,384]{1,0:T(1,128)S(1)} collective-permute-done((f32[1,384]{1,0:T(1,128)S(1)}, f32[1,384]{1,0:T(1,128)S(1)}, u32[]{:S(2)}, u32[]{:S(2)}) %collective-permute-start.5) | collective-permute-done | bytes 1568 | tf_op jit(solution)/shard_map/ppermute | solution.py:586
  33.2 0.0 collective-permute-done.8.ya_ref
  33.2 0.0 collective-permute-done.6.xb_ref
  33.2 0.0 collective-permute-done.7.xa_ref
  33.2 0.8 %all-to-all-done.1 = f32[32,8,1,128]{3,1,2,0:T(8,128)S(1)} async-done(((f32[32,8,1,128]{3,1,2,0:T(8,128)}), f32[32,8,1,128]{3,1,2,0:T(8,128)S(1)}, u32[]{:S(2)}, u32[]{:S(2)}) %all-to-all-start.1) | async-done | bytes 131104 | tf_op jit(solution)/shard_map/all_to_all | solution.py:563
  34.0 1.4 %shard_map.137 = (f32[12,32,128]{2,1,0:T(8,128)}, f32[1,32]{1,0:T(1,128)}) custom-call(f32[256,128]{1,0:T(8,128)S(1)} %bitcast.10, f32[3,8,128]{2,1,0:T(8,128)S(1)} %get-tuple-element.34.known_ref, s32[1,1024]{1,0:T(1,128)S(1)} %copy-done, s32[1,1024]{1,0:T(1,128)S(1)} %copy-done.1, f32[1,1024]{1,0:T(1,128)S(1)} %copy-done.2, ...), custom_call_target="tpu_custom_call" | custom-call | flops 1000000 | bytes 4000000 | tf_op jit(solution)/shard_map/pallas_call | solution.py:541
Async XLA Ops:
  0.6 16.7 %copy-start.2 = (f32[1,1024]{1,0:T(1,128)S(1)}, f32[1,1024]{1,0:T(1,128)}, u32[]{:S(2)}) copy-start(f32[1,1024]{1,0:T(1,128)} %index_ref.5) | copy-start | bytes 12292
  0.6 16.7 %copy-start.1 = (s32[1,1024]{1,0:T(1,128)S(1)}, s32[1,1024]{1,0:T(1,128)}, u32[]{:S(2)}) copy-start(s32[1,1024]{1,0:T(1,128)} %well_ref.5) | copy-start | bytes 12292
  0.7 16.7 %copy-start = (s32[1,1024]{1,0:T(1,128)S(1)}, s32[1,1024]{1,0:T(1,128)}, u32[]{:S(2)}) copy-start(s32[1,1024]{1,0:T(1,128)} %cell_ref.5) | copy-start | bytes 12292
  0.7 3.5 %copy-start.4 = (f32[32]{0:T(128)S(1)}, f32[32]{0:T(128)}, u32[]{:S(2)}) copy-start(f32[32]{0:T(128)} %param.23) | copy-start | bytes 388
  0.7 3.5 %copy-start.3 = (s32[32]{0:T(128)S(1)}, s32[32]{0:T(128)}, u32[]{:S(2)}) copy-start(s32[32]{0:T(128)} %param.22) | copy-start | bytes 388
  2.8 1.3 %collective-permute-start = (f32[8,128]{1,0:T(8,128)S(1)}, f32[8,128]{1,0:T(8,128)S(1)}, u32[]{:S(2)}, u32[]{:S(2)}) collective-permute-start(f32[8,128]{1,0:T(8,128)S(1)} %get-tuple-element.25), channel_id=1, source_target_pairs={{0,1},{1,0},{2,3},{3,2},{4,5},{5,4},{6,7},{7,6},{8,9},{9,8},{10,11... | collective-permute-start | bytes 12296 | tf_op jit(solution)/shard_map/ppermute | solution.py:570
  5.3 15.0 %all-to-all-start = ((f32[32,9,1,128]{3,2,1,0:T(1,128)}), f32[32,9,1,128]{3,2,1,0:T(1,128)S(1)}, u32[]{:S(2)}, u32[]{:S(2)}) async-start(f32[32,9,1,128]{3,2,1,0:T(1,128)} %bitcast.2), calls=%async_computation | async-start | bytes 294912 | tf_op jit(solution)/shard_map/all_to_all | solution.py:563
  12.5 7.0 %collective-permute-start.2 = (f32[72,128]{1,0:T(8,128)S(1)}, f32[72,128]{1,0:T(8,128)S(1)}, u32[]{:S(2)}, u32[]{:S(2)}) collective-permute-start(f32[72,128]{1,0:T(8,128)S(1)} %get-tuple-element.29.own_xb_ref), channel_id=1, source_target_pairs={{0,1},{1,0},{2,3},{3,2},{4,8},{5,9},{6,10},{7,11},{8,4},{9,5},{10,... | collective-permute-start | bytes 110600 | tf_op jit(solution)/shard_map/ppermute | solution.py:586
  12.8 6.7 %collective-permute-start.3 = (f32[72,128]{1,0:T(8,128)S(1)}, f32[72,128]{1,0:T(8,128)S(1)}, u32[]{:S(2)}, u32[]{:S(2)}) collective-permute-start(f32[72,128]{1,0:T(8,128)S(1)} %get-tuple-element.30.own_xa_ref), channel_id=1, source_target_pairs={{0,4},{4,0},{8,12},{12,8},{16,20},{20,16},{24,28},{28,24},{1,5},{5... | collective-permute-start | bytes 110600 | tf_op jit(solution)/shard_map/ppermute | solution.py:570
  15.8 3.7 %collective-permute-start.1 = (f32[8,384]{1,0:T(8,128)S(1)}, f32[8,384]{1,0:T(8,128)S(1)}, u32[]{:S(2)}, u32[]{:S(2)}) collective-permute-start(f32[8,384]{1,0:T(8,128)S(1)} %get-tuple-element.28.own_yb_ref), channel_id=1, source_target_pairs={{0,4},{1,2},{2,1},{3,7},{4,0},{5,6},{6,5},{7,3},{8,12},{9,10},{10,... | collective-permute-start | bytes 36872 | tf_op jit(solution)/shard_map/ppermute | solution.py:586
  15.8 3.7 %collective-permute-start.4 = (f32[8,384]{1,0:T(8,128)S(1)}, f32[8,384]{1,0:T(8,128)S(1)}, u32[]{:S(2)}, u32[]{:S(2)}) collective-permute-start(f32[8,384]{1,0:T(8,128)S(1)} %get-tuple-element.31.own_ya_ref), channel_id=1, source_target_pairs={{0,1},{1,0},{2,3},{3,2},{4,5},{5,4},{6,7},{7,6},{8,9},{9,8},{10,11... | collective-permute-start | bytes 36872 | tf_op jit(solution)/shard_map/ppermute | solution.py:570
  22.5 11.5 %all-to-all-start.1 = ((f32[32,8,1,128]{3,1,2,0:T(8,128)}), f32[32,8,1,128]{3,1,2,0:T(8,128)S(1)}, u32[]{:S(2)}, u32[]{:S(2)}) async-start(f32[32,8,1,128]{3,1,2,0:T(8,128)} %bitcast.5), calls=%async_computation.1 | async-start | bytes 262144 | tf_op jit(solution)/shard_map/all_to_all | solution.py:563
  26.2 6.9 %collective-permute-start.6 = (f32[12,128]{1,0:T(8,128)S(1)}, f32[12,128]{1,0:T(8,128)S(1)}, u32[]{:S(2)}, u32[]{:S(2)}) collective-permute-start(f32[12,128]{1,0:T(8,128)S(1)} %get-tuple-element.39), channel_id=1, source_target_pairs={{0,1},{1,0},{2,3},{3,2},{4,8},{5,9},{6,10},{7,11},{8,4},{9,5},{10,... | collective-permute-start | bytes 18440 | tf_op jit(solution)/shard_map/ppermute | solution.py:586
  26.5 6.6 %collective-permute-start.7 = (f32[12,128]{1,0:T(8,128)S(1)}, f32[12,128]{1,0:T(8,128)S(1)}, u32[]{:S(2)}, u32[]{:S(2)}) collective-permute-start(f32[12,128]{1,0:T(8,128)S(1)} %get-tuple-element.40), channel_id=1, source_target_pairs={{0,4},{4,0},{8,12},{12,8},{16,20},{20,16},{24,28},{28,24},{1,5},{5... | collective-permute-start | bytes 18440 | tf_op jit(solution)/shard_map/ppermute | solution.py:570
  29.5 3.6 %collective-permute-start.5 = (f32[1,384]{1,0:T(1,128)S(1)}, f32[1,384]{1,0:T(1,128)S(1)}, u32[]{:S(2)}, u32[]{:S(2)}) collective-permute-start(f32[1,384]{1,0:T(1,128)S(1)} %get-tuple-element.38), channel_id=1, source_target_pairs={{0,4},{1,2},{2,1},{3,7},{4,0},{5,6},{6,5},{7,3},{8,12},{9,10},{10,... | collective-permute-start | bytes 4616 | tf_op jit(solution)/shard_map/ppermute | solution.py:586
  29.6 3.6 %collective-permute-start.8 = (f32[1,384]{1,0:T(1,128)S(1)}, f32[1,384]{1,0:T(1,128)S(1)}, u32[]{:S(2)}, u32[]{:S(2)}) collective-permute-start(f32[1,384]{1,0:T(1,128)S(1)} %get-tuple-element.41), channel_id=1, source_target_pairs={{0,1},{1,0},{2,3},{3,2},{4,5},{5,4},{6,7},{7,6},{8,9},{9,8},{10,11... | collective-permute-start | bytes 4616 | tf_op jit(solution)/shard_map/ppermute | solution.py:570

commit v8 on v7

--- a/solution.py
+++ b/solution.py
@@ -474,6 +474,14 @@
         copy.wait()
 
 
+def whole_first_update(*refs):
+    given_ref, sums_ref, cell_ref, well_ref, index_ref = refs[:5]
+    rims, (grid_ref, bound_ref, flank_ref) = refs[5:13], refs[13:16]
+    outs, side_ref, scratch = refs[16:22], refs[22], refs[23:]
+    outer_terms(given_ref, *rims, grid_ref, bound_ref, flank_ref, side_ref)
+    first_update(given_ref, sums_ref, cell_ref, well_ref, index_ref, grid_ref, *outs, *scratch)
+
+
 def inner_terms(after_ref, grid_ref, out_ref):
     layers, width, lanes = out_ref.shape
     for z in range(layers):
@@ -637,24 +645,21 @@
         None,
         {0: 0},
     )
-    given, bound, flank = call(
-        outer_terms,
-        [(GRIDS,) + grid, (2, layers, lanes), (EDGE, rows)],
-        [given] + rims,
-        [(rows, 3 * lanes)],
-        aliases={0: 0},
-    )
     height = whole_tiles(well_rows, count, count)
-    given, sums, yb, xb, xa, ya, known = call(
-        first_update,
+    given, bound, flank, sums, yb, xb, xa, ya, known = call(
+        whole_first_update,
         [
-            (GRIDS,) + grid, (count * well_rows, LANES), (1, rows), (layers, lanes), (layers, lanes), (1, rows),
+            (GRIDS,) + grid, (2, layers, lanes), (EDGE, rows),
+            (count * well_rows, LANES), (1, rows), (layers, lanes), (layers, lanes), (1, rows),
             (3, well_rows, LANES),
         ],
-        [given, gathered] + slots,
-        [(well_rows, LANES), (height, LANES), pltpu.SemaphoreType.DMA((count * well_rows // height,))],
+        [given, gathered] + slots + rims,
+        [
+            (rows, 3 * lanes), (well_rows, LANES), (height, LANES),
+            pltpu.SemaphoreType.DMA((count * well_rows // height,)),
+        ],
         None,
-        [pltpu.VMEM, pltpu.HBM] + [pltpu.VMEM] * 5,
+        [pltpu.VMEM] * 3 + [pltpu.HBM] + [pltpu.VMEM] * 5,
         {0: 0},
     )
     gathered = everyone(sums, count)

time: 35.6 us -> 35.4 us (level)
  waiting for transfers between devices: 4.04 us -> 4.58 us
  starting transfers between devices: 21.2 us -> 20.7 us
    all_to_all x2, waiting for transfers between devices: 1.02 us -> 1.56 us  [everyone(): lax.all_to_all(rows.reshape(count, height, 1, LANES), AXES[::-1], 0, 0, t...]
    all_to_all x2, starting transfers between devices: 10.9 us -> 10.4 us  [everyone(): lax.all_to_all(rows.reshape(count, height, 1, LANES), AXES[::-1], 0, 0, t...]
    pallas_call x7 -> x6, Pallas kernels: 9.3 us -> 9.15 us  [call(): pl.pallas_call(kernel, out_shape=shapes, in_specs=[pl.BlockSpec(memory_sp...]
  transfers between devices with their start and end apart: 11 -> 11, of which waited for: 5 -> 5; matrix products, arithmetic and copies ran while one was open for 0% -> 0% of each run, Pallas kernels for 7% -> 6%
where the time goes in v8:
time: 35.4 us; the launch traced here: 35.2 us
  starting transfers between devices  20.7 us (58%)
  Pallas kernels  9.15 us (26%)
  waiting for transfers between devices  4.58 us (13%)
  between operations  0.75 us (2%)
    all_to_all x2, starting transfers between devices, everyone(): lax.all_to_all(rows.reshape(count, height, 1, LANES), AXES[::-1], 0, 0, t...  10.4 us
    ppermute x5, starting transfers between devices, to_pair(): return lax.ppermute(block, axis, [(i, i ^ 1) for i in range(count)])  9.57 us
    pallas_call x6, Pallas kernels, call(): pl.pallas_call(kernel, out_shape=shapes, in_specs=[pl.BlockSpec(memory_sp...  9.15 us
    ppermute x4, waiting for transfers between devices, to_other(): return lax.ppermute(block, AXES, moves)  2.19 us
    all_to_all x2, waiting for transfers between devices, everyone(): lax.all_to_all(rows.reshape(count, height, 1, LANES), AXES[::-1], 0, 0, t...  1.56 us
    ppermute x5, waiting for transfers between devices, to_pair(): return lax.ppermute(block, axis, [(i, i ^ 1) for i in range(count)])  0.83 us
  transfers between devices with their start and end apart: 11, of which 5 were waited for; matrix products, arithmetic and copies ran while one was open for 0% of the time, Pallas kernels for 6%

profile of v8, /device:TPU:0, one launch (start us, length us, event | category | flops | bytes accessed | tf_op | source)
XLA Modules:
  0.0 35.2 jit_solution(11508733426696948139)
XLA Ops:
  0.6 0.0 copy-start.2
  0.6 0.0 copy-start.1
  0.7 0.0 copy-start
  0.7 0.0 copy-start.4
  0.7 0.0 copy-start.3
  0.7 2.2 %shard_map.131 = (f32[8,128]{1,0:T(8,128)S(1)}, f32[8,128]{1,0:T(8,128)S(1)}, f32[11,12,32,128]{3,2,1,0:T(8,128)S(1)}, s32[12,32,128]{2,1,0:T(8,128)S(1)}) custom-call(s32[1,1024]{1,0:T(1,128)} %cell_ref.3, s32[1,1024]{1,0:T(1,128)} %well_ref.3, f32[1,1024]{1,0:T(1,128)} %index_ref.3, f32[2,12,32,128]{3,2,1,0:T(8,128)} %refs_3_.2, f32[12,32,128]{2,1,0:T(8,128)} %refs_4_.2, ...), custom_call_target="tpu_custom_call" | custom-call | flops 1000000 | bytes 4000000 | tf_op jit(solution)/shard_map/pallas_call | solution.py:549
  2.8 0.5 %collective-permute-start = (f32[8,128]{1,0:T(8,128)S(1)}, f32[8,128]{1,0:T(8,128)S(1)}, u32[]{:S(2)}, u32[]{:S(2)}) collective-permute-start(f32[8,128]{1,0:T(8,128)S(1)} %get-tuple-element.24), channel_id=1, source_target_pairs={{0,1},{1,0},{2,3},{3,2},{4,5},{5,4},{6,7},{7,6},{8,9},{9,8},{10,11... | collective-permute-start | bytes 12296 | tf_op jit(solution)/shard_map/ppermute | solution.py:578
  3.4 0.8 %collective-permute-done.given_ref = f32[8,128]{1,0:T(8,128)S(1)} collective-permute-done((f32[8,128]{1,0:T(8,128)S(1)}, f32[8,128]{1,0:T(8,128)S(1)}, u32[]{:S(2)}, u32[]{:S(2)}) %collective-permute-start) | collective-permute-done | bytes 4128 | tf_op jit(solution)/shard_map/ppermute | solution.py:578
  4.2 0.0 copy-done.4
  4.2 0.0 copy-done.3
  4.2 1.1 %shard_map.132 = (f32[288,128]{1,0:T(8,128)}, f32[8,384]{1,0:T(8,128)S(1)}, f32[72,128]{1,0:T(8,128)S(1)}, f32[72,128]{1,0:T(8,128)S(1)}, f32[8,384]{1,0:T(8,128)S(1)}) custom-call(f32[8,128]{1,0:T(8,128)S(1)} %get-tuple-element.23.keep_ref, f32[8,128]{1,0:T(8,128)S(1)} %collective-permute-done.given_ref, s32[1,32]{1,0:T(1,128)S(1)} %bitcast.11, ...), custom_call_target="tpu_custom_call" | custom-call | flops 1000000 | bytes 4000000 | tf_op jit(solution)/shard_map/pallas_call | solution.py:549
  5.3 7.2 %all-to-all-start = ((f32[32,9,1,128]{3,2,1,0:T(1,128)}), f32[32,9,1,128]{3,2,1,0:T(1,128)S(1)}, u32[]{:S(2)}, u32[]{:S(2)}) async-start(f32[32,9,1,128]{3,2,1,0:T(1,128)} %bitcast.2), calls=%async_computation | async-start | bytes 294912 | tf_op jit(solution)/shard_map/all_to_all | solution.py:571
  12.5 0.3 collective-permute-start.2
  12.8 3.0 %collective-permute-start.3 = (f32[72,128]{1,0:T(8,128)S(1)}, f32[72,128]{1,0:T(8,128)S(1)}, u32[]{:S(2)}, u32[]{:S(2)}) collective-permute-start(f32[72,128]{1,0:T(8,128)S(1)} %get-tuple-element.29.refs_7_), channel_id=1, source_target_pairs={{0,4},{4,0},{8,12},{12,8},{16,20},{20,16},{24,28},{28,24},{1,5},{5... | collective-permute-start | bytes 110600 | tf_op jit(solution)/shard_map/ppermute | solution.py:578
  15.8 0.0 collective-permute-start.1
  15.8 1.5 %collective-permute-start.4 = (f32[8,384]{1,0:T(8,128)S(1)}, f32[8,384]{1,0:T(8,128)S(1)}, u32[]{:S(2)}, u32[]{:S(2)}) collective-permute-start(f32[8,384]{1,0:T(8,128)S(1)} %get-tuple-element.30.refs_8_), channel_id=1, source_target_pairs={{0,1},{1,0},{2,3},{3,2},{4,5},{5,4},{6,7},{7,6},{8,9},{9,8},{10,11... | collective-permute-start | bytes 36872 | tf_op jit(solution)/shard_map/ppermute | solution.py:578
  17.3 0.0 copy-done.2
  17.4 0.0 copy-done.1
  17.4 0.0 copy-done
  17.4 1.8 %shard_map.133.refs_0_ = f32[11,12,32,128]{3,2,1,0:T(8,128)S(1)} custom-call(f32[11,12,32,128]{3,2,1,0:T(8,128)S(1)} %get-tuple-element.22.grid_ref.given_ref, f32[288,128]{1,0:T(8,128)} %get-tuple-element.26.after_ref, s32[12,32,128]{2,1,0:T(8,128)S(1)} %get-tuple-element.25.flag_ref, s32[1,1024]{1,0:T(1,128)S(1)} %copy-done, ...), custom_call_target="tpu_custom_call", output_to_operand_aliasing={{}: (0, {})} | custom-call | flops 1000000 | bytes 4000000 | tf_op jit(solution)/shard_map/pallas_call | solution.py:549
  19.2 0.3 collective-permute-done.1.refs_9_
  19.5 0.0 collective-permute-done.4.refs_12_
  19.5 0.0 collective-permute-done.2.refs_10_
  19.5 0.0 collective-permute-done.3.refs_11_
  19.5 0.8 %all-to-all-done = f32[32,9,1,128]{3,2,1,0:T(1,128)S(1)} async-done(((f32[32,9,1,128]{3,2,1,0:T(1,128)}), f32[32,9,1,128]{3,2,1,0:T(1,128)S(1)}, u32[]{:S(2)}, u32[]{:S(2)}) %all-to-all-start) | async-done | bytes 147488 | tf_op jit(solution)/shard_map/all_to_all | solution.py:571
  20.3 2.6 %shard_map.134 = (f32[11,12,32,128]{3,2,1,0:T(8,128)S(1)}, f32[2,12,128]{2,1,0:T(8,128)S(1)}, f32[8,384]{1,0:T(8,128)S(1)}, f32[256,128]{1,0:T(8,128)}, f32[1,38...) custom-call(f32[11,12,32,128]{3,2,1,0:T(8,128)S(1)} %shard_map.133.r, ...), custom_call_target="tpu_custom_call", output_to_operand_aliasing={{0}: (0, {})} | custom-call | flops 1000000 | bytes 4000000 | tf_op jit(solution)/shard_map/pallas_call | solution.py:549
  22.9 3.2 %all-to-all-start.1 = ((f32[32,8,1,128]{3,1,2,0:T(8,128)}), f32[32,8,1,128]{3,1,2,0:T(8,128)S(1)}, u32[]{:S(2)}, u32[]{:S(2)}) async-start(f32[32,8,1,128]{3,1,2,0:T(8,128)} %bitcast.5), calls=%async_computation.1 | async-start | bytes 262144 | tf_op jit(solution)/shard_map/all_to_all | solution.py:571
  26.1 0.3 collective-permute-start.6
  26.4 3.0 %collective-permute-start.7 = (f32[12,128]{1,0:T(8,128)S(1)}, f32[12,128]{1,0:T(8,128)S(1)}, u32[]{:S(2)}, u32[]{:S(2)}) collective-permute-start(f32[12,128]{1,0:T(8,128)S(1)} %get-tuple-element.38), channel_id=1, source_target_pairs={{0,4},{4,0},{8,12},{12,8},{16,20},{20,16},{24,28},{28,24},{1,5},{5... | collective-permute-start | bytes 18440 | tf_op jit(solution)/shard_map/ppermute | solution.py:578
  29.4 0.0 collective-permute-start.5
  29.4 1.5 %collective-permute-start.8 = (f32[1,384]{1,0:T(1,128)S(1)}, f32[1,384]{1,0:T(1,128)S(1)}, u32[]{:S(2)}, u32[]{:S(2)}) collective-permute-start(f32[1,384]{1,0:T(1,128)S(1)} %get-tuple-element.39), channel_id=1, source_target_pairs={{0,1},{1,0},{2,3},{3,2},{4,5},{5,4},{6,7},{7,6},{8,9},{9,8},{10,11... | collective-permute-start | bytes 4616 | tf_op jit(solution)/shard_map/ppermute | solution.py:578
  30.9 0.2 shard_map.135.inner_ref
  31.1 1.9 %collective-permute-done.5.yb_ref = f32[1,384]{1,0:T(1,128)S(1)} collective-permute-done((f32[1,384]{1,0:T(1,128)S(1)}, f32[1,384]{1,0:T(1,128)S(1)}, u32[]{:S(2)}, u32[]{:S(2)}) %collective-permute-start.5) | collective-permute-done | bytes 1568 | tf_op jit(solution)/shard_map/ppermute | solution.py:594
  33.0 0.0 collective-permute-done.8.ya_ref
  33.0 0.0 collective-permute-done.6.xb_ref
  33.0 0.0 collective-permute-done.7.xa_ref
  33.0 0.8 %all-to-all-done.1 = f32[32,8,1,128]{3,1,2,0:T(8,128)S(1)} async-done(((f32[32,8,1,128]{3,1,2,0:T(8,128)}), f32[32,8,1,128]{3,1,2,0:T(8,128)S(1)}, u32[]{:S(2)}, u32[]{:S(2)}) %all-to-all-start.1) | async-done | bytes 131104 | tf_op jit(solution)/shard_map/all_to_all | solution.py:571
  33.8 1.4 %shard_map.136 = (f32[12,32,128]{2,1,0:T(8,128)}, f32[1,32]{1,0:T(1,128)}) custom-call(f32[256,128]{1,0:T(8,128)S(1)} %bitcast.10, f32[3,8,128]{2,1,0:T(8,128)S(1)} %get-tuple-element.32.known_ref, s32[1,1024]{1,0:T(1,128)S(1)} %copy-done, s32[1,1024]{1,0:T(1,128)S(1)} %copy-done.1, f32[1,1024]{1,0:T(1,128)S(1)} %copy-done.2, ...), custom_call_target="tpu_custom_call" | custom-call | flops 1000000 | bytes 4000000 | tf_op jit(solution)/shard_map/pallas_call | solution.py:549
Async XLA Ops:
  0.6 16.7 %copy-start.2 = (f32[1,1024]{1,0:T(1,128)S(1)}, f32[1,1024]{1,0:T(1,128)}, u32[]{:S(2)}) copy-start(f32[1,1024]{1,0:T(1,128)} %index_ref.3) | copy-start | bytes 12292
  0.6 16.7 %copy-start.1 = (s32[1,1024]{1,0:T(1,128)S(1)}, s32[1,1024]{1,0:T(1,128)}, u32[]{:S(2)}) copy-start(s32[1,1024]{1,0:T(1,128)} %well_ref.3) | copy-start | bytes 12292
  0.7 16.7 %copy-start = (s32[1,1024]{1,0:T(1,128)S(1)}, s32[1,1024]{1,0:T(1,128)}, u32[]{:S(2)}) copy-start(s32[1,1024]{1,0:T(1,128)} %cell_ref.3) | copy-start | bytes 12292
  0.7 3.5 %copy-start.4 = (f32[32]{0:T(128)S(1)}, f32[32]{0:T(128)}, u32[]{:S(2)}) copy-start(f32[32]{0:T(128)} %param.23) | copy-start | bytes 388
  0.7 3.5 %copy-start.3 = (s32[32]{0:T(128)S(1)}, s32[32]{0:T(128)}, u32[]{:S(2)}) copy-start(s32[32]{0:T(128)} %param.22) | copy-start | bytes 388
  2.8 1.3 %collective-permute-start = (f32[8,128]{1,0:T(8,128)S(1)}, f32[8,128]{1,0:T(8,128)S(1)}, u32[]{:S(2)}, u32[]{:S(2)}) collective-permute-start(f32[8,128]{1,0:T(8,128)S(1)} %get-tuple-element.24), channel_id=1, source_target_pairs={{0,1},{1,0},{2,3},{3,2},{4,5},{5,4},{6,7},{7,6},{8,9},{9,8},{10,11... | collective-permute-start | bytes 12296 | tf_op jit(solution)/shard_map/ppermute | solution.py:578
  5.3 15.0 %all-to-all-start = ((f32[32,9,1,128]{3,2,1,0:T(1,128)}), f32[32,9,1,128]{3,2,1,0:T(1,128)S(1)}, u32[]{:S(2)}, u32[]{:S(2)}) async-start(f32[32,9,1,128]{3,2,1,0:T(1,128)} %bitcast.2), calls=%async_computation | async-start | bytes 294912 | tf_op jit(solution)/shard_map/all_to_all | solution.py:571
  12.5 7.0 %collective-permute-start.2 = (f32[72,128]{1,0:T(8,128)S(1)}, f32[72,128]{1,0:T(8,128)S(1)}, u32[]{:S(2)}, u32[]{:S(2)}) collective-permute-start(f32[72,128]{1,0:T(8,128)S(1)} %get-tuple-element.28.refs_6_), channel_id=1, source_target_pairs={{0,1},{1,0},{2,3},{3,2},{4,8},{5,9},{6,10},{7,11},{8,4},{9,5},{10,... | collective-permute-start | bytes 110600 | tf_op jit(solution)/shard_map/ppermute | solution.py:594
  12.8 6.7 %collective-permute-start.3 = (f32[72,128]{1,0:T(8,128)S(1)}, f32[72,128]{1,0:T(8,128)S(1)}, u32[]{:S(2)}, u32[]{:S(2)}) collective-permute-start(f32[72,128]{1,0:T(8,128)S(1)} %get-tuple-element.29.refs_7_), channel_id=1, source_target_pairs={{0,4},{4,0},{8,12},{12,8},{16,20},{20,16},{24,28},{28,24},{1,5},{5... | collective-permute-start | bytes 110600 | tf_op jit(solution)/shard_map/ppermute | solution.py:578
  15.8 3.7 %collective-permute-start.1 = (f32[8,384]{1,0:T(8,128)S(1)}, f32[8,384]{1,0:T(8,128)S(1)}, u32[]{:S(2)}, u32[]{:S(2)}) collective-permute-start(f32[8,384]{1,0:T(8,128)S(1)} %get-tuple-element.27.refs_5_), channel_id=1, source_target_pairs={{0,4},{1,2},{2,1},{3,7},{4,0},{5,6},{6,5},{7,3},{8,12},{9,10},{10,... | collective-permute-start | bytes 36872 | tf_op jit(solution)/shard_map/ppermute | solution.py:594
  15.8 3.7 %collective-permute-start.4 = (f32[8,384]{1,0:T(8,128)S(1)}, f32[8,384]{1,0:T(8,128)S(1)}, u32[]{:S(2)}, u32[]{:S(2)}) collective-permute-start(f32[8,384]{1,0:T(8,128)S(1)} %get-tuple-element.30.refs_8_), channel_id=1, source_target_pairs={{0,1},{1,0},{2,3},{3,2},{4,5},{5,4},{6,7},{7,6},{8,9},{9,8},{10,11... | collective-permute-start | bytes 36872 | tf_op jit(solution)/shard_map/ppermute | solution.py:578
  22.9 10.9 %all-to-all-start.1 = ((f32[32,8,1,128]{3,1,2,0:T(8,128)}), f32[32,8,1,128]{3,1,2,0:T(8,128)S(1)}, u32[]{:S(2)}, u32[]{:S(2)}) async-start(f32[32,8,1,128]{3,1,2,0:T(8,128)} %bitcast.5), calls=%async_computation.1 | async-start | bytes 262144 | tf_op jit(solution)/shard_map/all_to_all | solution.py:571
  26.1 6.9 %collective-permute-start.6 = (f32[12,128]{1,0:T(8,128)S(1)}, f32[12,128]{1,0:T(8,128)S(1)}, u32[]{:S(2)}, u32[]{:S(2)}) collective-permute-start(f32[12,128]{1,0:T(8,128)S(1)} %get-tuple-element.37), channel_id=1, source_target_pairs={{0,1},{1,0},{2,3},{3,2},{4,8},{5,9},{6,10},{7,11},{8,4},{9,5},{10,... | collective-permute-start | bytes 18440 | tf_op jit(solution)/shard_map/ppermute | solution.py:594
  26.4 6.6 %collective-permute-start.7 = (f32[12,128]{1,0:T(8,128)S(1)}, f32[12,128]{1,0:T(8,128)S(1)}, u32[]{:S(2)}, u32[]{:S(2)}) collective-permute-start(f32[12,128]{1,0:T(8,128)S(1)} %get-tuple-element.38), channel_id=1, source_target_pairs={{0,4},{4,0},{8,12},{12,8},{16,20},{20,16},{24,28},{28,24},{1,5},{5... | collective-permute-start | bytes 18440 | tf_op jit(solution)/shard_map/ppermute | solution.py:578
  29.4 3.6 %collective-permute-start.5 = (f32[1,384]{1,0:T(1,128)S(1)}, f32[1,384]{1,0:T(1,128)S(1)}, u32[]{:S(2)}, u32[]{:S(2)}) collective-permute-start(f32[1,384]{1,0:T(1,128)S(1)} %get-tuple-element.36), channel_id=1, source_target_pairs={{0,4},{1,2},{2,1},{3,7},{4,0},{5,6},{6,5},{7,3},{8,12},{9,10},{10,... | collective-permute-start | bytes 4616 | tf_op jit(solution)/shard_map/ppermute | solution.py:594
  29.4 3.6 %collective-permute-start.8 = (f32[1,384]{1,0:T(1,128)S(1)}, f32[1,384]{1,0:T(1,128)S(1)}, u32[]{:S(2)}, u32[]{:S(2)}) collective-permute-start(f32[1,384]{1,0:T(1,128)S(1)} %get-tuple-element.39), channel_id=1, source_target_pairs={{0,1},{1,0},{2,3},{3,2},{4,5},{5,4},{6,7},{7,6},{8,9},{9,8},{10,11... | collective-permute-start | bytes 4616 | tf_op jit(solution)/shard_map/ppermute | solution.py:578

commit v9 on v8

--- a/solution.py
+++ b/solution.py
@@ -414,7 +414,7 @@
 
 
 def first_update(
-    given_ref, sums_ref, cell_ref, well_ref, index_ref,
+    between, sums_ref, cell_ref, well_ref, index_ref,
     grid_ref, out_ref, yb_ref, xb_ref, xa_ref, ya_ref, known_ref, line_ref, block_ref, sems,
 ):
     layers, width, lanes = grid_ref.shape[1:]
@@ -454,6 +454,7 @@
     row, lane = places(cell_ref[...], lanes)
     well_row, well_lane = places(well_ref[...], LANES)
     push = cell_scatter(slot_bhp(bhp, well_ref, index_ref), row, lane, rows, lanes)
+    between()
     current = grid_ref[CURRENT].reshape(rows, lanes) + grid_ref[GAIN].reshape(rows, lanes) * push
     grid_ref[CURRENT] = current.reshape(layers, width, lanes)
     xa_ref[...], xb_ref[...] = sides(
@@ -478,8 +479,11 @@
     given_ref, sums_ref, cell_ref, well_ref, index_ref = refs[:5]
     rims, (grid_ref, bound_ref, flank_ref) = refs[5:13], refs[13:16]
     outs, side_ref, scratch = refs[16:22], refs[22], refs[23:]
-    outer_terms(given_ref, *rims, grid_ref, bound_ref, flank_ref, side_ref)
-    first_update(given_ref, sums_ref, cell_ref, well_ref, index_ref, grid_ref, *outs, *scratch)
+
+    def between():
+        outer_terms(given_ref, *rims, grid_ref, bound_ref, flank_ref, side_ref)
+
+    first_update(between, sums_ref, cell_ref, well_ref, index_ref, grid_ref, *outs, *scratch)
 
 
 def inner_terms(after_ref, grid_ref, out_ref):

time: 35.4 us -> 35.3 us (level)
  no operation moved by 1% of the time
where the time goes in v9:
time: 35.3 us; the launch traced here: 35 us
  starting transfers between devices  20.7 us (59%)
  Pallas kernels  9.03 us (26%)
  waiting for transfers between devices  4.58 us (13%)
  between operations  0.75 us (2%)
    all_to_all x2, starting transfers between devices, everyone(): lax.all_to_all(rows.reshape(count, height, 1, LANES), AXES[::-1], 0, 0, t...  10.4 us
    ppermute x5, starting transfers between devices, to_pair(): return lax.ppermute(block, axis, [(i, i ^ 1) for i in range(count)])  9.57 us
    pallas_call x6, Pallas kernels, call(): pl.pallas_call(kernel, out_shape=shapes, in_specs=[pl.BlockSpec(memory_sp...  9.03 us
    ppermute x4, waiting for transfers between devices, to_other(): return lax.ppermute(block, AXES, moves)  2.19 us
    all_to_all x2, waiting for transfers between devices, everyone(): lax.all_to_all(rows.reshape(count, height, 1, LANES), AXES[::-1], 0, 0, t...  1.56 us
    ppermute x5, waiting for transfers between devices, to_pair(): return lax.ppermute(block, axis, [(i, i ^ 1) for i in range(count)])  0.83 us
  transfers between devices with their start and end apart: 11, of which 5 were waited for; matrix products, arithmetic and copies ran while one was open for 0% of the time, Pallas kernels for 6%

profile of v9, /device:TPU:0, one launch (start us, length us, event | category | flops | bytes accessed | tf_op | source)
XLA Modules:
  0.0 35.0 jit_solution(12487625781151118940)
XLA Ops:
  0.6 0.0 copy-start.2
  0.6 0.0 copy-start.1
  0.7 0.0 copy-start
  0.7 0.0 copy-start.4
  0.7 0.0 copy-start.3
  0.7 2.2 %shard_map.131 = (f32[8,128]{1,0:T(8,128)S(1)}, f32[8,128]{1,0:T(8,128)S(1)}, f32[11,12,32,128]{3,2,1,0:T(8,128)S(1)}, s32[12,32,128]{2,1,0:T(8,128)S(1)}) custom-call(s32[1,1024]{1,0:T(1,128)} %cell_ref.3, s32[1,1024]{1,0:T(1,128)} %well_ref.3, f32[1,1024]{1,0:T(1,128)} %index_ref.3, f32[2,12,32,128]{3,2,1,0:T(8,128)} %refs_3_.2, f32[12,32,128]{2,1,0:T(8,128)} %refs_4_.2, ...), custom_call_target="tpu_custom_call" | custom-call | flops 1000000 | bytes 4000000 | tf_op jit(solution)/shard_map/pallas_call | solution.py:553
  2.8 0.5 %collective-permute-start = (f32[8,128]{1,0:T(8,128)S(1)}, f32[8,128]{1,0:T(8,128)S(1)}, u32[]{:S(2)}, u32[]{:S(2)}) collective-permute-start(f32[8,128]{1,0:T(8,128)S(1)} %get-tuple-element.24), channel_id=1, source_target_pairs={{0,1},{1,0},{2,3},{3,2},{4,5},{5,4},{6,7},{7,6},{8,9},{9,8},{10,11... | collective-permute-start | bytes 12296 | tf_op jit(solution)/shard_map/ppermute | solution.py:582
  3.4 0.8 %collective-permute-done.given_ref = f32[8,128]{1,0:T(8,128)S(1)} collective-permute-done((f32[8,128]{1,0:T(8,128)S(1)}, f32[8,128]{1,0:T(8,128)S(1)}, u32[]{:S(2)}, u32[]{:S(2)}) %collective-permute-start) | collective-permute-done | bytes 4128 | tf_op jit(solution)/shard_map/ppermute | solution.py:582
  4.2 0.0 copy-done.4
  4.2 0.0 copy-done.3
  4.2 1.1 %shard_map.132 = (f32[288,128]{1,0:T(8,128)}, f32[8,384]{1,0:T(8,128)S(1)}, f32[72,128]{1,0:T(8,128)S(1)}, f32[72,128]{1,0:T(8,128)S(1)}, f32[8,384]{1,0:T(8,128)S(1)}) custom-call(f32[8,128]{1,0:T(8,128)S(1)} %get-tuple-element.23.keep_ref, f32[8,128]{1,0:T(8,128)S(1)} %collective-permute-done.given_ref, s32[1,32]{1,0:T(1,128)S(1)} %bitcast.11, ...), custom_call_target="tpu_custom_call" | custom-call | flops 1000000 | bytes 4000000 | tf_op jit(solution)/shard_map/pallas_call | solution.py:553
  5.3 7.2 %all-to-all-start = ((f32[32,9,1,128]{3,2,1,0:T(1,128)}), f32[32,9,1,128]{3,2,1,0:T(1,128)S(1)}, u32[]{:S(2)}, u32[]{:S(2)}) async-start(f32[32,9,1,128]{3,2,1,0:T(1,128)} %bitcast.2), calls=%async_computation | async-start | bytes 294912 | tf_op jit(solution)/shard_map/all_to_all | solution.py:575
  12.5 0.3 collective-permute-start.2
  12.8 3.0 %collective-permute-start.3 = (f32[72,128]{1,0:T(8,128)S(1)}, f32[72,128]{1,0:T(8,128)S(1)}, u32[]{:S(2)}, u32[]{:S(2)}) collective-permute-start(f32[72,128]{1,0:T(8,128)S(1)} %get-tuple-element.29.refs_7_), channel_id=1, source_target_pairs={{0,4},{4,0},{8,12},{12,8},{16,20},{20,16},{24,28},{28,24},{1,5},{5... | collective-permute-start | bytes 110600 | tf_op jit(solution)/shard_map/ppermute | solution.py:582
  15.8 0.0 collective-permute-start.1
  15.8 1.5 %collective-permute-start.4 = (f32[8,384]{1,0:T(8,128)S(1)}, f32[8,384]{1,0:T(8,128)S(1)}, u32[]{:S(2)}, u32[]{:S(2)}) collective-permute-start(f32[8,384]{1,0:T(8,128)S(1)} %get-tuple-element.30.refs_8_), channel_id=1, source_target_pairs={{0,1},{1,0},{2,3},{3,2},{4,5},{5,4},{6,7},{7,6},{8,9},{9,8},{10,11... | collective-permute-start | bytes 36872 | tf_op jit(solution)/shard_map/ppermute | solution.py:582
  17.3 0.0 copy-done.2
  17.4 0.0 copy-done.1
  17.4 0.0 copy-done
  17.4 1.8 %shard_map.133.refs_0_ = f32[11,12,32,128]{3,2,1,0:T(8,128)S(1)} custom-call(f32[11,12,32,128]{3,2,1,0:T(8,128)S(1)} %get-tuple-element.22.grid_ref.given_ref, f32[288,128]{1,0:T(8,128)} %get-tuple-element.26.after_ref, s32[12,32,128]{2,1,0:T(8,128)S(1)} %get-tuple-element.25.flag_ref, s32[1,1024]{1,0:T(1,128)S(1)} %copy-done, ...), custom_call_target="tpu_custom_call", output_to_operand_aliasing={{}: (0, {})} | custom-call | flops 1000000 | bytes 4000000 | tf_op jit(solution)/shard_map/pallas_call | solution.py:553
  19.2 0.3 collective-permute-done.1.refs_9_
  19.5 0.0 collective-permute-done.4.refs_12_
  19.5 0.0 collective-permute-done.2.refs_10_
  19.5 0.0 collective-permute-done.3.refs_11_
  19.5 0.8 %all-to-all-done = f32[32,9,1,128]{3,2,1,0:T(1,128)S(1)} async-done(((f32[32,9,1,128]{3,2,1,0:T(1,128)}), f32[32,9,1,128]{3,2,1,0:T(1,128)S(1)}, u32[]{:S(2)}, u32[]{:S(2)}) %all-to-all-start) | async-done | bytes 147488 | tf_op jit(solution)/shard_map/all_to_all | solution.py:575
  20.3 2.4 %shard_map.134 = (f32[11,12,32,128]{3,2,1,0:T(8,128)S(1)}, f32[2,12,128]{2,1,0:T(8,128)S(1)}, f32[8,384]{1,0:T(8,128)S(1)}, f32[256,128]{1,0:T(8,128)}, f32[1,38...) custom-call(f32[11,12,32,128]{3,2,1,0:T(8,128)S(1)} %shard_map.133.r, ...), custom_call_target="tpu_custom_call", output_to_operand_aliasing={{0}: (0, {})} | custom-call | flops 1000000 | bytes 4000000 | tf_op jit(solution)/shard_map/pallas_call | solution.py:553
  22.7 3.2 %all-to-all-start.1 = ((f32[32,8,1,128]{3,1,2,0:T(8,128)}), f32[32,8,1,128]{3,1,2,0:T(8,128)S(1)}, u32[]{:S(2)}, u32[]{:S(2)}) async-start(f32[32,8,1,128]{3,1,2,0:T(8,128)} %bitcast.5), calls=%async_computation.1 | async-start | bytes 262144 | tf_op jit(solution)/shard_map/all_to_all | solution.py:575
  25.9 0.3 collective-permute-start.6
  26.3 3.0 %collective-permute-start.7 = (f32[12,128]{1,0:T(8,128)S(1)}, f32[12,128]{1,0:T(8,128)S(1)}, u32[]{:S(2)}, u32[]{:S(2)}) collective-permute-start(f32[12,128]{1,0:T(8,128)S(1)} %get-tuple-element.38), channel_id=1, source_target_pairs={{0,4},{4,0},{8,12},{12,8},{16,20},{20,16},{24,28},{28,24},{1,5},{5... | collective-permute-start | bytes 18440 | tf_op jit(solution)/shard_map/ppermute | solution.py:582
  29.2 0.0 collective-permute-start.5
  29.3 1.5 %collective-permute-start.8 = (f32[1,384]{1,0:T(1,128)S(1)}, f32[1,384]{1,0:T(1,128)S(1)}, u32[]{:S(2)}, u32[]{:S(2)}) collective-permute-start(f32[1,384]{1,0:T(1,128)S(1)} %get-tuple-element.39), channel_id=1, source_target_pairs={{0,1},{1,0},{2,3},{3,2},{4,5},{5,4},{6,7},{7,6},{8,9},{9,8},{10,11... | collective-permute-start | bytes 4616 | tf_op jit(solution)/shard_map/ppermute | solution.py:582
  30.8 0.2 shard_map.135.inner_ref
  31.0 1.9 %collective-permute-done.5.yb_ref = f32[1,384]{1,0:T(1,128)S(1)} collective-permute-done((f32[1,384]{1,0:T(1,128)S(1)}, f32[1,384]{1,0:T(1,128)S(1)}, u32[]{:S(2)}, u32[]{:S(2)}) %collective-permute-start.5) | collective-permute-done | bytes 1568 | tf_op jit(solution)/shard_map/ppermute | solution.py:598
  32.9 0.0 collective-permute-done.8.ya_ref
  32.9 0.0 collective-permute-done.6.xb_ref
  32.9 0.0 collective-permute-done.7.xa_ref
  32.9 0.8 %all-to-all-done.1 = f32[32,8,1,128]{3,1,2,0:T(8,128)S(1)} async-done(((f32[32,8,1,128]{3,1,2,0:T(8,128)}), f32[32,8,1,128]{3,1,2,0:T(8,128)S(1)}, u32[]{:S(2)}, u32[]{:S(2)}) %all-to-all-start.1) | async-done | bytes 131104 | tf_op jit(solution)/shard_map/all_to_all | solution.py:575
  33.7 1.4 %shard_map.136 = (f32[12,32,128]{2,1,0:T(8,128)}, f32[1,32]{1,0:T(1,128)}) custom-call(f32[256,128]{1,0:T(8,128)S(1)} %bitcast.10, f32[3,8,128]{2,1,0:T(8,128)S(1)} %get-tuple-element.32.known_ref, s32[1,1024]{1,0:T(1,128)S(1)} %copy-done, s32[1,1024]{1,0:T(1,128)S(1)} %copy-done.1, f32[1,1024]{1,0:T(1,128)S(1)} %copy-done.2, ...), custom_call_target="tpu_custom_call" | custom-call | flops 1000000 | bytes 4000000 | tf_op jit(solution)/shard_map/pallas_call | solution.py:553
Async XLA Ops:
  0.6 16.7 %copy-start.2 = (f32[1,1024]{1,0:T(1,128)S(1)}, f32[1,1024]{1,0:T(1,128)}, u32[]{:S(2)}) copy-start(f32[1,1024]{1,0:T(1,128)} %index_ref.3) | copy-start | bytes 12292
  0.6 16.7 %copy-start.1 = (s32[1,1024]{1,0:T(1,128)S(1)}, s32[1,1024]{1,0:T(1,128)}, u32[]{:S(2)}) copy-start(s32[1,1024]{1,0:T(1,128)} %well_ref.3) | copy-start | bytes 12292
  0.7 16.7 %copy-start = (s32[1,1024]{1,0:T(1,128)S(1)}, s32[1,1024]{1,0:T(1,128)}, u32[]{:S(2)}) copy-start(s32[1,1024]{1,0:T(1,128)} %cell_ref.3) | copy-start | bytes 12292
  0.7 3.5 %copy-start.4 = (f32[32]{0:T(128)S(1)}, f32[32]{0:T(128)}, u32[]{:S(2)}) copy-start(f32[32]{0:T(128)} %param.23) | copy-start | bytes 388
  0.7 3.5 %copy-start.3 = (s32[32]{0:T(128)S(1)}, s32[32]{0:T(128)}, u32[]{:S(2)}) copy-start(s32[32]{0:T(128)} %param.22) | copy-start | bytes 388
  2.8 1.3 %collective-permute-start = (f32[8,128]{1,0:T(8,128)S(1)}, f32[8,128]{1,0:T(8,128)S(1)}, u32[]{:S(2)}, u32[]{:S(2)}) collective-permute-start(f32[8,128]{1,0:T(8,128)S(1)} %get-tuple-element.24), channel_id=1, source_target_pairs={{0,1},{1,0},{2,3},{3,2},{4,5},{5,4},{6,7},{7,6},{8,9},{9,8},{10,11... | collective-permute-start | bytes 12296 | tf_op jit(solution)/shard_map/ppermute | solution.py:582
  5.3 15.0 %all-to-all-start = ((f32[32,9,1,128]{3,2,1,0:T(1,128)}), f32[32,9,1,128]{3,2,1,0:T(1,128)S(1)}, u32[]{:S(2)}, u32[]{:S(2)}) async-start(f32[32,9,1,128]{3,2,1,0:T(1,128)} %bitcast.2), calls=%async_computation | async-start | bytes 294912 | tf_op jit(solution)/shard_map/all_to_all | solution.py:575
  12.5 7.0 %collective-permute-start.2 = (f32[72,128]{1,0:T(8,128)S(1)}, f32[72,128]{1,0:T(8,128)S(1)}, u32[]{:S(2)}, u32[]{:S(2)}) collective-permute-start(f32[72,128]{1,0:T(8,128)S(1)} %get-tuple-element.28.refs_6_), channel_id=1, source_target_pairs={{0,1},{1,0},{2,3},{3,2},{4,8},{5,9},{6,10},{7,11},{8,4},{9,5},{10,... | collective-permute-start | bytes 110600 | tf_op jit(solution)/shard_map/ppermute | solution.py:598
  12.8 6.7 %collective-permute-start.3 = (f32[72,128]{1,0:T(8,128)S(1)}, f32[72,128]{1,0:T(8,128)S(1)}, u32[]{:S(2)}, u32[]{:S(2)}) collective-permute-start(f32[72,128]{1,0:T(8,128)S(1)} %get-tuple-element.29.refs_7_), channel_id=1, source_target_pairs={{0,4},{4,0},{8,12},{12,8},{16,20},{20,16},{24,28},{28,24},{1,5},{5... | collective-permute-start | bytes 110600 | tf_op jit(solution)/shard_map/ppermute | solution.py:582
  15.8 3.7 %collective-permute-start.1 = (f32[8,384]{1,0:T(8,128)S(1)}, f32[8,384]{1,0:T(8,128)S(1)}, u32[]{:S(2)}, u32[]{:S(2)}) collective-permute-start(f32[8,384]{1,0:T(8,128)S(1)} %get-tuple-element.27.refs_5_), channel_id=1, source_target_pairs={{0,4},{1,2},{2,1},{3,7},{4,0},{5,6},{6,5},{7,3},{8,12},{9,10},{10,... | collective-permute-start | bytes 36872 | tf_op jit(solution)/shard_map/ppermute | solution.py:598
  15.8 3.7 %collective-permute-start.4 = (f32[8,384]{1,0:T(8,128)S(1)}, f32[8,384]{1,0:T(8,128)S(1)}, u32[]{:S(2)}, u32[]{:S(2)}) collective-permute-start(f32[8,384]{1,0:T(8,128)S(1)} %get-tuple-element.30.refs_8_), channel_id=1, source_target_pairs={{0,1},{1,0},{2,3},{3,2},{4,5},{5,4},{6,7},{7,6},{8,9},{9,8},{10,11... | collective-permute-start | bytes 36872 | tf_op jit(solution)/shard_map/ppermute | solution.py:582
  22.7 10.9 %all-to-all-start.1 = ((f32[32,8,1,128]{3,1,2,0:T(8,128)}), f32[32,8,1,128]{3,1,2,0:T(8,128)S(1)}, u32[]{:S(2)}, u32[]{:S(2)}) async-start(f32[32,8,1,128]{3,1,2,0:T(8,128)} %bitcast.5), calls=%async_computation.1 | async-start | bytes 262144 | tf_op jit(solution)/shard_map/all_to_all | solution.py:575
  25.9 6.9 %collective-permute-start.6 = (f32[12,128]{1,0:T(8,128)S(1)}, f32[12,128]{1,0:T(8,128)S(1)}, u32[]{:S(2)}, u32[]{:S(2)}) collective-permute-start(f32[12,128]{1,0:T(8,128)S(1)} %get-tuple-element.37), channel_id=1, source_target_pairs={{0,1},{1,0},{2,3},{3,2},{4,8},{5,9},{6,10},{7,11},{8,4},{9,5},{10,... | collective-permute-start | bytes 18440 | tf_op jit(solution)/shard_map/ppermute | solution.py:598
  26.3 6.6 %collective-permute-start.7 = (f32[12,128]{1,0:T(8,128)S(1)}, f32[12,128]{1,0:T(8,128)S(1)}, u32[]{:S(2)}, u32[]{:S(2)}) collective-permute-start(f32[12,128]{1,0:T(8,128)S(1)} %get-tuple-element.38), channel_id=1, source_target_pairs={{0,4},{4,0},{8,12},{12,8},{16,20},{20,16},{24,28},{28,24},{1,5},{5... | collective-permute-start | bytes 18440 | tf_op jit(solution)/shard_map/ppermute | solution.py:582
  29.2 3.6 %collective-permute-start.5 = (f32[1,384]{1,0:T(1,128)S(1)}, f32[1,384]{1,0:T(1,128)S(1)}, u32[]{:S(2)}, u32[]{:S(2)}) collective-permute-start(f32[1,384]{1,0:T(1,128)S(1)} %get-tuple-element.36), channel_id=1, source_target_pairs={{0,4},{1,2},{2,1},{3,7},{4,0},{5,6},{6,5},{7,3},{8,12},{9,10},{10,... | collective-permute-start | bytes 4616 | tf_op jit(solution)/shard_map/ppermute | solution.py:598
  29.3 3.6 %collective-permute-start.8 = (f32[1,384]{1,0:T(1,128)S(1)}, f32[1,384]{1,0:T(1,128)S(1)}, u32[]{:S(2)}, u32[]{:S(2)}) collective-permute-start(f32[1,384]{1,0:T(1,128)S(1)} %get-tuple-element.39), channel_id=1, source_target_pairs={{0,1},{1,0},{2,3},{3,2},{4,5},{5,4},{6,7},{7,6},{8,9},{9,8},{10,11... | collective-permute-start | bytes 4616 | tf_op jit(solution)/shard_map/ppermute | solution.py:582
